TPU v7x, 32 devices: a whole 2x2x4 slice. The times are simulated.
32 devices in a mesh: dp: 16 (over z, x, core), seq: 2 (over y).
Axes of the slice: x: 2, y: 2, z: 4, core: 2. Of those that a mesh axis runs over, the one named last changes fastest.
Arguments:
- tokens: bfloat16 [64, 1024, 1024], P('dp', 'seq'), may hold values from -6 to 6
- first_gain: bfloat16 [1024], P(('dp', 'seq')), may hold values from 0.25 to 1.75
- first_shift: bfloat16 [1024], P(('dp', 'seq')), may hold values from -1.75 to 1.75
- query_weight: bfloat16 [1024, 1024], P('dp', 'seq'), may hold values from -0.1875 to 0.1875
- query_bias: bfloat16 [1024], P(('dp', 'seq')), may hold values from -1.75 to 1.75
- key_weight: bfloat16 [1024, 1024], P('dp', 'seq'), may hold values from -0.1875 to 0.1875
- value_weight: bfloat16 [1024, 1024], P('dp', 'seq'), may hold values from -0.1875 to 0.1875
- value_bias: bfloat16 [1024], P(('dp', 'seq')), may hold values from -0.625 to 0.625
- output_weight: bfloat16 [1024, 1024], P('dp', 'seq'), may hold values from -0.375 to 0.375
- output_bias: bfloat16 [1024], P(('dp', 'seq')), may hold values from -1.75 to 1.75
- second_gain: bfloat16 [1024], P(('dp', 'seq')), may hold values from 0.25 to 1.75
- second_shift: bfloat16 [1024], P(('dp', 'seq')), may hold values from -1.75 to 1.75
- up_weight: bfloat16 [1024, 4096], P('dp', 'seq'), may hold values from -0.1875 to 0.1875
- up_bias: bfloat16 [4096], P(('dp', 'seq')), may hold values from -6 to 6
- down_weight: bfloat16 [4096, 1024], P('dp', 'seq'), may hold values from -0.09375 to 0.09375
- down_bias: bfloat16 [1024], P(('dp', 'seq')), may hold values from -1.75 to 1.75
- piece_starts: int32 [64, 2], P('dp'), may hold values from 0 to 768, as said below
- out_grad: bfloat16 [64, 1024, 1024], P('dp', 'seq'), may hold values from -6 to 6
Outputs:
- output: bfloat16 [64, 1024, 1024], P('dp', 'seq')
- input_grad: bfloat16 [64, 1024, 1024], P('dp', 'seq')
- first_gain_grad: float32 [1024], P(('dp', 'seq'))
- first_shift_grad: float32 [1024], P(('dp', 'seq'))
- query_weight_grad: float32 [1024, 1024], P('dp', 'seq')
- query_bias_grad: float32 [1024], P(('dp', 'seq'))
- key_weight_grad: float32 [1024, 1024], P('dp', 'seq')
- value_weight_grad: float32 [1024, 1024], P('dp', 'seq')
- value_bias_grad: float32 [1024], P(('dp', 'seq'))
- output_weight_grad: float32 [1024, 1024], P('dp', 'seq')
- output_bias_grad: float32 [1024], P(('dp', 'seq'))
- second_gain_grad: float32 [1024], P(('dp', 'seq'))
- second_shift_grad: float32 [1024], P(('dp', 'seq'))
- up_weight_grad: float32 [1024, 4096], P('dp', 'seq')
- up_bias_grad: float32 [4096], P(('dp', 'seq'))
- down_weight_grad: float32 [4096, 1024], P('dp', 'seq')
- down_bias_grad: float32 [1024], P(('dp', 'seq'))
Inputs may be any that keep to these rules, and one draw needn't show every extreme that they name: `piece_starts`: each sequence holds two picture pieces of 256 tokens inside its 1024 tokens; the second starts at or after the end of the first.
All inputs are finite; a program needn't handle non-finite values.
Results may differ from a plain program's by a relative error of at most 0.024.
Values may be sent and summed in bfloat16 or wider, within the bound.
No kernel may reach another device: no remote copies, remote signals or barrier semaphores. Data moves between devices by JAX's collectives and lax.ppermute only.
A program may use at most 640 MiB of HBM per device.

v0:
```python
import math

import jax
import jax.numpy as jnp
from jax import lax
from jax.sharding import PartitionSpec as P

HEAD_DIM = 64
PIECE = 256


NEGATIVE = -1e30
EPSILON = 1e-05
BENDING = math.sqrt(2.0 / math.pi)
CUBIC_TERM = 0.044715


def smooth_gate(values):
    return (
        0.5 * values * (1.0 + jnp.tanh(BENDING * (values + CUBIC_TERM * values * values * values)))
    )


def smooth_slope(values):
    curved = jnp.tanh(BENDING * (values + CUBIC_TERM * values * values * values))
    return 0.5 * (1.0 + curved) + 0.5 * values * (1.0 - curved * curved) * BENDING * (
        1.0 + 3.0 * CUBIC_TERM * values * values
    )


def norm_parts(values):
    centre = values - jnp.mean(values, axis=-1, keepdims=True)
    spread = jnp.mean(centre * centre, axis=-1, keepdims=True)
    inverse = lax.rsqrt(spread + EPSILON)
    return (centre * inverse, inverse)


def norm_back(upstream, normal_rows, inverse, scale_row):
    scaled = upstream * scale_row
    return inverse * (
        scaled
        - jnp.mean(scaled, axis=-1, keepdims=True)
        - normal_rows * jnp.mean(scaled * normal_rows, axis=-1, keepdims=True)
    )


def piece_index(positions, starts):
    opening = starts[:, 0:1]
    closing = starts[:, 1:2]
    inside_first = (positions[None, :] >= opening) & (positions[None, :] < opening + PIECE)
    inside_second = (positions[None, :] >= closing) & (positions[None, :] < closing + PIECE)
    return jnp.where(inside_first, 0, jnp.where(inside_second, 1, -1))


def visible_pairs(starts, query_places, key_places):
    query_piece = piece_index(query_places, starts)
    key_piece = piece_index(key_places, starts)
    causal = key_places[None, :] <= query_places[:, None]
    joined = (query_piece[:, :, None] == key_piece[:, None, :]) & (query_piece[:, :, None] >= 0)
    return causal[None] | joined


def split_heads(rows):
    return rows.reshape(rows.shape[0], rows.shape[1], rows.shape[2] // HEAD_DIM, HEAD_DIM)


def join_heads(rows):
    return rows.reshape(rows.shape[0], rows.shape[1], rows.shape[2] * rows.shape[3])


def score_block(queries, key_rows, visible):
    scores = jnp.einsum(
        "sqhd,skhd->shqk",
        split_heads(queries),
        split_heads(key_rows),
        preferred_element_type=jnp.float32,
    ) * HEAD_DIM ** (-0.5)
    return jnp.where(visible[:, None], scores, NEGATIVE)


def fetch_weights(shards):
    within = (
        lax.all_gather(shards[0], "seq", axis=0, tiled=True),
        lax.all_gather(shards[1], "seq", axis=0, tiled=True),
        lax.all_gather(shards[2], "seq", axis=1, tiled=True),
        lax.all_gather(shards[3], "seq", axis=0, tiled=True),
        lax.all_gather(shards[4], "seq", axis=1, tiled=True),
        lax.all_gather(shards[5], "seq", axis=1, tiled=True),
        lax.all_gather(shards[6], "seq", axis=0, tiled=True),
        lax.all_gather(shards[7], "seq", axis=1, tiled=True),
        lax.all_gather(shards[8], "seq", axis=0, tiled=True),
        lax.all_gather(shards[9], "seq", axis=0, tiled=True),
        lax.all_gather(shards[10], "seq", axis=0, tiled=True),
        lax.all_gather(shards[11], "seq", axis=1, tiled=True),
        lax.all_gather(shards[12], "seq", axis=0, tiled=True),
        lax.all_gather(shards[13], "seq", axis=1, tiled=True),
        lax.all_gather(shards[14], "seq", axis=0, tiled=True),
    )
    return (
        lax.all_gather(within[0], "dp", axis=0, tiled=True),
        lax.all_gather(within[1], "dp", axis=0, tiled=True),
        lax.all_gather(within[2], "dp", axis=0, tiled=True),
        lax.all_gather(within[3], "dp", axis=0, tiled=True),
        lax.all_gather(within[4], "dp", axis=0, tiled=True),
        lax.all_gather(within[5], "dp", axis=0, tiled=True),
        lax.all_gather(within[6], "dp", axis=0, tiled=True),
        lax.all_gather(within[7], "dp", axis=0, tiled=True),
        lax.all_gather(within[8], "dp", axis=0, tiled=True),
        lax.all_gather(within[9], "dp", axis=0, tiled=True),
        lax.all_gather(within[10], "dp", axis=0, tiled=True),
        lax.all_gather(within[11], "dp", axis=0, tiled=True),
        lax.all_gather(within[12], "dp", axis=0, tiled=True),
        lax.all_gather(within[13], "dp", axis=0, tiled=True),
        lax.all_gather(within[14], "dp", axis=0, tiled=True),
    )


def fetch_again(shards):
    within = (
        lax.all_gather(shards[0], "seq", axis=0, tiled=True),
        lax.all_gather(shards[1], "seq", axis=0, tiled=True),
        lax.all_gather(shards[2], "seq", axis=1, tiled=True),
        lax.all_gather(shards[3], "seq", axis=0, tiled=True),
        lax.all_gather(shards[4], "seq", axis=1, tiled=True),
        lax.all_gather(shards[5], "seq", axis=1, tiled=True),
        lax.all_gather(shards[6], "seq", axis=0, tiled=True),
        lax.all_gather(shards[7], "seq", axis=1, tiled=True),
        lax.all_gather(shards[8], "seq", axis=0, tiled=True),
        lax.all_gather(shards[9], "seq", axis=0, tiled=True),
        lax.all_gather(shards[10], "seq", axis=0, tiled=True),
        lax.all_gather(shards[11], "seq", axis=1, tiled=True),
        lax.all_gather(shards[12], "seq", axis=0, tiled=True),
        lax.all_gather(shards[13], "seq", axis=1, tiled=True),
        lax.all_gather(shards[14], "seq", axis=0, tiled=True),
    )
    return (
        lax.all_gather(within[0], "dp", axis=0, tiled=True),
        lax.all_gather(within[1], "dp", axis=0, tiled=True),
        lax.all_gather(within[2], "dp", axis=0, tiled=True),
        lax.all_gather(within[3], "dp", axis=0, tiled=True),
        lax.all_gather(within[4], "dp", axis=0, tiled=True),
        lax.all_gather(within[5], "dp", axis=0, tiled=True),
        lax.all_gather(within[6], "dp", axis=0, tiled=True),
        lax.all_gather(within[7], "dp", axis=0, tiled=True),
        lax.all_gather(within[8], "dp", axis=0, tiled=True),
        lax.all_gather(within[9], "dp", axis=0, tiled=True),
        lax.all_gather(within[10], "dp", axis=0, tiled=True),
        lax.all_gather(within[11], "dp", axis=0, tiled=True),
        lax.all_gather(within[12], "dp", axis=0, tiled=True),
        lax.all_gather(within[13], "dp", axis=0, tiled=True),
        lax.all_gather(within[14], "dp", axis=0, tiled=True),
    )


def return_grads(grads):
    folded = (
        lax.psum_scatter(
            grads[0].astype(jnp.bfloat16), "dp", scatter_dimension=0, tiled=True
        ).astype(jnp.float32),
        lax.psum_scatter(
            grads[1].astype(jnp.bfloat16), "dp", scatter_dimension=0, tiled=True
        ).astype(jnp.float32),
        lax.psum_scatter(
            grads[2].astype(jnp.bfloat16), "dp", scatter_dimension=0, tiled=True
        ).astype(jnp.float32),
        lax.psum_scatter(
            grads[3].astype(jnp.bfloat16), "dp", scatter_dimension=0, tiled=True
        ).astype(jnp.float32),
        lax.psum_scatter(
            grads[4].astype(jnp.bfloat16), "dp", scatter_dimension=0, tiled=True
        ).astype(jnp.float32),
        lax.psum_scatter(
            grads[5].astype(jnp.bfloat16), "dp", scatter_dimension=0, tiled=True
        ).astype(jnp.float32),
        lax.psum_scatter(
            grads[6].astype(jnp.bfloat16), "dp", scatter_dimension=0, tiled=True
        ).astype(jnp.float32),
        lax.psum_scatter(
            grads[7].astype(jnp.bfloat16), "dp", scatter_dimension=0, tiled=True
        ).astype(jnp.float32),
        lax.psum_scatter(
            grads[8].astype(jnp.bfloat16), "dp", scatter_dimension=0, tiled=True
        ).astype(jnp.float32),
        lax.psum_scatter(
            grads[9].astype(jnp.bfloat16), "dp", scatter_dimension=0, tiled=True
        ).astype(jnp.float32),
        lax.psum_scatter(
            grads[10].astype(jnp.bfloat16), "dp", scatter_dimension=0, tiled=True
        ).astype(jnp.float32),
        lax.psum_scatter(
            grads[11].astype(jnp.bfloat16), "dp", scatter_dimension=0, tiled=True
        ).astype(jnp.float32),
        lax.psum_scatter(
            grads[12].astype(jnp.bfloat16), "dp", scatter_dimension=0, tiled=True
        ).astype(jnp.float32),
        lax.psum_scatter(
            grads[13].astype(jnp.bfloat16), "dp", scatter_dimension=0, tiled=True
        ).astype(jnp.float32),
        lax.psum_scatter(
            grads[14].astype(jnp.bfloat16), "dp", scatter_dimension=0, tiled=True
        ).astype(jnp.float32),
    )
    return (
        lax.psum_scatter(
            folded[0].astype(jnp.bfloat16), "seq", scatter_dimension=0, tiled=True
        ).astype(jnp.float32),
        lax.psum_scatter(
            folded[1].astype(jnp.bfloat16), "seq", scatter_dimension=0, tiled=True
        ).astype(jnp.float32),
        lax.psum_scatter(
            folded[2].astype(jnp.bfloat16), "seq", scatter_dimension=1, tiled=True
        ).astype(jnp.float32),
        lax.psum_scatter(
            folded[3].astype(jnp.bfloat16), "seq", scatter_dimension=0, tiled=True
        ).astype(jnp.float32),
        lax.psum_scatter(
            folded[4].astype(jnp.bfloat16), "seq", scatter_dimension=1, tiled=True
        ).astype(jnp.float32),
        lax.psum_scatter(
            folded[5].astype(jnp.bfloat16), "seq", scatter_dimension=1, tiled=True
        ).astype(jnp.float32),
        lax.psum_scatter(
            folded[6].astype(jnp.bfloat16), "seq", scatter_dimension=0, tiled=True
        ).astype(jnp.float32),
        lax.psum_scatter(
            folded[7].astype(jnp.bfloat16), "seq", scatter_dimension=1, tiled=True
        ).astype(jnp.float32),
        lax.psum_scatter(
            folded[8].astype(jnp.bfloat16), "seq", scatter_dimension=0, tiled=True
        ).astype(jnp.float32),
        lax.psum_scatter(
            folded[9].astype(jnp.bfloat16), "seq", scatter_dimension=0, tiled=True
        ).astype(jnp.float32),
        lax.psum_scatter(
            folded[10].astype(jnp.bfloat16), "seq", scatter_dimension=0, tiled=True
        ).astype(jnp.float32),
        lax.psum_scatter(
            folded[11].astype(jnp.bfloat16), "seq", scatter_dimension=1, tiled=True
        ).astype(jnp.float32),
        lax.psum_scatter(
            folded[12].astype(jnp.bfloat16), "seq", scatter_dimension=0, tiled=True
        ).astype(jnp.float32),
        lax.psum_scatter(
            folded[13].astype(jnp.bfloat16), "seq", scatter_dimension=1, tiled=True
        ).astype(jnp.float32),
        lax.psum_scatter(
            folded[14].astype(jnp.bfloat16), "seq", scatter_dimension=0, tiled=True
        ).astype(jnp.float32),
    )


def token_sum(values):
    return jnp.sum(values.astype(jnp.float32), axis=(0, 1))


def body(
    tokens,
    first_gain,
    first_shift,
    query_weight,
    query_bias,
    key_weight,
    value_weight,
    value_bias,
    output_weight,
    output_bias,
    second_gain,
    second_shift,
    up_weight,
    up_bias,
    down_weight,
    down_bias,
    piece_starts,
    out_grad,
):
    shards = (
        first_gain,
        first_shift,
        query_weight,
        query_bias,
        key_weight,
        value_weight,
        value_bias,
        output_weight,
        output_bias,
        second_gain,
        second_shift,
        up_weight,
        up_bias,
        down_weight,
        down_bias,
    )
    fetched = fetch_weights(shards)
    (
        gain_one,
        shift_one,
        query_full,
        query_add,
        key_full,
        value_full,
        value_add,
        output_full,
        output_add,
        gain_two,
        shift_two,
        up_full,
        up_add,
        down_full,
        down_add,
    ) = fetched
    local_rows = tokens.shape[1]
    length = local_rows * lax.axis_size("seq")
    query_places = lax.axis_index("seq") * local_rows + jnp.arange(local_rows, dtype=jnp.int32)
    key_places = jnp.arange(length, dtype=jnp.int32)
    visible = visible_pairs(piece_starts, query_places, key_places)
    inputs = tokens.astype(jnp.float32)
    normal_one, inverse_one = norm_parts(inputs)
    normed_one = (normal_one * gain_one.astype(jnp.float32) + shift_one.astype(jnp.float32)).astype(
        jnp.bfloat16
    )
    queries = (
        jnp.dot(normed_one, query_full, preferred_element_type=jnp.float32)
        + query_add.astype(jnp.float32)
    ).astype(jnp.bfloat16)
    key_rows = jnp.dot(normed_one, key_full, preferred_element_type=jnp.float32).astype(
        jnp.bfloat16
    )
    value_rows = (
        jnp.dot(normed_one, value_full, preferred_element_type=jnp.float32)
        + value_add.astype(jnp.float32)
    ).astype(jnp.bfloat16)
    all_keys, all_values = (
        lax.all_gather(key_rows, "seq", axis=1, tiled=True),
        lax.all_gather(value_rows, "seq", axis=1, tiled=True),
    )
    scores = score_block(queries, all_keys, visible)
    highest = jnp.max(scores, axis=-1, keepdims=True)
    log_total = highest + jnp.log(jnp.sum(jnp.exp(scores - highest), axis=-1, keepdims=True))
    softened = jnp.exp(scores - log_total).astype(jnp.bfloat16)
    attended = join_heads(
        jnp.einsum(
            "shqk,skhd->sqhd", softened, split_heads(all_values), preferred_element_type=jnp.float32
        )
    ).astype(jnp.bfloat16)
    middle = inputs + (
        jnp.dot(attended, output_full, preferred_element_type=jnp.float32)
        + output_add.astype(jnp.float32)
    )
    normal_two, inverse_two = norm_parts(middle)
    normed_two = (normal_two * gain_two.astype(jnp.float32) + shift_two.astype(jnp.float32)).astype(
        jnp.bfloat16
    )
    before = jnp.dot(normed_two, up_full, preferred_element_type=jnp.float32) + up_add.astype(
        jnp.float32
    )
    active = smooth_gate(before).astype(jnp.bfloat16)
    output = (
        middle
        + (
            jnp.dot(active, down_full, preferred_element_type=jnp.float32)
            + down_add.astype(jnp.float32)
        )
    ).astype(jnp.bfloat16)
    backing = fetch_again(shards)
    (
        gain_one,
        shift_one,
        query_full,
        query_add,
        key_full,
        value_full,
        value_add,
        output_full,
        output_add,
        gain_two,
        shift_two,
        up_full,
        up_add,
        down_full,
        down_add,
    ) = backing
    incoming = out_grad.astype(jnp.float32)
    down_grad = jnp.einsum("stf,std->fd", active, out_grad, preferred_element_type=jnp.float32)
    down_add_grad = jnp.sum(incoming, axis=(0, 1))
    before_grad = (
        smooth_slope(before)
        * jnp.einsum("std,fd->stf", out_grad, down_full, preferred_element_type=jnp.float32)
    ).astype(jnp.bfloat16)
    up_grad = jnp.einsum("std,stf->df", normed_two, before_grad, preferred_element_type=jnp.float32)
    up_add_grad = token_sum(before_grad)
    normed_two_grad = jnp.einsum(
        "stf,df->std", before_grad, up_full, preferred_element_type=jnp.float32
    )
    gain_two_grad = jnp.sum(normed_two_grad * normal_two, axis=(0, 1))
    shift_two_grad = jnp.sum(normed_two_grad, axis=(0, 1))
    middle_grad = incoming + norm_back(
        normed_two_grad, normal_two, inverse_two, gain_two.astype(jnp.float32)
    )
    branch_grad = middle_grad.astype(jnp.bfloat16)
    output_matrix_grad = jnp.einsum(
        "std,ste->de", attended, branch_grad, preferred_element_type=jnp.float32
    )
    output_add_grad = token_sum(branch_grad)
    attended_grad = jnp.einsum(
        "ste,de->std", branch_grad, output_full, preferred_element_type=jnp.float32
    ).astype(jnp.bfloat16)
    back_keys, back_values = (
        lax.all_gather(key_rows, "seq", axis=1, tiled=True),
        lax.all_gather(value_rows, "seq", axis=1, tiled=True),
    )
    scores = score_block(queries, back_keys, visible)
    chances = jnp.exp(scores - log_total)
    chance_grad = jnp.einsum(
        "sqhd,skhd->shqk",
        split_heads(attended_grad),
        split_heads(back_values),
        preferred_element_type=jnp.float32,
    )
    settled = jnp.sum(chances * chance_grad, axis=-1, keepdims=True)
    score_grad = (chances * (chance_grad - settled)).astype(jnp.bfloat16)
    queries_grad = (
        join_heads(
            jnp.einsum(
                "shqk,skhd->sqhd",
                score_grad,
                split_heads(back_keys),
                preferred_element_type=jnp.float32,
            )
        )
        * HEAD_DIM ** (-0.5)
    ).astype(jnp.bfloat16)
    key_terms = join_heads(
        jnp.einsum(
            "shqk,sqhd->skhd", score_grad, split_heads(queries), preferred_element_type=jnp.float32
        )
    ) * HEAD_DIM ** (-0.5)
    value_terms = join_heads(
        jnp.einsum(
            "shqk,sqhd->skhd",
            chances.astype(jnp.bfloat16),
            split_heads(attended_grad),
            preferred_element_type=jnp.float32,
        )
    )
    key_sums, value_sums = (
        lax.psum_scatter(
            key_terms.astype(jnp.bfloat16), "seq", scatter_dimension=1, tiled=True
        ).astype(jnp.float32),
        lax.psum_scatter(
            value_terms.astype(jnp.bfloat16), "seq", scatter_dimension=1, tiled=True
        ).astype(jnp.float32),
    )
    keys_grad = key_sums.astype(jnp.bfloat16)
    values_grad = value_sums.astype(jnp.bfloat16)
    query_matrix_grad = jnp.einsum(
        "std,ste->de", normed_one, queries_grad, preferred_element_type=jnp.float32
    )
    query_add_grad = token_sum(queries_grad)
    key_matrix_grad = jnp.einsum(
        "std,ste->de", normed_one, keys_grad, preferred_element_type=jnp.float32
    )
    value_matrix_grad = jnp.einsum(
        "std,ste->de", normed_one, values_grad, preferred_element_type=jnp.float32
    )
    value_add_grad = token_sum(values_grad)
    normed_one_grad = (
        jnp.einsum("ste,de->std", queries_grad, query_full, preferred_element_type=jnp.float32)
        + jnp.einsum("ste,de->std", keys_grad, key_full, preferred_element_type=jnp.float32)
        + jnp.einsum("ste,de->std", values_grad, value_full, preferred_element_type=jnp.float32)
    )
    gain_one_grad = jnp.sum(normed_one_grad * normal_one, axis=(0, 1))
    shift_one_grad = jnp.sum(normed_one_grad, axis=(0, 1))
    input_grad = (
        middle_grad
        + norm_back(normed_one_grad, normal_one, inverse_one, gain_one.astype(jnp.float32))
    ).astype(jnp.bfloat16)
    summed = return_grads(
        (
            gain_one_grad,
            shift_one_grad,
            query_matrix_grad,
            query_add_grad,
            key_matrix_grad,
            value_matrix_grad,
            value_add_grad,
            output_matrix_grad,
            output_add_grad,
            gain_two_grad,
            shift_two_grad,
            up_grad,
            up_add_grad,
            down_grad,
            down_add_grad,
        )
    )
    return (
        output,
        input_grad,
        summed[0],
        summed[1],
        summed[2],
        summed[3],
        summed[4],
        summed[5],
        summed[6],
        summed[7],
        summed[8],
        summed[9],
        summed[10],
        summed[11],
        summed[12],
        summed[13],
        summed[14],
    )


def solution(mesh):
    in_specs = (
        P("dp", "seq", None),
        P(("dp", "seq")),
        P(("dp", "seq")),
        P("dp", "seq"),
        P(("dp", "seq")),
        P("dp", "seq"),
        P("dp", "seq"),
        P(("dp", "seq")),
        P("dp", "seq"),
        P(("dp", "seq")),
        P(("dp", "seq")),
        P(("dp", "seq")),
        P("dp", "seq"),
        P(("dp", "seq")),
        P("dp", "seq"),
        P(("dp", "seq")),
        P("dp", None),
        P("dp", "seq", None),
    )
    out_specs = (
        P("dp", "seq", None),
        P("dp", "seq", None),
        P(("dp", "seq")),
        P(("dp", "seq")),
        P("dp", "seq"),
        P(("dp", "seq")),
        P("dp", "seq"),
        P("dp", "seq"),
        P(("dp", "seq")),
        P("dp", "seq"),
        P(("dp", "seq")),
        P(("dp", "seq")),
        P(("dp", "seq")),
        P("dp", "seq"),
        P(("dp", "seq")),
        P("dp", "seq"),
        P(("dp", "seq")),
    )
    return jax.shard_map(body, mesh=mesh, in_specs=in_specs, out_specs=out_specs, check_vma=False)
```

profile of v0, /device:TPU:0, one launch (start us, length us, event | category | flops | bytes accessed | tf_op | source)
XLA Modules:
  0.0 1635.4 jit_solution(3323225138705528250)
XLA Ops:
  7.2 7.6 all_gather.127
  14.9 5.3 all_gather.118
  20.3 6.1 all_gather.123
  36.0 5.4 all-reduce.37
  42.8 58.2 %all-reduce.35 = (bf16[1024]{0:T(1024)(128)(2,1)S(1)}, bf16[1024]{0:T(1024)(128)(2,1)S(1)}, bf16[1024]{0:T(1024)(128)(2,1)S(1)}, bf16[1024]{0:T(1024)(128)(2,1)S...) all-reduce(bf16[1024]{0:T(1024)(128)(2,1)S(1)} %dynamic-update-slic, ...), channel_id=1, replica_groups=mesh['dp'=16,'seq'=2] {'dp'}, use_global_device_ids=true, to_apply=%add.9 | all-reduce | flops 7168 | bytes 28672
  101.0 2.8 convert_reduce_fusion
  103.9 3.0 fusion.23
  106.9 9.9 convolution_convert_fusion.3
  117.4 10.0 add_convert_fusion.3
  127.5 5.8 all_gather.130
  133.4 9.5 all_gather.138
  143.0 7.2 all_gather.142
  150.9 4.2 all-gather
  156.9 17.1 %all-gather.1 = bf16[16,1,256]{2,1,0:T(2,128)(2,1)S(1)} all-gather(bf16[1,1,256]{2,1,0:T(2,128)(2,1)S(1)} %bitcast.123), channel_id=1, replica_groups=mesh['dp'=16,'seq'=2] {'dp'}, dimensions={0}, use_global_device_ids=true | all-gather | bytes 8704 | tf_op jit(solution)/shard_map/all_gather | solution.py:112
  174.6 2.0 and_or_fusion
  176.7 10.6 add_convert_fusion.2
  187.4 6.2 copy.68
  193.6 52.4 %all-gather.19.cloned.1.call-done = bf16[4,1024,1024]{2,1,0:T(8,128)(2,1)} async-done(((bf16[4,512,1024]{2,1,0:T(8,128)(2,1)}), bf16[4,1024,1024]{2,1,0:T(8,128)(2,1)}) %all-gather.19.cloned.1.call-update) | async-done | bytes 8388624 | tf_op jit(solution)/shard_map/all_gather | solution.py:333
  245.9 11.6 copy.69
  257.6 51.7 %fusion = (f32[4,16,512]{2,1,0:T(8,128)S(1)}, f32[4,16,512,1024]{3,2,1,0:T(8,128)}) fusion(pred[4,512,1024]{2,1,0:T(8,128)(4,1)S(1)} %and_or_fusion, bf16[4,512,16,64]{1,3,2,0:T(8,128)(2,1)} %bitcast.111, bf16[4,1024,16,64]{1,3,2,0:T(8,128)(2,1)} %bitcast.109), kind=kOutput, calls=%fused_computation.5 | convolution fusion | flops 4395597824 | bytes 149028864 | tf_op jit(solution)/shard_map/sqhd,skhd->shqk/dot_general | solution.py:72
  309.3 41.3 %exponential_reduce_fusion = f32[4,16,512]{2,1,0:T(8,128)S(1)} fusion(f32[4,16,512,1024]{3,2,1,0:T(8,128)} %get-tuple-element.71, f32[4,16,512]{2,1,0:T(8,128)S(1)} %get-tuple-element.70, pred[4,512,1024]{2,1,0:T(8,128)(4,1)S(1)} %and_or_fusion), kind=kLoop, calls=%fused_computation.3 | loop fusion | flops 134184960 | bytes 136577024 | tf_op jit(solution)/shard_map/reduce_sum | solution.py:338
  352.0 11.4 copy.67
  363.5 50.6 %convolution_convert_fusion.1 = bf16[4,16,64,512]{3,2,1,0:T(8,128)(2,1)} fusion(bf16[4,1024,16,64]{1,3,2,0:T(8,128)(2,1)} %bitcast.113, f32[4,16,512,1024]{3,2,1,0:T(8,128)} %get-tuple-element.71, f32[4,16,512]{2,1,0:T(8,128)S(1)} %log_add_fusion, pred[4,512,1024]{2,1,0:T(8,128)(4,1)S(1)} %and_or_fusion), kind=kOutput, calls=%fused_computation.64 | convolution fusion | flops 4431282176 | bytes 149028864 | tf_op jit(solution)/shard_map/shqk,skhd->sqhd/dot_general | solution.py:341
  414.0 9.6 fusion.61
  423.7 3.1 copy-done.2
  428.0 43.3 %all-gather.23.cloned.1.call-done = bf16[1024,4096]{1,0:T(8,128)(2,1)} async-done(((bf16[64,4096]{1,0:T(8,128)(2,1)}), bf16[1024,4096]{1,0:T(8,128)(2,1)}) %all-gather.23.cloned.1.call-update) | async-done | bytes 8388624 | tf_op jit(solution)/shard_map/all_gather | solution.py:111
  471.3 36.6 %multiply_convert_fusion.1 = (bf16[4,512,4096]{2,1,0:T(8,128)(2,1)}, f32[4,512,4096]{2,1,0:T(8,128)}) fusion(f32[4096]{0:T(1024)S(1)} %bitcast.121, bf16[1024,4096]{1,0:T(8,128)(2,1)} %all-gather.23.cloned.1.call-done, f32[4,512,1024]{2,1,0:T(8,128)} %copy-done.2, f32[1024]{0:T(1024)S(1)} %copy-done.33, f32[1024]{0:T(1024)S(1)} %copy-done.21, ...), kind=kOutput, calls=%fused_computation.16 | convolution fusion | flops 17274241024 | bytes 67149824 | tf_op jit(solution)/shard_map/dot_general | solution.py:353
  507.9 38.7 %all-gather.25.cloned.1.call-done = bf16[4096,1024]{1,0:T(8,128)(2,1)} async-done(((bf16[256,1024]{1,0:T(8,128)(2,1)}), bf16[4096,1024]{1,0:T(8,128)(2,1)}) %all-gather.25.cloned.1.call-update) | async-done | bytes 8388624 | tf_op jit(solution)/shard_map/all_gather | solution.py:113
  546.6 46.6 %fusion.63 = (bf16[4096]{0:T(1024)(128)(2,1)}, bf16[4,512,4096]{2,1,0:T(8,128)(2,1)}) fusion(bf16[4,512,1024]{2,1,0:T(8,128)(2,1)} %param.35, bf16[4096,1024]{1,0:T(8,128)(2,1)} %all-gather.25.cloned.1.call-done, f32[4,512,4096]{2,1,0:T(8,128)} %get-tuple-element.83, f32[4096]{0:T(1024)S(1)} %bitcast.122), kind=kOutput, calls=%fused_computation.121 | convolution fusion | flops 17356025856 | bytes 62939136 | tf_op jit(solution)/shard_map/std,fd->stf/dot_general | solution.py:387
  593.2 27.3 %multiply_reduce_fusion.1 = (bf16[1024]{0:T(1024)(128)(2,1)}, f32[4,512]{1,0:T(4,128)S(1)}, f32[4,512]{1,0:T(4,128)S(1)}, bf16[1024]{0:T(1024)(128)(2,1)}, f32[4,512,1024]{2,1,0:T(8,128)}) fusion(f32[4,512,1024]{2,1,0:T(8,128)S(1)} %copy-done.3, f32[4,512]{1,0:T(4,128)S(1)} %add_rsqrt_fusion, f32[4,512]{1,0:T(4,128)S(1)} %broadcast_multiply_fusion.4, ...), kind=kOutput, calls=%fused_computation.45 | convolution fusion | flops 17198739456 | bytes 41984000 | tf_op jit(solution)/shard_map/stf,df->std/dot_general | solution.py:391
  620.6 8.8 convert_reduce_fusion.1
  629.4 3.3 copy-done.4
  632.7 5.7 bitcast_convert_fusion.2
  638.5 9.7 convolution_convert_fusion.2
  648.2 6.4 copy.71
  654.6 102.5 %multiply_reduce_fusion = (f32[4,16,512]{2,1,0:T(8,128)S(1)}, f32[4,16,512,1024]{3,2,1,0:T(8,128)}) fusion(f32[4,16,512,1024]{3,2,1,0:T(8,128)} %get-tuple-element.71, f32[4,16,512]{2,1,0:T(8,128)S(1)} %copy-done.6, pred[4,512,1024]{2,1,0:T(8,128)(4,1)S(1)} %copy-done.1, bf16[4,512,16,64]{1,3,2,0:T(8,128)(2,1)} %bitcast.116, ...), kind=kOutput, calls=%fused_computation.1 | convolution fusion | flops 4462706688 | bytes 283377664 | tf_op jit(solution)/shard_map/sqhd,skhd->shqk/dot_general | solution.py:413
  757.1 103.2 %multiply_convert_fusion = bf16[4,16,512,1024]{3,2,1,0:T(8,128)(2,1)} fusion(f32[4,16,512,1024]{3,2,1,0:T(8,128)} %get-tuple-element.76, f32[4,16,512,1024]{3,2,1,0:T(8,128)} %get-tuple-element.71, f32[4,16,512]{2,1,0:T(8,128)S(1)} %get-tuple-element.75, f32[4,16,512]{2,1,0:T(8,128)S(1)} %copy-done.6, pred[4,512,1024]{2,1,0:T(8,128)(4,1)S(1)} %copy-done.1), kind=kLoop, calls=%fused_computation | loop fusion | flops 201326592 | bytes 337903616 | tf_op jit(solution)/shard_map/convert_element_type | solution.py:420
  860.3 33.9 %fusion.62 = (bf16[16,64]{1,0:T(8,128)(2,1)}, bf16[4,16,64,512]{3,2,1,0:T(8,128)(2,1)}) fusion(bf16[4,1024,16,64]{1,3,2,0:T(8,128)(2,1)} %bitcast.110, bf16[4,16,512,1024]{3,2,1,0:T(8,128)(2,1)} %multiply_convert_fusion), kind=kOutput, calls=%fused_computation.120 | convolution fusion | flops 4301257728 | bytes 79693824 | tf_op jit(solution)/shard_map/shqk,skhd->sqhd/dot_general | solution.py:423
  894.3 9.9 bitcast_convert_fusion.5
  904.3 27.4 %bitcast_convert_fusion.1 = bf16[1024,4096]{1,0:T(8,128)(2,1)} fusion(bf16[4,512,4096]{2,1,0:T(8,128)(2,1)} %get-tuple-element.81, f32[4,512,1024]{2,1,0:T(8,128)} %copy-done.2, f32[1024]{0:T(1024)S(1)} %copy-done.34, f32[1024]{0:T(1024)S(1)} %copy-done.22, f32[4,512]{1,0:T(4,128)S(1)} %copy-done.19, f32[4,512]{1,0:T(4,128)S(1)} %copy-done.13), kind=kOutput, calls=%fused_computation.18 | convolution fusion | flops 17194549248 | bytes 33579008 | tf_op jit(solution)/shard_map/std,stf->df/dot_general | solution.py:389
  931.8 24.4 %bitcast_convert_fusion = bf16[4096,1024]{1,0:T(8,128)(2,1)} fusion(bf16[4,512,4096]{2,1,0:T(8,128)(2,1)} %get-tuple-element.82, bf16[4,512,1024]{2,1,0:T(8,128)(2,1)} %param.35), kind=kOutput, calls=%fused_computation.17 | convolution fusion | flops 17184063488 | bytes 29360128 | tf_op jit(solution)/shard_map/stf,std->fd/dot_general | solution.py:383
  957.1 7.4 reduce-scatter.19.cloned.1.call-done
  964.5 107.6 %reduce-scatter.35.cloned.1.call-done = bf16[64,4096]{1,0:T(8,128)(2,1)} async-done(((bf16[1024,4096]{1,0:T(8,128)(2,1)}), bf16[64,4096]{1,0:T(8,128)(2,1)}) %reduce-scatter.35.cloned.1.call-update) | async-done | bytes 524304 | tf_op jit(solution)/shard_map/reduce_scatter | solution.py:190
  1072.3 108.2 %reduce-scatter.39.cloned.1.call-done = bf16[256,1024]{1,0:T(8,128)(2,1)} async-done(((bf16[4096,1024]{1,0:T(8,128)(2,1)}), bf16[256,1024]{1,0:T(8,128)(2,1)}) %reduce-scatter.39.cloned.1.call-update) | async-done | bytes 524304 | tf_op jit(solution)/shard_map/reduce_scatter | solution.py:196
  1180.6 52.8 %convolution_convert_fusion = bf16[4,16,64,1024]{3,2,1,0:T(8,128)(2,1)} fusion(bf16[4,512,16,64]{1,3,2,0:T(8,128)(2,1)} %bitcast.117, f32[4,16,512,1024]{3,2,1,0:T(8,128)} %get-tuple-element.71, f32[4,16,512]{2,1,0:T(8,128)S(1)} %copy-done.6, pred[4,512,1024]{2,1,0:T(8,128)(4,1)S(1)} %copy-done.1), kind=kOutput, calls=%fused_computation.59 | convolution fusion | flops 4433379328 | bytes 149028864 | tf_op jit(solution)/shard_map/shqk,sqhd->skhd/dot_general | solution.py:438
  1233.3 11.4 copy.74
  1244.8 29.6 %multiply_convert_fusion.2 = bf16[4,16,64,1024]{3,2,1,0:T(8,128)(2,1)} fusion(bf16[4,512,16,64]{1,3,2,0:T(8,128)(2,1)} %bitcast.112, bf16[4,16,512,1024]{3,2,1,0:T(8,128)(2,1)} %multiply_convert_fusion), kind=kOutput, calls=%fused_computation.19 | convolution fusion | flops 4303355904 | bytes 79691776 | tf_op jit(solution)/shard_map/shqk,sqhd->skhd/dot_general | solution.py:433
  1274.4 11.7 copy.73
  1289.3 9.1 fusion.38
  1303.1 1.8 convert_element_type.290
  1304.9 39.0 %reduce-scatter.17.cloned.1.call-done = bf16[4,512,1024]{2,1,0:T(8,128)(2,1)} async-done(((bf16[4,1024,1024]{2,1,0:T(8,128)(2,1)}), bf16[4,512,1024]{2,1,0:T(8,128)(2,1)}) %reduce-scatter.17.cloned.1.call-update) | async-done | bytes 4194320 | tf_op jit(solution)/shard_map/reduce_scatter | solution.py:449
  1343.9 10.1 bitcast_convert_fusion.3
  1354.1 91.4 %reduce-scatter.15.cloned.1.call-done = bf16[4,512,1024]{2,1,0:T(8,128)(2,1)} async-done(((bf16[4,1024,1024]{2,1,0:T(8,128)(2,1)}), bf16[4,512,1024]{2,1,0:T(8,128)(2,1)}) %reduce-scatter.15.cloned.1.call-update) | async-done | bytes 4194320 | tf_op jit(solution)/shard_map/reduce_scatter | solution.py:446
  1445.4 9.3 fusion.35
  1454.7 3.0 reduce_sum.202
  1457.7 14.9 fusion.22
  1472.7 61.5 %all-reduce.34 = (bf16[1024]{0:T(1024)(128)(2,1)S(1)}, bf16[1024]{0:T(1024)(128)(2,1)S(1)}, bf16[1024]{0:T(1024)(128)(2,1)S(1)}, bf16[1024]{0:T(1024)(128)(2,1)S...) all-reduce(bf16[1024]{0:T(1024)(128)(2,1)S(1)} %dynamic-update-slic, ...), channel_id=1, replica_groups=mesh['dp'=16,'seq'=2] {'dp'}, use_global_device_ids=true, to_apply=%add.15 | all-reduce | flops 13312 | bytes 53248
  1534.2 10.0 bitcast_convert_fusion.4
  1544.3 24.9 %add_convert_fusion = bf16[4,512,1024]{2,1,0:T(8,128)(2,1)} fusion(f32[4,512,1024]{2,1,0:T(8,128)} %copy-done.2, f32[1024]{0:T(1024)S(1)} %convert_element_type.250, bf16[4,512,4096]{2,1,0:T(8,128)(2,1)} %get-tuple-element.82, bf16[4096,1024]{1,0:T(8,128)(2,1)} %all-gather.25.cloned.1.call-done), kind=kOutput, calls=%fused_computation.50 | convolution fusion | flops 17186160640 | bytes 37752832 | tf_op jit(solution)/shard_map/dot_general | solution.py:360
  1569.9 5.0 all-reduce.36
  1576.6 10.7 fusion.21
  1589.2 13.5 reduce-scatter.23.cloned.1.call-done
  1604.4 9.7 reduce-scatter.29.cloned.1.call-done
  1615.7 11.0 reduce-scatter.25.cloned.1.call-done
  (225 shorter events, 31.8 us)
Async XLA Ops:
  7.2 99.7 %all-gather.17.cloned.1.call-start = ((), (), s32[]{:S(2)}) async-start(), calls=%async_computation.17 | async-start | bytes 2228224 | tf_op jit(solution)/shard_map/all_gather | solution.py:104
  14.9 102.5 %all-gather.11.cloned.1.call-start = ((), (), s32[]{:S(2)}) async-start(), calls=%async_computation.14 | async-start | bytes 2228224 | tf_op jit(solution)/shard_map/all_gather | solution.py:105
  20.2 156.4 %all-gather.15.cloned.1.call-start = ((), (), s32[]{:S(2)}) async-start(), calls=%async_computation.16 | async-start | bytes 2228224 | tf_op jit(solution)/shard_map/all_gather | solution.py:102
  26.4 219.5 %all-gather.19.cloned.1.call-start = ((), (), s32[]{:S(2)}) async-start(), calls=%async_computation.18 | async-start | bytes 12582912 | tf_op jit(solution)/shard_map/all_gather | solution.py:333
  101.0 75.7 %copy-start.24 = (f32[1024]{0:T(1024)}, f32[1024]{0:T(1024)S(1)}, u32[]{:S(2)}) copy-start(f32[1024]{0:T(1024)S(1)} %convert_element_type.232) | copy-start | bytes 12292
  101.0 75.7 %copy-start.30 = (f32[1024]{0:T(1024)}, f32[1024]{0:T(1024)S(1)}, u32[]{:S(2)}) copy-start(f32[1024]{0:T(1024)S(1)} %convert_element_type.233) | copy-start | bytes 12292
  103.9 72.9 %copy-start.9 = (f32[4,512]{1,0:T(4,128)}, f32[4,512]{1,0:T(4,128)S(1)}, u32[]{:S(2)}) copy-start(f32[4,512]{1,0:T(4,128)S(1)} %broadcast_multiply_fusion.5) | copy-start | bytes 24580
  106.9 69.8 %copy-start.15 = (f32[4,512]{1,0:T(4,128)}, f32[4,512]{1,0:T(4,128)S(1)}, u32[]{:S(2)}) copy-start(f32[4,512]{1,0:T(4,128)S(1)} %add_rsqrt_fusion.1) | copy-start | bytes 24580
  116.9 235.1 %all-gather.13.cloned.1.call-start = ((), (), s32[]{:S(2)}) async-start(), calls=%async_computation.15 | async-start | bytes 12582912 | tf_op jit(solution)/shard_map/all_gather | solution.py:334
  117.3 10.1 copy-start.14
  117.3 16.0 copy-start.7
  117.3 25.6 %copy-start.8 = (bf16[256,512]{1,0:T(8,128)(2,1)S(1)}, bf16[256,512]{1,0:T(8,128)(2,1)}, u32[]{:S(2)}) copy-start(bf16[256,512]{1,0:T(8,128)(2,1)} %param.32) | copy-start | bytes 786436
  117.3 32.9 %copy-start.38 = (s32[4,2]{0,1:T(2,128)S(1)}, s32[4,2]{0,1:T(2,128)}, u32[]{:S(2)}) copy-start(s32[4,2]{0,1:T(2,128)} %param.34) | copy-start | bytes 100
  117.3 33.5 %copy-start.42 = (bf16[128]{0:T(256)(128)(2,1)S(1)}, bf16[128]{0:T(256)(128)(2,1)}, u32[]{:S(2)}) copy-start(bf16[128]{0:T(256)(128)(2,1)} %param.31) | copy-start | bytes 772
  127.4 286.6 %all-gather.21.cloned.1.call-start = ((), (), s32[]{:S(2)}) async-start(), calls=%async_computation.19 | async-start | bytes 2228224 | tf_op jit(solution)/shard_map/all_gather | solution.py:107
  133.3 338.0 %all-gather.23.cloned.1.call-start = ((), (), s32[]{:S(2)}) async-start(), calls=%async_computation.20 | async-start | bytes 8912896 | tf_op jit(solution)/shard_map/all_gather | solution.py:111
  142.9 403.7 %all-gather.25.cloned.1.call-start = ((), (), s32[]{:S(2)}) async-start(), calls=%async_computation.21 | async-start | bytes 8912896 | tf_op jit(solution)/shard_map/all_gather | solution.py:113
  150.1 806.2 %reduce-scatter.31.cloned.1.call-start = ((), (), s32[]{:S(2)}) async-start(), calls=%async_computation.30 | async-start | bytes 2228224 | tf_op jit(solution)/shard_map/reduce_scatter | solution.py:178
  176.6 186.8 %copy-start = (pred[4,512,1024]{2,1,0:T(8,128)(4,1)}, pred[4,512,1024]{2,1,0:T(8,128)(4,1)S(1)}, u32[]{:S(2)}) copy-start(pred[4,512,1024]{2,1,0:T(8,128)(4,1)S(1)} %and_or_fusion) | copy-start | bytes 6291460
  363.4 50.6 %copy-start.5 = (f32[4,16,512]{2,1,0:T(8,128)}, f32[4,16,512]{2,1,0:T(8,128)S(1)}, u32[]{:S(2)}) copy-start(f32[4,16,512]{2,1,0:T(8,128)S(1)} %log_add_fusion) | copy-start | bytes 393220
  363.4 50.6 %copy-start.35 = (f32[1024]{0:T(1024)S(1)}, f32[1024]{0:T(1024)}, u32[]{:S(2)}) copy-start(f32[1024]{0:T(1024)} %convert_element_type.244) | copy-start | bytes 12292
  423.6 3.2 copy-start.2
  423.7 47.6 %copy-start.21 = (f32[1024]{0:T(1024)S(1)}, f32[1024]{0:T(1024)}, u32[]{:S(2)}) copy-start(f32[1024]{0:T(1024)} %convert_element_type.245) | copy-start | bytes 12292
  423.7 47.6 %copy-start.23 = (f32[16,1,256]{2,1,0:T(1,128)S(1)}, f32[16,1,256]{2,1,0:T(1,128)}, u32[]{:S(2)}) copy-start(f32[16,1,256]{2,1,0:T(1,128)} %convert_element_type.292) | copy-start | bytes 49156
  423.7 47.6 %copy-start.33 = (f32[1024]{0:T(1024)S(1)}, f32[1024]{0:T(1024)}, u32[]{:S(2)}) copy-start(f32[1024]{0:T(1024)} %convert_element_type.246) | copy-start | bytes 12292
  423.7 196.9 %copy-start.12 = (f32[4,512]{1,0:T(4,128)}, f32[4,512]{1,0:T(4,128)S(1)}, u32[]{:S(2)}) copy-start(f32[4,512]{1,0:T(4,128)S(1)} %broadcast_multiply_fusion.4) | copy-start | bytes 24580
  428.0 192.6 %copy-start.18 = (f32[4,512]{1,0:T(4,128)}, f32[4,512]{1,0:T(4,128)S(1)}, u32[]{:S(2)}) copy-start(f32[4,512]{1,0:T(4,128)S(1)} %add_rsqrt_fusion) | copy-start | bytes 24580
  546.6 46.6 %copy-start.3 = (f32[4,512,1024]{2,1,0:T(8,128)S(1)}, f32[4,512,1024]{2,1,0:T(8,128)}, u32[]{:S(2)}) copy-start(f32[4,512,1024]{2,1,0:T(8,128)} %copy-done.2) | copy-start | bytes 25165828
  620.6 12.1 copy-start.44
  629.4 3.3 copy-start.4
  632.7 5.8 copy-start.41
  638.4 326.0 %reduce-scatter.19.cloned.1.call-start = ((), (), s32[]{:S(2)}) async-start(), calls=%async_computation.24 | async-start | bytes 2228224 | tf_op jit(solution)/shard_map/reduce_scatter | solution.py:163
  648.2 6.4 copy-start.1
  648.2 6.4 copy-start.6
  860.3 33.9 %copy-start.10 = (f32[4,512]{1,0:T(4,128)S(1)}, f32[4,512]{1,0:T(4,128)}, u32[]{:S(2)}) copy-start(f32[4,512]{1,0:T(4,128)} %copy-done.9) | copy-start | bytes 24580
  860.3 33.9 %copy-start.16 = (f32[4,512]{1,0:T(4,128)S(1)}, f32[4,512]{1,0:T(4,128)}, u32[]{:S(2)}) copy-start(f32[4,512]{1,0:T(4,128)} %copy-done.15) | copy-start | bytes 24580
  860.3 33.9 %copy-start.25 = (f32[1024]{0:T(1024)S(1)}, f32[1024]{0:T(1024)}, u32[]{:S(2)}) copy-start(f32[1024]{0:T(1024)} %copy-done.24) | copy-start | bytes 12292
  860.3 33.9 %copy-start.31 = (f32[1024]{0:T(1024)S(1)}, f32[1024]{0:T(1024)}, u32[]{:S(2)}) copy-start(f32[1024]{0:T(1024)} %copy-done.30) | copy-start | bytes 12292
  894.2 10.1 copy-start.13
  894.2 10.1 copy-start.19
  894.2 10.1 copy-start.22
  894.3 10.1 copy-start.34
  904.2 168.0 %reduce-scatter.35.cloned.1.call-start = ((), (), s32[]{:S(2)}) async-start(), calls=%async_computation.32 | async-start | bytes 8912896 | tf_op jit(solution)/shard_map/reduce_scatter | solution.py:190
  931.8 248.7 %reduce-scatter.39.cloned.1.call-start = ((), (), s32[]{:S(2)}) async-start(), calls=%async_computation.34 | async-start | bytes 8912896 | tf_op jit(solution)/shard_map/reduce_scatter | solution.py:196
  956.3 342.0 %reduce-scatter.33.cloned.1.call-start = ((), (), s32[]{:S(2)}) async-start(), calls=%async_computation.31 | async-start | bytes 196608 | tf_op jit(solution)/shard_map/reduce_scatter | solution.py:225
  957.1 342.8 %reduce-scatter.21.cloned.1.call-start = ((), (), s32[]{:S(2)}) async-start(), calls=%async_computation.25 | async-start | bytes 196608 | tf_op jit(solution)/shard_map/reduce_scatter | solution.py:210
  964.5 336.9 %reduce-scatter.37.cloned.1.call-start = ((), (), s32[]{:S(2)}) async-start(), calls=%async_computation.33 | async-start | bytes 786432 | tf_op jit(solution)/shard_map/reduce_scatter | solution.py:237
  1072.2 230.9 %reduce-scatter.41.cloned.1.call-start = ((), (), s32[]{:S(2)}) async-start(), calls=%async_computation.35 | async-start | bytes 786432 | tf_op jit(solution)/shard_map/reduce_scatter | solution.py:243
  1180.5 163.4 %reduce-scatter.17.cloned.1.call-start = ((), (), s32[]{:S(2)}) async-start(), calls=%async_computation.23 | async-start | bytes 12582912 | tf_op jit(solution)/shard_map/reduce_scatter | solution.py:449
  1244.8 200.7 %reduce-scatter.15.cloned.1.call-start = ((), (), s32[]{:S(2)}) async-start(), calls=%async_computation.22 | async-start | bytes 12582912 | tf_op jit(solution)/shard_map/reduce_scatter | solution.py:446
  1286.1 301.2 %reduce-scatter.27.cloned.1.call-start = ((), (), s32[]{:S(2)}) async-start(), calls=%async_computation.28 | async-start | bytes 2228224 | tf_op jit(solution)/shard_map/reduce_scatter | solution.py:172
  1289.2 54.7 %copy-start.11 = (f32[4,512]{1,0:T(4,128)S(1)}, f32[4,512]{1,0:T(4,128)}, u32[]{:S(2)}) copy-start(f32[4,512]{1,0:T(4,128)} %copy-done.9) | copy-start | bytes 24580
  1289.2 54.7 %copy-start.17 = (f32[4,512]{1,0:T(4,128)S(1)}, f32[4,512]{1,0:T(4,128)}, u32[]{:S(2)}) copy-start(f32[4,512]{1,0:T(4,128)} %copy-done.15) | copy-start | bytes 24580
  1289.3 54.7 %copy-start.26 = (f32[1024]{0:T(1024)S(1)}, f32[1024]{0:T(1024)}, u32[]{:S(2)}) copy-start(f32[1024]{0:T(1024)} %copy-done.24) | copy-start | bytes 12292
  1289.3 54.7 %copy-start.32 = (f32[1024]{0:T(1024)S(1)}, f32[1024]{0:T(1024)}, u32[]{:S(2)}) copy-start(f32[1024]{0:T(1024)} %copy-done.30) | copy-start | bytes 12292
  1304.9 140.5 %copy-start.39 = (bf16[1024,1024]{1,0:T(8,128)(2,1)S(1)}, bf16[1024,1024]{1,0:T(8,128)(2,1)}, u32[]{:S(2)}) copy-start(bf16[1024,1024]{1,0:T(8,128)(2,1)} %all-gather.17.cloned.1.call-done) | copy-start | bytes 6291460
  1354.0 248.6 %reduce-scatter.23.cloned.1.call-start = ((), (), s32[]{:S(2)}) async-start(), calls=%async_computation.26 | async-start | bytes 2228224 | tf_op jit(solution)/shard_map/reduce_scatter | solution.py:169
  1457.7 15.0 copy-start.27
  1457.7 15.0 copy-start.28
  1457.7 15.0 copy-start.29
  1457.7 15.0 copy-start.36
  1457.7 15.0 copy-start.37
  1544.3 69.9 %reduce-scatter.29.cloned.1.call-start = ((), (), s32[]{:S(2)}) async-start(), calls=%async_computation.29 | async-start | bytes 196608 | tf_op jit(solution)/shard_map/reduce_scatter | solution.py:219
  1587.4 39.3 %reduce-scatter.25.cloned.1.call-start = ((), (), s32[]{:S(2)}) async-start(), calls=%async_computation.27 | async-start | bytes 196608 | tf_op jit(solution)/shard_map/reduce_scatter | solution.py:216
  (3 other events, 9.1 us)
Sparse Core Ops, SparseCore 0:
  15.0 41.6 all-gather.16
  58.9 40.4 all-gather.10
  101.5 40.1 all-gather.14
  143.1 102.8 all-gather.18
  247.9 103.9 all-gather.12
  354.0 41.3 all-gather.20
  397.6 73.6 all-gather.22
  473.4 73.1 all-gather.24
  638.5 59.7 reduce-scatter.30
  904.4 60.0 reduce-scatter.18
  968.5 103.5 reduce-scatter.34
  1076.1 104.3 reduce-scatter.38
  1182.7 10.0 reduce-scatter.32
  1194.8 10.2 reduce-scatter.20
  1207.2 14.5 reduce-scatter.36
  1224.0 14.5 reduce-scatter.40
  1244.9 98.9 reduce-scatter.16
  1346.2 99.2 reduce-scatter.14
  1449.2 62.0 reduce-scatter.26
  1544.4 58.2 reduce-scatter.22
  1604.9 9.2 reduce-scatter.28
  1616.4 10.2 reduce-scatter.24
where the time goes:
time: 1650 us; the launch traced here: 1640 us
  matrix products  627 us (38%)
  waiting for transfers between devices  525 us (32%)
  other arithmetic  194 us (12%)
  blocking collectives  193 us (12%)
  local copies, waits for them, and re-layouts  75.9 us (5%)
  between operations  19.5 us (1%)
    unnamed x4, blocking collectives  130 us
    reduce_scatter x1, waiting for transfers between devices, return_grads(): lax.psum_scatter(grads[13].astype(jnp.bfloat16), 'dp', scatter_dimension=...  108 us
    reduce_scatter x1, waiting for transfers between devices, return_grads(): lax.psum_scatter(grads[11].astype(jnp.bfloat16), 'dp', scatter_dimension=...  108 us
    convert_element_type x1, other arithmetic, body(): score_grad = (chances * (chance_grad - settled)).astype(jnp.bfloat16)  103 us
    dot_general x1, matrix products, body(): jnp.einsum('sqhd,skhd->shqk', split_heads(attended_grad), split_heads(bac...  102 us
    reduce_scatter x1, waiting for transfers between devices, body(): lax.psum_scatter(key_terms.astype(jnp.bfloat16), 'seq', scatter_dimension...  91.4 us
    dot_general x1, matrix products, body(): jnp.einsum('shqk,sqhd->skhd', chances.astype(jnp.bfloat16), split_heads(a...  52.8 us
    all_gather x1, waiting for transfers between devices, body(): lax.all_gather(key_rows, 'seq', axis=1, tiled=True)  52.4 us
  transfers between devices with their start and end apart: 22, of which 12 were waited for; matrix products, arithmetic and copies ran while one was open for 49% of the time, Pallas kernels for 0%

commit v1 on v0

v1 whole, which is shorter than its diff:
```python
import functools
import math

import jax
import jax.numpy as jnp
from jax import lax
from jax.experimental import pallas as pl
from jax.experimental.pallas import tpu as pltpu
from jax.sharding import Mesh, PartitionSpec as P

HEAD_DIM = 64
PIECE = 256
NEGATIVE = -1e30
EPSILON = 1e-05
BENDING = math.sqrt(2.0 / math.pi)
CUBIC_TERM = 0.044715
SCALE = HEAD_DIM**-0.5
LOG2E = math.log2(math.e)

BF = jnp.bfloat16
F32 = jnp.float32
VMEM_LIMIT = 60 * 2**20

NN = (((1,), (0,)), ((), ()))
NT = (((1,), (1,)), ((), ()))
TN = (((0,), (0,)), ((), ()))


def dot(left, right, form):
    return lax.dot_general(left, right, form, preferred_element_type=F32)


def params():
    return pltpu.CompilerParams(vmem_limit_bytes=VMEM_LIMIT)


def cost(flops, nbytes, trans=0):
    return pl.CostEstimate(flops=int(flops), bytes_accessed=int(nbytes), transcendentals=int(trans))


def shape(dims, dtype):
    return jax.ShapeDtypeStruct(dims, dtype)


def once(block, index):
    return pl.BlockSpec(block, index, pipeline_mode=pl.Buffered(1))


def after(values, *earlier):
    return lax.optimization_barrier((values,) + earlier)[0]


def norm_parts(values):
    centre = values - jnp.mean(values, axis=-1, keepdims=True)
    inverse = lax.rsqrt(jnp.mean(centre * centre, axis=-1, keepdims=True) + EPSILON)
    return centre * inverse, inverse


def norm_back(upstream, hat, inverse, gain):
    scaled = upstream * gain
    return inverse * (
        scaled
        - jnp.mean(scaled, axis=-1, keepdims=True)
        - hat * jnp.mean(scaled * hat, axis=-1, keepdims=True)
    )


def fold(values):
    rows, columns = values.shape
    return jnp.sum(values.reshape(rows // 8, 8, columns), axis=0)


def accumulate(ref, values):
    @pl.when(pl.program_id(0) == 0)
    def _():
        ref[...] = values

    @pl.when(pl.program_id(0) > 0)
    def _():
        ref[...] += values


GAIN_ONE, SHIFT_ONE, QUERY_BIAS, VALUE_BIAS, OUTPUT_BIAS, GAIN_TWO, SHIFT_TWO, DOWN_BIAS = range(8)


def row(ref, index):
    return ref[index : index + 1, :]


def weight_columns(ref, j, rows=slice(None)):
    block = ref[:, j, rows, :]
    return block.reshape(block.shape[0] * block.shape[1], block.shape[2])


def project_body(x_ref, vec_ref, w_ref, x1_ref, q_ref, k_ref, v_ref):
    hat, _ = norm_parts(x_ref[...].astype(F32))
    x1 = (hat * row(vec_ref, GAIN_ONE) + row(vec_ref, SHIFT_ONE)).astype(BF)
    x1_ref[...] = x1
    groups, per, width = w_ref.shape[1], w_ref.shape[2] // 3, w_ref.shape[3]
    for m, (out, bias) in enumerate(((q_ref, QUERY_BIAS), (k_ref, None), (v_ref, VALUE_BIAS))):
        for j in range(groups):
            at = slice(j * width, (j + 1) * width)
            y = dot(x1, weight_columns(w_ref, j, slice(m * per, (m + 1) * per)), NN)
            if bias is not None:
                y = y + vec_ref[bias : bias + 1, at]
            out[:, at] = y.astype(BF)


def project(x, vec, first, tile):
    tokens, d = x.shape
    dp, g, rows, width = first.shape
    per = d // dp
    tok = pl.BlockSpec((tile, d), lambda i: (i, 0))
    return pl.pallas_call(
        project_body,
        grid=(tokens // tile,),
        in_specs=[tok, once((8, d), lambda i: (0, 0)), once((dp, g, 3 * per, width), lambda i: (0, 0, 0, 0))],
        out_specs=[tok] * 4,
        out_shape=[shape((tokens, d), BF)] * 4,
        compiler_params=params(),
        cost_estimate=cost(6 * tokens * d * d, 10 * tokens * d + 6 * d * d),
        name="project",
    )(x, vec, first)


def reach_of(places, first, second):
    in_first = (places >= first) & (places < first + PIECE)
    in_second = (places >= second) & (places < second + PIECE)
    return jnp.where(in_first, first + (PIECE - 1), jnp.where(in_second, second + (PIECE - 1), places))


def query_blocks(starts_ref, offset_ref, queries, keys, fixed_offset, run):
    b = pl.program_id(0)
    first, second = starts_ref[b, 0], starts_ref[b, 1]
    offset = offset_ref[0]
    block = min(256, queries)
    for n in range(queries // block):
        begin = offset + n * block
        last = reach_of(begin + (block - 1), first, second)
        places = begin + lax.broadcasted_iota(jnp.int32, (1, block), 1)
        reach = reach_of(places, first, second)
        if fixed_offset:
            options = range(n + 1, min(n + 2, keys // 256) + 1)
        else:
            options = range(1, keys // 256 + 1)
        for tiles in options:
            clear = n if fixed_offset else 0

            @pl.when((last >= (tiles - 1) * 256) & (last < tiles * 256))
            def _(n=n, tiles=tiles, clear=clear, reach=reach):
                run(slice(n * block, (n + 1) * block), clear * 256, tiles * 256, reach)


def hide(scores, clear, reach):
    span, block = scores.shape
    places = clear + lax.broadcasted_iota(jnp.int32, (span - clear, block), 0)
    tail = jnp.where(places <= reach, scores[clear:], NEGATIVE)
    return tail if clear == 0 else jnp.concatenate([scores[:clear], tail], axis=0)


def head_masks():
    lanes = lax.broadcasted_iota(jnp.int32, (1, 2 * HEAD_DIM), 1)
    return [lanes < HEAD_DIM, lanes >= HEAD_DIM]


def pick(mask, values):
    return jnp.where(mask, values, jnp.zeros_like(values))


def attend_body(fixed_offset, starts_ref, offset_ref, q_ref, k_ref, v_ref, out_ref, lse_ref):
    masks = head_masks()
    queries, keys = q_ref.shape[1], k_ref.shape[1]

    def run(at, clear, span, reach):
        q = q_ref[0, at, :]
        k = k_ref[0, :span, :]
        v = v_ref[0, :span, :]
        total = None
        scales = []
        for h in range(2):
            s = hide(dot(k, pick(masks[h], q), NT), clear, reach)
            top = jnp.max(s, axis=0, keepdims=True)
            p = jnp.exp2((s - top) * (SCALE * LOG2E))
            size = jnp.sum(p, axis=0, keepdims=True)
            lse_ref[0, 0, h : h + 1, at] = top * (SCALE * LOG2E) + jnp.log2(size)
            scales.append(1.0 / size)
            part = dot(pick(masks[h], v), p.astype(BF), TN)
            total = part if total is None else total + part
        half = HEAD_DIM
        out_ref[:half, at] = (total[:half] * scales[0]).astype(BF)
        out_ref[half:, at] = (total[half:] * scales[1]).astype(BF)

    query_blocks(starts_ref, offset_ref, queries, keys, fixed_offset, run)


def attend(starts, offset, q, k, v, fixed_offset):
    count, queries, d = q.shape
    keys = k.shape[1]
    pairs = d // 128
    rows = lambda n: pl.BlockSpec((1, n, 128), lambda b, p, *_: (b, 0, p))
    return pl.pallas_call(
        functools.partial(attend_body, fixed_offset),
        grid_spec=pltpu.PrefetchScalarGridSpec(
            num_scalar_prefetch=2,
            grid=(count, pairs),
            in_specs=[rows(queries), rows(keys), rows(keys)],
            out_specs=[
                pl.BlockSpec((128, queries), lambda b, p, *_: (p, b)),
                pl.BlockSpec((1, 1, 2, queries), lambda b, p, *_: (b, p, 0, 0)),
            ],
        ),
        out_shape=[shape((d, count * queries), BF), shape((count, pairs, 2, queries), F32)],
        compiler_params=params(),
        cost_estimate=cost(12 * count * queries * keys * d, 8 * count * keys * d, count * pairs * 2 * queries * keys),
        name="attend",
    )(starts, offset, q, k, v)


def attend_back_body(
    fixed_offset, starts_ref, offset_ref, q_ref, k_ref, v_ref, g_ref, lse_ref, dq_ref, dkv_ref, dk_acc, dv_acc
):
    masks = head_masks()
    queries, keys = q_ref.shape[1], k_ref.shape[1]
    dk_acc[...] = jnp.zeros_like(dk_acc)
    dv_acc[...] = jnp.zeros_like(dv_acc)

    def run(at, clear, span, reach):
        q = q_ref[0, at, :]
        g = g_ref[0, at, :]
        k = k_ref[0, :span, :]
        v = v_ref[0, :span, :]
        dq = None
        chances, slopes, qs, gs = [], [], [], []
        for h in range(2):
            qh, gh = pick(masks[h], q), pick(masks[h], g)
            s = hide(dot(k, qh, NT), clear, reach)
            p = jnp.exp2(s * (SCALE * LOG2E) - lse_ref[0, 0, h : h + 1, at])
            dp = dot(v, gh, NT)
            settled = jnp.sum(p * dp, axis=0, keepdims=True)
            ds = (p * (dp - settled)).astype(BF)
            part = dot(pick(masks[h], k), ds, TN)
            dq = part if dq is None else dq + part
            chances.append(p.astype(BF))
            slopes.append(ds)
            qs.append(qh)
            gs.append(gh)
        dv_acc[:span, :] += dot(jnp.concatenate(chances, axis=1), jnp.concatenate(gs, axis=0), NN)
        dk_acc[:span, :] += dot(jnp.concatenate(slopes, axis=1), jnp.concatenate(qs, axis=0), NN)
        dq_ref[0, at, :] = (dq.T * SCALE).astype(BF)

    query_blocks(starts_ref, offset_ref, queries, keys, fixed_offset, run)
    dkv_ref[0, 0] = (dk_acc[...] * SCALE).astype(BF)
    dkv_ref[1, 0] = dv_acc[...].astype(BF)


def attend_back(starts, offset, q, k, v, g, lse, fixed_offset):
    count, queries, d = q.shape
    keys = k.shape[1]
    pairs = d // 128
    rows = lambda n: pl.BlockSpec((1, n, 128), lambda b, p, *_: (b, 0, p))
    return pl.pallas_call(
        functools.partial(attend_back_body, fixed_offset),
        grid_spec=pltpu.PrefetchScalarGridSpec(
            num_scalar_prefetch=2,
            grid=(count, pairs),
            in_specs=[
                rows(queries),
                rows(keys),
                rows(keys),
                rows(queries),
                pl.BlockSpec((1, 1, 2, queries), lambda b, p, *_: (b, p, 0, 0)),
            ],
            out_specs=[
                rows(queries),
                pl.BlockSpec((2, 1, keys, 128), lambda b, p, *_: (0, b, 0, p)),
            ],
            scratch_shapes=[pltpu.VMEM((keys, 128), F32)] * 2,
        ),
        out_shape=[shape((count, queries, d), BF), shape((2, count, keys, d), BF)],
        compiler_params=params(),
        cost_estimate=cost(30 * count * queries * keys * d, 14 * count * keys * d, count * pairs * 2 * queries * keys),
        name="attend_back",
    )(starts, offset, q, k, v, g, lse)


def hidden_chunk(up_ref):
    return min(512, up_ref.shape[3])


def up_chunk(up_ref, n, size):
    per = up_ref.shape[3] // size
    block = up_ref[:, n // per, :, (n % per) * size : (n % per + 1) * size]
    return block.reshape(block.shape[0] * block.shape[1], size)


def rise_body(x_ref, att_ref, vec_ref, upb_ref, wo_ref, up_ref, mid_ref, x2_ref, act_ref, slope_ref):
    att = att_ref[...]
    width = wo_ref.shape[3]
    parts = [dot(att, weight_columns(wo_ref, j), TN) for j in range(wo_ref.shape[1])]
    branch = jnp.concatenate(parts, axis=1)
    middle = x_ref[...].astype(F32) + (branch + row(vec_ref, OUTPUT_BIAS))
    mid_ref[...] = middle
    hat, _ = norm_parts(middle)
    x2 = (hat * row(vec_ref, GAIN_TWO) + row(vec_ref, SHIFT_TWO)).astype(BF)
    x2_ref[...] = x2
    size = hidden_chunk(up_ref)
    for n in range(up_ref.shape[1] * up_ref.shape[3] // size):
        at = slice(n * size, (n + 1) * size)
        x = dot(x2, up_chunk(up_ref, n, size), NN) + upb_ref[:, at]
        square = x * x
        t = jnp.tanh(x * (BENDING + (BENDING * CUBIC_TERM) * square))
        half = 0.5 * (1.0 + t)
        act_ref[:, at] = (x * half).astype(BF)
        bend = (0.5 * BENDING) * x * (1.0 + (3.0 * CUBIC_TERM) * square)
        slope_ref[:, at] = (half + bend * (1.0 - t * t)).astype(BF)


def rise(x, att, vec, upb, first, up, tile):
    tokens, d = x.shape
    dp, g, _, width = first.shape
    per = d // dp
    ff = upb.shape[1]
    tok = pl.BlockSpec((tile, d), lambda i: (i, 0))
    wide = pl.BlockSpec((tile, ff), lambda i: (i, 0))
    return pl.pallas_call(
        rise_body,
        grid=(tokens // tile,),
        in_specs=[
            tok,
            pl.BlockSpec((d, tile), lambda i: (0, i)),
            once((8, d), lambda i: (0, 0)),
            once((1, ff), lambda i: (0, 0)),
            once((dp, g, per, width), lambda i: (0, 0, 3, 0)),
            once(up.shape, lambda i: (0, 0, 0, 0)),
        ],
        out_specs=[tok, tok, wide, wide],
        out_shape=[shape((tokens, d), F32), shape((tokens, d), BF), shape((tokens, ff), BF), shape((tokens, ff), BF)],
        compiler_params=params(),
        cost_estimate=cost(2 * tokens * d * (d + ff), tokens * (10 * d + 4 * ff) + 2 * d * (d + ff), tokens * ff),
        name="rise",
    )(x, att, vec, upb, first, up)


def fall_body(
    mid_ref, act_ref, slope_ref, og_ref, vec_ref, wo_ref, up_ref, down_ref,
    out_ref, bg_ref, mg_ref, br_ref, dat_ref, upb_ref, sums_ref,
):
    og = og_ref[...]
    incoming = og.astype(F32)
    g, width = down_ref.shape[1], down_ref.shape[3]
    size = hidden_chunk(up_ref)
    per = size // down_ref.shape[2]
    chunks = up_ref.shape[1] * up_ref.shape[3] // size
    outs = [None] * g
    e = None
    for n in range(chunks):
        at = slice(n * size, (n + 1) * size)
        act = act_ref[:, at]
        rise_grad = None
        for j in range(g):
            block = down_ref[n * per : (n + 1) * per, j].reshape(size, width)
            part = dot(og[:, j * width : (j + 1) * width], block, NT)
            rise_grad = part if rise_grad is None else rise_grad + part
            part = dot(act, block, NN)
            outs[j] = part if outs[j] is None else outs[j] + part
        bg = (slope_ref[:, at].astype(F32) * rise_grad).astype(BF)
        bg_ref[:, at] = bg
        accumulate(upb_ref.at[:, at], fold(bg.astype(F32)))
        part = dot(bg, up_chunk(up_ref, n, size), NT)
        e = part if e is None else e + part
    middle = mid_ref[...]
    out_ref[...] = (middle + (jnp.concatenate(outs, axis=1) + row(vec_ref, DOWN_BIAS))).astype(BF)
    hat, inverse = norm_parts(middle)
    middle_grad = incoming + norm_back(e, hat, inverse, row(vec_ref, GAIN_TWO))
    mg_ref[...] = middle_grad
    branch = middle_grad.astype(BF)
    br_ref[...] = branch
    back = None
    for j in range(wo_ref.shape[1]):
        part = dot(branch[:, j * width : (j + 1) * width], weight_columns(wo_ref, j), NT)
        back = part if back is None else back + part
    dat_ref[...] = back.astype(BF)
    accumulate(sums_ref.at[0], fold(e * hat))
    accumulate(sums_ref.at[1], fold(e))
    accumulate(sums_ref.at[2], fold(branch.astype(F32)))
    accumulate(sums_ref.at[3], fold(incoming))


def fall(middle, act, slope, og, vec, first, up, down, tile):
    tokens, d = og.shape
    dp, g, _, width = first.shape
    per = d // dp
    ff = act.shape[1]
    tok = pl.BlockSpec((tile, d), lambda i: (i, 0))
    wide = pl.BlockSpec((tile, ff), lambda i: (i, 0))
    return pl.pallas_call(
        fall_body,
        grid=(tokens // tile,),
        in_specs=[
            tok, wide, wide, tok,
            once((8, d), lambda i: (0, 0)),
            once((dp, g, per, width), lambda i: (0, 0, 3, 0)),
            once(up.shape, lambda i: (0, 0, 0, 0)),
            once(down.shape, lambda i: (0, 0, 0, 0)),
        ],
        out_specs=[
            tok, wide, tok, tok, tok,
            pl.BlockSpec((8, ff), lambda i: (0, 0)),
            pl.BlockSpec((4, 8, d), lambda i: (0, 0, 0)),
        ],
        out_shape=[
            shape((tokens, d), BF), shape((tokens, ff), BF), shape((tokens, d), F32), shape((tokens, d), BF),
            shape((tokens, d), BF), shape((8, ff), F32), shape((4, 8, d), F32),
        ],
        compiler_params=params(),
        cost_estimate=cost(2 * tokens * d * (d + 3 * ff), tokens * (16 * d + 6 * ff) + 2 * d * (d + 2 * ff)),
        name="fall",
    )(middle, act, slope, og, vec, first, up, down)


def split_cores(core_ref, values, keep_ref, send_ref):
    even, odd = values[:, 0], values[:, 1]
    mine = core_ref[0] == 0
    keep_ref[...] = jnp.where(mine, even, odd).astype(BF)
    send_ref[...] = jnp.where(mine, odd, even).astype(BF)


def down_grad_body(core_ref, act_ref, og_ref, keep_ref, send_ref):
    y = dot(act_ref[...], og_ref[...], TN)
    chips, g, rows, width = keep_ref.shape
    for j in range(g):
        part = y[:, j * width : (j + 1) * width].reshape(chips, 2, rows, width)
        split_cores(core_ref, part, keep_ref.at[:, j], send_ref.at[:, j])


def down_grad(core, act, og, dp, g):
    tokens, ff = act.shape
    d = og.shape[1]
    size = min(512, ff)
    rows, width = ff // dp, d // g
    chips = size // rows // 2
    out = pl.BlockSpec((chips, g, rows, width), lambda i, *_: (i, 0, 0, 0))
    return pl.pallas_call(
        down_grad_body,
        grid_spec=pltpu.PrefetchScalarGridSpec(
            num_scalar_prefetch=1,
            grid=(ff // size,),
            in_specs=[pl.BlockSpec((tokens, size), lambda i, *_: (0, i)), once((tokens, d), lambda i, *_: (0, 0))],
            out_specs=[out, out],
        ),
        out_shape=[shape((dp // 2, g, rows, width), BF)] * 2,
        compiler_params=params(),
        cost_estimate=cost(2 * tokens * d * ff, 2 * (tokens * (d + ff) + d * ff)),
        name="down_grad",
    )(core, act, og)


def weight_grad_body(form, core_ref, x_ref, dy_ref, keep_ref, send_ref):
    dy = dy_ref[...]
    y = dot(x_ref[...], dy.reshape(dy.shape[-2:]), form)
    chips, _, rows, width = keep_ref.shape
    split_cores(core_ref, y.reshape(chips, 2, rows, width), keep_ref.at[:, 0], send_ref.at[:, 0])


def weight_grad(core, x, dy, dp, g, form, name):
    count, tokens, columns = dy.shape
    d = x.shape[0] if form == NN else x.shape[1]
    share = columns // g
    size = min(512, share)
    per = share // size
    rows = d // dp
    out = pl.BlockSpec((dp // 2, 1, rows, size), lambda m, i, *_: (0, i // per, m, i % per))
    return pl.pallas_call(
        functools.partial(weight_grad_body, form),
        grid_spec=pltpu.PrefetchScalarGridSpec(
            num_scalar_prefetch=1,
            grid=(count, columns // size),
            in_specs=[
                once(x.shape, lambda m, i, *_: (0, 0)),
                pl.BlockSpec((1, tokens, size), lambda m, i, *_: (m, 0, i)),
            ],
            out_specs=[out, out],
        ),
        out_shape=[shape((dp // 2, g, count * rows, share), BF)] * 2,
        compiler_params=params(),
        cost_estimate=cost(2 * count * tokens * d * columns, 2 * (tokens * d + count * columns * (tokens + d))),
        name=name,
    )(core, x, dy)


def input_body(x_ref, mg_ref, dq_ref, dkv_ref, vec_ref, w_ref, out_ref, sums_ref):
    groups, per, width = w_ref.shape[1], w_ref.shape[2] // 3, w_ref.shape[3]
    e = None
    grads = (dq_ref[...], dkv_ref[0], dkv_ref[1])
    for m in range(3):
        for j in range(groups):
            at = slice(j * width, (j + 1) * width)
            part = dot(grads[m][:, at], weight_columns(w_ref, j, slice(m * per, (m + 1) * per)), NT)
            e = part if e is None else e + part
    hat, inverse = norm_parts(x_ref[...].astype(F32))
    out_ref[...] = (mg_ref[...] + norm_back(e, hat, inverse, row(vec_ref, GAIN_ONE))).astype(BF)
    accumulate(sums_ref.at[0], fold(e * hat))
    accumulate(sums_ref.at[1], fold(e))
    accumulate(sums_ref.at[2], fold(grads[0].astype(F32)))
    accumulate(sums_ref.at[3], fold(grads[2].astype(F32)))


def input_back(x, mg, dq, dkv, vec, first, tile):
    tokens, d = x.shape
    dp, g, rows, width = first.shape
    per = d // dp
    tok = pl.BlockSpec((tile, d), lambda i: (i, 0))
    return pl.pallas_call(
        input_body,
        grid=(tokens // tile,),
        in_specs=[
            tok, tok, tok,
            pl.BlockSpec((2, tile, d), lambda i: (0, i, 0)),
            once((8, d), lambda i: (0, 0)),
            once((dp, g, 3 * per, width), lambda i: (0, 0, 0, 0)),
        ],
        out_specs=[tok, pl.BlockSpec((4, 8, d), lambda i: (0, 0, 0))],
        out_shape=[shape((tokens, d), BF), shape((4, 8, d), F32)],
        compiler_params=params(),
        cost_estimate=cost(6 * tokens * d * d, 16 * tokens * d + 6 * d * d),
        name="input_back",
    )(x, mg, dq, dkv, vec, first)


def swap_cores(values):
    return lax.ppermute(values, "core", [(0, 1), (1, 0)])


def add_cores(keep, send):
    return (keep.astype(F32) + swap_cores(send).astype(F32)).astype(BF)


def add_chips(mine):
    chips, g = mine.shape[:2]
    flat = mine.reshape((chips * g,) + mine.shape[2:])
    return lax.psum_scatter(flat, ("z", "x", "seq"), scatter_dimension=0, tiled=True)[0].astype(F32)


NEAR = ("z", [(0, 1), (1, 0), (2, 3), (3, 2)])
FAR = ("z", [(0, 2), (2, 0), (1, 3), (3, 1)])
ACROSS = ("x", [(0, 1), (1, 0)])
ALONG = ("seq", [(0, 1), (1, 0)])


def halve(values, dim, own, route):
    keep = lax.dynamic_index_in_dim(values, own, dim, keepdims=False)
    send = lax.dynamic_index_in_dim(values, 1 - own, dim, keepdims=False)
    return (keep.astype(F32) + lax.ppermute(send, *route).astype(F32)).astype(BF)


def add_chips_stepwise(mine, across_first):
    z, x, y = (lax.axis_index(name) for name in ("z", "x", "seq"))
    values = mine.reshape((2, 2, 2) + mine.shape[1:])
    if across_first:
        values = halve(values, 2, x, ACROSS)
    values = halve(values, 1, z % 2, NEAR)
    values = halve(values, 0, z // 2, FAR)
    if not across_first:
        values = halve(values, 0, x, ACROSS)
    return halve(values, 0, y, ALONG).astype(F32)


def body(
    tokens, first_gain, first_shift, query_weight, query_bias, key_weight, value_weight, value_bias,
    output_weight, output_bias, second_gain, second_shift, up_weight, up_bias, down_weight, down_bias,
    piece_starts, out_grad,
):
    chips, g = lax.axis_size("z") * lax.axis_size("x"), lax.axis_size("seq")
    dp = 2 * chips
    everyone = ("z", "x", "core", "seq")
    count, local, d = tokens.shape
    width = query_weight.shape[1]
    per = query_weight.shape[0]
    small = first_gain.shape[0]
    wide = up_bias.shape[0]
    ff = wide * dp * g
    length = local * g
    place = lax.axis_index("seq")
    core = lax.axis_index("core").astype(jnp.int32).reshape(1)
    paired = g == 2 and count % 2 == 0

    vectors = jnp.concatenate(
        [first_gain, first_shift, query_bias, value_bias, output_bias, second_gain, second_shift, down_bias, up_bias]
    )
    extra = -(-vectors.shape[0] // (16 * width)) * 16
    vectors = jnp.pad(vectors, (0, extra * width - vectors.shape[0])).reshape(extra, width)
    packed = jnp.concatenate([query_weight, key_weight, value_weight, output_weight, vectors], axis=0)
    first = lax.all_gather(packed, everyone, axis=0).reshape(dp, g, 4 * per + extra, width)
    up = lax.all_gather(up_weight, everyone, axis=0).reshape((dp, g) + up_weight.shape)
    down = lax.all_gather(down_weight, everyone, axis=0).reshape((dp, g) + down_weight.shape)

    flat = first[:, :, 4 * per :, :].reshape(dp * g, extra * width)[:, : 8 * small + wide].astype(F32)
    vec = flat[:, : 8 * small].reshape(dp * g, 8, small).transpose(1, 0, 2).reshape(8, d)
    upb = flat[:, 8 * small :].reshape(1, ff)

    if paired:
        half = count // 2

        def gather_rows(values):
            kept = lax.dynamic_slice_in_dim(values, place * half, half, 0)
            sent = lax.dynamic_slice_in_dim(values, (1 - place) * half, half, 0)
            came = lax.ppermute(sent, "seq", [(0, 1), (1, 0)])
            low = jnp.where(place == 0, kept, came)
            high = jnp.where(place == 0, came, kept)
            return jnp.concatenate([low, high], axis=1).reshape(half * length, d)

        def return_rows(values):
            values = values.reshape(half, 2, local, d)
            kept = lax.dynamic_index_in_dim(values, place, 1, keepdims=False)
            sent = lax.dynamic_index_in_dim(values, 1 - place, 1, keepdims=False)
            came = lax.ppermute(sent, "seq", [(0, 1), (1, 0)])
            low = jnp.where(place == 0, kept, came)
            high = jnp.where(place == 0, came, kept)
            return jnp.concatenate([low, high], axis=0)

        starts = lax.dynamic_slice_in_dim(piece_starts, place * half, half, 0)
        offset = jnp.zeros((1,), jnp.int32)
        sequences, queries = half, length
    else:
        gather_rows = lambda values: values.reshape(count * local, d)
        return_rows = lambda values: values.reshape(count, local, d)
        starts = piece_starts
        offset = (place * local).astype(jnp.int32).reshape(1)
        sequences, queries = count, local

    rows = sequences * queries
    tile = min(256, rows)
    x = gather_rows(tokens)
    og = gather_rows(after(out_grad, first))
    x1, q, k, v = project(x, vec, first, tile)
    q, k, v = (t.reshape(sequences, queries, d) for t in (q, k, v))
    if not paired:
        k, v = (lax.all_gather(t, "seq", axis=1, tiled=True) for t in (k, v))
    att, lse = attend(starts, offset, q, k, v, paired)
    middle, x2, act, slope = rise(x, att, vec, upb, first, up, tile)
    down_mine = add_cores(*down_grad(core, act, og, dp, g))
    down_sum = add_chips(down_mine)
    act = after(act, down_mine)
    out, bg, mg, branch, dat, upb_sums, sums_two = fall(middle, act, slope, og, vec, first, up, down, tile)
    output = return_rows(out)
    up_parts = weight_grad(core, x2, bg[None], dp, g, TN, "up_grad")
    out_parts = weight_grad(core, att, branch[None], dp, g, NN, "out_grad")
    up_mine = jnp.concatenate([add_cores(*up_parts), add_cores(*out_parts)], axis=-1)
    up_sum = add_chips(up_mine)
    dat = after(dat, up_mine, down_sum)
    dq, dkv = attend_back(starts, offset, q, k, v, dat.reshape(sequences, queries, d), lse, paired)
    dq = after(dq.reshape(rows, d), output)
    if not paired:
        dkv = lax.psum_scatter(dkv, "seq", scatter_dimension=2, tiled=True)
    dkv = dkv.reshape(2, rows, d)
    query_parts = weight_grad(core, x1, dq[None], dp, g, TN, "query_grad")
    kv_parts = weight_grad(core, x1, dkv, dp, g, TN, "key_value_grad")
    matrix_mine = jnp.concatenate([add_cores(*query_parts), add_cores(*kv_parts)], axis=2)
    in_grad, sums_one = input_back(x, mg, dq, after(dkv, matrix_mine, up_sum), vec, first, tile)
    input_grad = return_rows(in_grad)

    one, two = jnp.sum(sums_one, axis=1), jnp.sum(sums_two, axis=1)
    eight = jnp.stack([one[0], one[1], one[2], one[3], two[2], two[0], two[1], two[3]])
    eight = eight.reshape(8, chips, 2, g, small).transpose(2, 1, 3, 0, 4).reshape(2, chips, g, 8 * small)
    upb_grad = jnp.sum(upb_sums, axis=0).reshape(chips, 2, g, wide).transpose(1, 0, 2, 3)
    lines = jnp.concatenate([eight, upb_grad], axis=-1)
    lines = jnp.pad(lines, ((0, 0), (0, 0), (0, 0), (0, extra * width - lines.shape[-1])))
    lines = lines.reshape(2, chips, g, extra, width).astype(BF)
    own = lax.axis_index("core")
    line_mine = add_cores(
        lax.dynamic_index_in_dim(lines, own, 0, keepdims=False),
        lax.dynamic_index_in_dim(lines, 1 - own, 0, keepdims=False),
    )
    if (lax.axis_size("z"), lax.axis_size("x"), g) == (4, 2, 2):
        tail = jnp.concatenate([matrix_mine[:, :, 2 * per :], line_mine], axis=2)
        last = [add_chips_stepwise(matrix_mine[:, :, : 2 * per], True), add_chips_stepwise(tail, False)]
        last = jnp.concatenate(last, axis=0)
    else:
        last = add_chips(jnp.concatenate([matrix_mine, line_mine], axis=2))
    dw = [last[m * per : (m + 1) * per] for m in range(3)] + [up_sum[:, -width:]]
    up_sum = up_sum[:, :-width]
    line = last[3 * per :].reshape(extra * width)
    grads = [line[m * small : (m + 1) * small] for m in range(8)]
    gain_one, shift_one, query_add, value_add, output_add, gain_two, shift_two, down_add = grads
    up_add = line[8 * small : 8 * small + wide]
    return (
        output, input_grad, gain_one, shift_one, dw[0], query_add, dw[1], dw[2], value_add, dw[3], output_add,
        gain_two, shift_two, up_sum, up_add, down_sum, down_add,
    )


def solution(mesh):
    dp, g = mesh.shape["dp"], mesh.shape["seq"]
    fine = Mesh(mesh.devices.reshape(4, dp // 8, 2, g), ("z", "x", "core", "seq"))
    both = ("z", "x", "core")
    rows, vector, matrix = P(both, "seq", None), P(both + ("seq",)), P(both, "seq")
    in_specs = (
        rows, vector, vector, matrix, vector, matrix, matrix, vector, matrix, vector, vector, vector, matrix,
        vector, matrix, vector, P(both, None), rows,
    )
    out_specs = (
        rows, rows, vector, vector, matrix, vector, matrix, matrix, vector, matrix, vector, vector, vector,
        matrix, vector, matrix, vector,
    )
    return jax.shard_map(body, mesh=fine, in_specs=in_specs, out_specs=out_specs, check_vma=False)
```

time: 1650 us -> 768 us (0.47)
  matrix products: 627 us -> 0 us
  Pallas kernels: 0 us -> 433 us
  waiting for transfers between devices: 525 us -> 213 us
  blocking collectives: 193 us -> 0 us
  other arithmetic: 194 us -> 43.9 us
  local copies, waits for them, and re-layouts: 75.9 us -> 34.9 us
  starting transfers between devices: 1.24 us -> 21.5 us
    dot_general x24 -> x0, matrix products: 627 us -> none  [the longest x1 102 us: body(): jnp.einsum('sqhd,skhd->shqk', split_heads(attended_grad), split_heads(bac...]
    pallas_call x0 -> x11, Pallas kernels: none -> 433 us  [the longest x1 111 us: attend_back(): pl.pallas_call(functools.partial(attend_back_body, fixed_offset), grid_sp...]
    reduce_scatter x14 -> x2, waiting for transfers between devices: 388 us -> 0.01 us  [add_chips(): lax.psum_scatter(flat, ('z', 'x', 'seq'), scatter_dimension=0, tiled=True)]
    unnamed x4 -> x0, blocking collectives: 130 us -> none
    ppermute x0 -> x18, waiting for transfers between devices: none -> 130 us  [the longest x8 57.3 us: halve(): lax.ppermute(send, *route).astype(F32)]
    convert_element_type x26 -> x17, other arithmetic: 131 us -> 24 us  [the longest x6 17.1 us: add_cores(): return (keep.astype(F32) + swap_cores(send).astype(F32)).astype(BF)]
    all_gather x8 -> x0, blocking collectives: 62.9 us -> none  [the longest x1 17.1 us: fetch_weights(): lax.all_gather(within[12], 'dp', axis=0, tiled=True)]
    reduce_sum x6 -> x3, other arithmetic: 60 us -> 1.04 us  [the longest x2 0.99 us: body(): one, two = (jnp.sum(sums_one, axis=1), jnp.sum(sums_two, axis=1))]
  transfers between devices with their start and end apart: 22 -> 23, of which waited for: 12 -> 11; matrix products, arithmetic and copies ran while one was open for 49% -> 8% of each run, Pallas kernels for 0% -> 57%
where the time goes in v1:
time: 768 us; the launch traced here: 761 us
  Pallas kernels  433 us (56%)
  waiting for transfers between devices  213 us (28%)
  other arithmetic  43.9 us (6%)
  local copies, waits for them, and re-layouts  34.9 us (5%)
  starting transfers between devices  21.5 us (3%)
  between operations  14.8 us (2%)
    pallas_call x1, Pallas kernels, attend_back(): pl.pallas_call(functools.partial(attend_back_body, fixed_offset), grid_sp...  111 us
    pallas_call x1, Pallas kernels, fall(): pl.pallas_call(fall_body, grid=(tokens // tile,), in_specs=[tok, wide, wi...  84.9 us
    all_gather x1, waiting for transfers between devices, body(): lax.all_gather(packed, everyone, axis=0)  81.4 us
    pallas_call x1, Pallas kernels, attend(): pl.pallas_call(functools.partial(attend_body, fixed_offset), grid_spec=pl...  64.9 us
    ppermute x8, waiting for transfers between devices, halve(): lax.ppermute(send, *route).astype(F32)  57.3 us
    pallas_call x4, Pallas kernels, weight_grad(): pl.pallas_call(functools.partial(weight_grad_body, form), grid_spec=pltpu...  54.1 us
    pallas_call x1, Pallas kernels, rise(): pl.pallas_call(rise_body, grid=(tokens // tile,), in_specs=[tok, pl.Block...  50.9 us
    ppermute x2, waiting for transfers between devices, gather_rows(): came = lax.ppermute(sent, 'seq', [(0, 1), (1, 0)])  50.3 us
  transfers between devices with their start and end apart: 23, of which 11 were waited for; matrix products, arithmetic and copies ran while one was open for 8% of the time, Pallas kernels for 57%

profile of v1, /device:TPU:0, one launch (start us, length us, event | category | flops | bytes accessed | tf_op | source)
XLA Modules:
  0.0 761.0 jit_solution(1908146479415892565)
XLA Ops:
  7.3 0.8 constant_dynamic-update-slice_fusion.4
  8.1 6.1 concatenate.32
  14.2 0.8 constant_dynamic-update-slice_fusion.3
  15.1 0.8 constant_dynamic-update-slice_fusion.2
  15.9 0.8 constant_dynamic-update-slice_fusion.1
  19.0 3.1 constant_dynamic-slice_fusion.6
  22.1 3.0 collective-permute-start
  25.1 81.4 %all-gather.7.cloned.1.call-done = bf16[8704,512]{1,0:T(8,128)(2,1)} async-done(((bf16[272,512]{1,0:T(8,128)(2,1)}), bf16[8704,512]{1,0:T(8,128)(2,1)}) %all-gather.7.cloned.1.call-update) | async-done | bytes 8912912 | tf_op jit(solution)/shard_map/all_gather | solution.py:593
  106.5 3.1 constant_dynamic-slice_fusion.4
  109.5 1.5 collective-permute-start.1
  111.8 1.1 slice.106
  113.9 0.7 reshape.147.vec_ref
  114.7 50.3 %collective-permute-done.1 = bf16[2,512,1024]{2,1,0:T(8,128)(2,1)} collective-permute-done((bf16[2,512,1024]{2,1,0:T(8,128)(2,1)}, bf16[2,512,1024]{2,1,0:T(8,128)(2,1)}, u32[]{:S(2)}, u32[]{:S(2)}) %collective-permute-start.1) | collective-permute-done | bytes 2097184 | tf_op jit(solution)/shard_map/ppermute | solution.py:607
  164.9 3.3 broadcast_select_fusion.1
  168.2 2.5 pad_maximum_fusion.1
  170.7 2.4 pad_maximum_fusion.2
  173.1 20.6 %project.1 = (bf16[2048,1024]{1,0:T(8,128)(2,1)}, bf16[2048,1024]{1,0:T(8,128)(2,1)}, bf16[2048,1024]{1,0:T(8,128)(2,1)}, bf16[2048,1024]{1,0:T(8,128)(2,1)}) custom-call(bf16[2048,1024]{1,0:T(8,128)(2,1)} %bitcast.125, f32[8,1024]{1,0:T(8,128)} %reshape.147.vec_ref, bf16[16,2,272,512]{3,2,1,0:T(8,128)(2,1)} %bitcast.142), custom_call_target="tpu_custom_call" | custom-call | flops 12884901888 | bytes 27262976 | tf_op jit(solution)/shard_map/project/pallas_call | solution.py:114
  193.7 64.9 %attend.1 = (bf16[1024,2048]{1,0:T(8,128)(2,1)}, f32[2,8,2,1024]{3,2,1,0:T(2,128)}) custom-call(s32[2,2]{1,0:T(2,128)} %copy.55.starts_ref, s32[1]{0:T(128)} %constant.117.clone.1.offset_ref, bf16[2,1024,1024]{2,1,0:T(8,128)(2,1)} %bitcast.155, bf16[2,1024,1024]{2,1,0:T(8,128)(2,1)} %bitcast.157, bf16[2,1024,1024]{2,1,0:T(8,128)(2,1)} %bitcast.159), custom_call_target="tpu_custom_call" | custom-call | flops 25769803776 | bytes 16777216 | tf_op jit(solution)/shard_map/attend/pallas_call | solution.py:201
  258.6 50.9 %rise.1 = (f32[2048,1024]{1,0:T(8,128)}, bf16[2048,1024]{1,0:T(8,128)(2,1)}, bf16[2048,4096]{1,0:T(8,128)(2,1)}, bf16[2048,4096]{1,0:T(8,128)(2,1)}) custom-call(bf16[2048,1024]{1,0:T(8,128)(2,1)} %bitcast.126, bf16[1024,2048]{1,0:T(8,128)(2,1)} %get-tuple-element.56.att_ref.x_ref, f32[8,1024]{1,0:T(8,128)} %reshape.147.vec_ref, f32[1,4096]{1,0:T(1,128)} %bitcast.146, ...), custom_call_target="tpu_custom_call" | custom-call | flops 21474836480 | bytes 65011712 | tf_op jit(solution)/shard_map/rise/pallas_call | solution.py:325
  309.6 22.8 %down_grad.1 = (bf16[8,2,256,512]{3,2,1,0:T(8,128)(2,1)}, bf16[8,2,256,512]{3,2,1,0:T(8,128)(2,1)}) custom-call(s32[1]{0:T(128)} %bitcast.8.core_ref, bf16[2048,4096]{1,0:T(8,128)(2,1)} %get-tuple-element.62.act_ref, bf16[2048,1024]{1,0:T(8,128)(2,1)} %bitcast.128), custom_call_target="tpu_custom_call" | custom-call | flops 17179869184 | bytes 29360128 | tf_op jit(solution)/shard_map/down_grad/pallas_call | solution.py:443
  332.4 7.4 collective-permute-done.2
  339.8 5.5 add_convert_fusion.1
  345.4 84.9 %fall.1 = (bf16[2048,1024]{1,0:T(8,128)(2,1)}, bf16[2048,4096]{1,0:T(8,128)(2,1)}, f32[2048,1024]{1,0:T(8,128)}, bf16[2048,1024]{1,0:T(8,128)(2,1)}, bf16[2048,1...) custom-call(f32[2048,1024]{1,0:T(8,128)} %get-tuple-element.57.mid_ref, ...), custom_call_target="tpu_custom_call" | custom-call | flops 55834574848 | bytes 102760448 | tf_op jit(solution)/shard_map/fall/pallas_call | solution.py:396
  430.2 23.3 %up_grad.1 = (bf16[8,2,64,2048]{3,2,1,0:T(8,128)(2,1)}, bf16[8,2,64,2048]{3,2,1,0:T(8,128)(2,1)}) custom-call(s32[1]{0:T(128)} %bitcast.8.core_ref, bf16[2048,1024]{1,0:T(8,128)(2,1)} %get-tuple-element.67.x_ref, bf16[1,2048,4096]{2,1,0:T(8,128)(2,1)} %bitcast.150), custom_call_target="tpu_custom_call" | custom-call | flops 17179869184 | bytes 29360128 | tf_op jit(solution)/shard_map/up_grad/pallas_call | solution.py:473
  453.7 8.5 %out_grad.1 = (bf16[8,2,64,512]{3,2,1,0:T(8,128)(2,1)}, bf16[8,2,64,512]{3,2,1,0:T(8,128)(2,1)}) custom-call(s32[1]{0:T(128)} %bitcast.8.core_ref, bf16[1024,2048]{1,0:T(8,128)(2,1)} %get-tuple-element.56.att_ref.x_ref, bf16[1,2048,1024]{2,1,0:T(8,128)(2,1)} %bitcast.162), custom_call_target="tpu_custom_call" | custom-call | flops 4294967296 | bytes 10485760 | tf_op jit(solution)/shard_map/out_grad/pallas_call | solution.py:473
  462.5 2.5 collective-permute-done.5
  465.0 1.5 add_convert_fusion.4
  466.6 5.5 add_convert_fusion
  472.1 2.9 pad_maximum_fusion
  475.0 3.2 dynamic-slice_bitcast_fusion.1
  478.2 2.7 collective-permute-start.3
  480.9 1.8 bitcast_convert_fusion.1
  482.7 110.6 %attend_back.1 = (bf16[2,1024,1024]{2,1,0:T(8,128)(2,1)}, bf16[2,2,1024,1024]{3,2,1,0:T(8,128)(2,1)}) custom-call(s32[2,2]{1,0:T(2,128)} %copy.55.starts_ref, s32[1]{0:T(128)} %constant.117.clone.1.offset_ref, bf16[2,1024,1024]{2,1,0:T(8,128)(2,1)} %bitcast.156, bf16[2,1024,1024]{2,1,0:T(8,128)(2,1)} %bitcast.158, bf16[2,1024,1024]{2,1,0:T(8,128)(2,1)} %bitcast.160, ...), custom_call_target="tpu_custom_call" | custom-call | flops 64424509440 | bytes 29360128 | tf_op jit(solution)/shard_map/attend_back/pallas_call | solution.py:261
  593.4 13.7 %key_value_grad.1 = (bf16[8,2,128,512]{3,2,1,0:T(8,128)(2,1)}, bf16[8,2,128,512]{3,2,1,0:T(8,128)(2,1)}) custom-call(s32[1]{0:T(128)} %bitcast.8.core_ref, bf16[2048,1024]{1,0:T(8,128)(2,1)} %get-tuple-element.79.x_ref, bf16[2,2048,1024]{2,1,0:T(8,128)(2,1)} %bitcast.151), custom_call_target="tpu_custom_call" | custom-call | flops 8589934592 | bytes 16777216 | tf_op jit(solution)/shard_map/key_value_grad/pallas_call | solution.py:473
  607.1 9.8 %collective-permute-done.3 = bf16[2,512,1024]{2,1,0:T(8,128)(2,1)} collective-permute-done((bf16[2,512,1024]{2,1,0:T(8,128)(2,1)}, bf16[2,512,1024]{2,1,0:T(8,128)(2,1)}, u32[]{:S(2)}, u32[]{:S(2)}) %collective-permute-start.3) | collective-permute-done | bytes 2097184 | tf_op jit(solution)/shard_map/ppermute | solution.py:616
  617.0 2.5 bitcast_select_fusion.3
  619.5 2.4 pad_maximum_fusion.3
  621.9 8.6 %query_grad.1 = (bf16[8,2,64,512]{3,2,1,0:T(8,128)(2,1)}, bf16[8,2,64,512]{3,2,1,0:T(8,128)(2,1)}) custom-call(s32[1]{0:T(128)} %bitcast.8.core_ref, bf16[2048,1024]{1,0:T(8,128)(2,1)} %get-tuple-element.79.x_ref, bf16[1,2048,1024]{2,1,0:T(8,128)(2,1)} %bitcast.153), custom_call_target="tpu_custom_call" | custom-call | flops 4294967296 | bytes 10485760 | tf_op jit(solution)/shard_map/query_grad/pallas_call | solution.py:473
  630.6 2.7 collective-permute-done.6
  633.4 1.5 add_convert_fusion.3
  634.9 1.3 copy-done.7
  636.2 2.9 add_convert_fusion.2
  639.5 1.0 copy-done.2
  640.5 1.1 copy.73
  641.6 1.7 collective-permute-start.14
  643.2 1.9 bitcast_convert_fusion
  645.1 24.2 %input_back.1 = (bf16[2048,1024]{1,0:T(8,128)(2,1)}, f32[4,8,1024]{2,1,0:T(8,128)}) custom-call(bf16[2048,1024]{1,0:T(8,128)(2,1)} %bitcast.127, f32[2048,1024]{1,0:T(8,128)} %get-tuple-element.65.mg_ref, bf16[2048,1024]{1,0:T(8,128)(2,1)} %bitcast.154, bf16[2,2048,1024]{2,1,0:T(8,128)(2,1)} %bitcast.152, f32[8,1024]{1,0:T(8,128)} %reshape.147.vec_ref, ...), custom_call_target="tpu_custom_call" | custom-call | flops 12884901888 | bytes 39845888 | tf_op jit(solution)/shard_map/input_back/pallas_call | solution.py:513
  669.3 0.9 reduce_sum.27
  670.9 1.5 fusion.1
  672.5 0.9 dynamic-slice_bitcast_fusion.3
  673.4 4.9 collective-permute-start.15
  678.5 0.9 dynamic-slice_bitcast_fusion.2
  679.7 11.7 %collective-permute-done.15 = bf16[2,2,128,512]{3,2,1,0:T(8,128)(2,1)} collective-permute-done((bf16[2,2,128,512]{3,2,1,0:T(8,128)(2,1)}, bf16[2,2,128,512]{3,2,1,0:T(8,128)(2,1)}, u32[]{:S(2)}, u32[]{:S(2)}) %collective-permute-start.15) | collective-permute-done | bytes 524320 | tf_op jit(solution)/shard_map/ppermute | solution.py:553
  691.4 1.2 fusion.5
  692.7 1.8 dynamic-slice_bitcast_fusion
  694.4 2.8 collective-permute-start.8
  697.2 13.5 %collective-permute-done.10 = bf16[2,2,2,80,512]{4,3,2,1,0:T(8,128)(2,1)S(1)} collective-permute-done((bf16[2,2,2,80,512]{4,3,2,1,0:T(8,128)(2,1)}, bf16[2,2,2,80,512]{4,3,2,1,0:T(8,128)(2,1)S(1)}, u32[]{:S(2)}, u32[]{:S(2)}) %collective-permute-start.10) | collective-permute-done | bytes 655392 | tf_op jit(solution)/shard_map/ppermute | solution.py:553
  711.1 1.9 collective-permute-start.17
  713.0 14.5 %collective-permute-done.11 = bf16[2,2,80,512]{3,2,1,0:T(8,128)(2,1)S(1)} collective-permute-done((bf16[2,2,80,512]{3,2,1,0:T(8,128)(2,1)S(1)}, bf16[2,2,80,512]{3,2,1,0:T(8,128)(2,1)S(1)}, u32[]{:S(2)}, u32[]{:S(2)}) %collective-permute-start.11) | collective-permute-done | bytes 327712 | tf_op jit(solution)/shard_map/ppermute | solution.py:553
  727.8 17.1 %collective-permute-done.17 = bf16[128,512]{1,0:T(8,128)(2,1)S(1)} collective-permute-done((bf16[128,512]{1,0:T(8,128)(2,1)S(1)}, bf16[128,512]{1,0:T(8,128)(2,1)S(1)}, u32[]{:S(2)}, u32[]{:S(2)}) %collective-permute-start.17) | collective-permute-done | bytes 131104 | tf_op jit(solution)/shard_map/ppermute | solution.py:553
  745.0 1.8 collective-permute-start.13
  746.8 0.7 fusion.15
  747.5 0.8 slice.128
  751.6 2.4 pad_maximum_fusion.4
  (104 shorter events, 10.3 us)
Async XLA Ops:
  7.2 103.9 %copy-start = (s32[4,2]{0,1:T(2,128)S(1)}, s32[4,2]{0,1:T(2,128)}, u32[]{:S(2)}) copy-start(s32[4,2]{0,1:T(2,128)} %param.34) | copy-start | bytes 100
  7.2 99.3 %all-gather.7.cloned.1.call-start = ((), (), s32[]{:S(2)}) async-start(), calls=%async_computation.4 | async-start | bytes 9191424 | tf_op jit(solution)/shard_map/all_gather | solution.py:593
  16.8 0.7 copy-start.8
  17.5 241.1 %all-gather.9.cloned.1.call-start = ((), (), s32[]{:S(2)}) async-start(), calls=%async_computation.5 | async-start | bytes 8650752 | tf_op jit(solution)/shard_map/all_gather | solution.py:594
  18.3 327.1 %all-gather.11.cloned.1.call-start = ((), (), s32[]{:S(2)}) async-start(), calls=%async_computation.6 | async-start | bytes 8650752 | tf_op jit(solution)/shard_map/all_gather | solution.py:595
  19.0 461.9 %reduce-scatter.3.cloned.1.call-start = ((), (), s32[]{:S(2)}) async-start(), calls=%async_computation.2 | async-start | bytes 4456448 | tf_op jit(solution)/shard_map/reduce_scatter | solution.py:541
  22.1 92.5 %collective-permute-start = (bf16[2,512,1024]{2,1,0:T(8,128)(2,1)}, bf16[2,512,1024]{2,1,0:T(8,128)(2,1)S(1)}, u32[]{:S(2)}, u32[]{:S(2)}) collective-permute-start(bf16[2,512,1024]{2,1,0:T(8,128)(2,1)} %constant_dynamic-slice_fusion.6), channel_id=1, source_target_pairs={{0,1},{1,0},{2,3},{3,2},{4,5},{5,4},{6,7},{7,6},{8,9},{9,8},{10,11... | collective-permute-start | bytes 6291464 | tf_op jit(solution)/shard_map/ppermute | solution.py:607
  109.5 55.4 %collective-permute-start.1 = (bf16[2,512,1024]{2,1,0:T(8,128)(2,1)}, bf16[2,512,1024]{2,1,0:T(8,128)(2,1)}, u32[]{:S(2)}, u32[]{:S(2)}) collective-permute-start(bf16[2,512,1024]{2,1,0:T(8,128)(2,1)} %constant_dynamic-slice_fusion.4), channel_id=1, source_target_pairs={{0,1},{1,0},{2,3},{3,2},{4,5},{5,4},{6,7},{7,6},{8,9},{9,8},{10,11... | collective-permute-start | bytes 6291464 | tf_op jit(solution)/shard_map/ppermute | solution.py:607
  332.4 7.4 collective-permute-start.2
  345.3 297.9 %reduce-scatter.5.cloned.1.call-start = ((), (), s32[]{:S(2)}) async-start(), calls=%async_computation.3 | async-start | bytes 5570560 | tf_op jit(solution)/shard_map/reduce_scatter | solution.py:541
  453.6 13.0 %collective-permute-start.4 = (bf16[8,2,64,2048]{3,2,1,0:T(8,128)(2,1)}, bf16[8,2,64,2048]{3,2,1,0:T(8,128)(2,1)}, u32[]{:S(2)}, u32[]{:S(2)}) collective-permute-start(bf16[8,2,64,2048]{3,2,1,0:T(8,128)(2,1)} %get-tuple-element.70), channel_id=1, source_target_pairs={{0,2},{2,0},{1,3},{3,1},{4,6},{6,4},{5,7},{7,5},{8,10},{10,8},{9,1... | collective-permute-start | bytes 12582920 | tf_op jit(solution)/shard_map/ppermute | solution.py:531
  462.2 2.9 collective-permute-start.5
  478.2 138.8 %collective-permute-start.3 = (bf16[2,512,1024]{2,1,0:T(8,128)(2,1)}, bf16[2,512,1024]{2,1,0:T(8,128)(2,1)}, u32[]{:S(2)}, u32[]{:S(2)}) collective-permute-start(bf16[2,512,1024]{2,1,0:T(8,128)(2,1)} %dynamic-slice_bitcast_fusion.1), channel_id=1, source_target_pairs={{0,1},{1,0},{2,3},{3,2},{4,5},{5,4},{6,7},{7,6},{8,9},{9,8},{10,11... | collective-permute-start | bytes 6291464 | tf_op jit(solution)/shard_map/ppermute | solution.py:616
  607.0 27.9 %collective-permute-start.7 = (bf16[8,2,128,512]{3,2,1,0:T(8,128)(2,1)}, bf16[8,2,128,512]{3,2,1,0:T(8,128)(2,1)S(1)}, u32[]{:S(2)}, u32[]{:S(2)}) collective-permute-start(bf16[8,2,128,512]{3,2,1,0:T(8,128)(2,1)} %get-tuple-element.83), channel_id=1, source_target_pairs={{0,2},{2,0},{1,3},{3,1},{4,6},{6,4},{5,7},{7,5},{8,10},{10,8},{9,1... | collective-permute-start | bytes 6291464 | tf_op jit(solution)/shard_map/ppermute | solution.py:531
  621.9 8.6 %copy-start.10 = (f32[4,8,1024]{2,1,0:T(8,128)S(1)}, f32[4,8,1024]{2,1,0:T(8,128)}, u32[]{:S(2)}) copy-start(f32[4,8,1024]{2,1,0:T(8,128)} %get-tuple-element.87) | copy-start | bytes 393220
  621.9 8.7 %copy-start.9 = (f32[8,4096]{1,0:T(8,128)S(1)}, f32[8,4096]{1,0:T(8,128)}, u32[]{:S(2)}) copy-start(f32[8,4096]{1,0:T(8,128)} %get-tuple-element.88) | copy-start | bytes 393220
  630.5 2.9 collective-permute-start.6
  630.6 8.6 %copy-start.11 = (bf16[4,1024]{1,0:T(4,128)(2,1)}, bf16[4,1024]{1,0:T(4,128)(2,1)S(1)}, u32[]{:S(2)}) copy-start(bf16[4,1024]{1,0:T(4,128)(2,1)S(1)} %reduce_sum.28) | copy-start | bytes 24580
  634.9 1.3 copy-start.7
  639.2 1.3 copy-start.2
  641.6 29.4 %collective-permute-start.14 = (bf16[2,2,2,128,512]{4,3,2,0,1:T(8,128)(2,1)}, bf16[2,2,2,128,512]{4,3,2,0,1:T(8,128)(2,1)}, u32[]{:S(2)}, u32[]{:S(2)}) collective-permute-start(bf16[2,2,2,128,512]{4,3,2,0,1:T(8,128)(2,1)} %bitcast.112), channel_id=1, source_target_pairs={{0,4},{4,0},{1,5},{5,1},{2,6},{6,2},{3,7},{7,3},{8,12},{12,8},{9,1... | collective-permute-start | bytes 3145736 | tf_op jit(solution)/shard_map/ppermute | solution.py:553
  645.1 25.2 %slice-start.1 = ((bf16[4,1024]{1,0:T(4,128)(2,1)}), bf16[2,1024]{1,0:T(2,128)(2,1)S(1)}, s32[]{:S(2)}) async-start(bf16[4,1024]{1,0:T(4,128)(2,1)} %copy-done.11), calls=%async_computation.8 | async-start | bytes 8192 | tf_op jit(solution)/shard_map/slice | solution.py:663
  670.4 8.0 %slice-start = ((bf16[8,2,128,512]{3,2,1,0:T(8,128)(2,1)}), bf16[8,2,64,512]{3,2,1,0:T(8,128)(2,1)S(1)}, s32[]{:S(2)}) async-start(bf16[8,2,128,512]{3,2,1,0:T(8,128)(2,1)} %copy-done.2), calls=%async_computation.7 | async-start | bytes 2097152 | tf_op jit(solution)/shard_map/slice | solution.py:675
  670.9 7.4 collective-permute-start.9
  672.5 5.8 copy-start.4
  673.4 18.0 %collective-permute-start.15 = (bf16[2,2,128,512]{3,2,1,0:T(8,128)(2,1)}, bf16[2,2,128,512]{3,2,1,0:T(8,128)(2,1)}, u32[]{:S(2)}, u32[]{:S(2)}) collective-permute-start(bf16[2,2,128,512]{3,2,1,0:T(8,128)(2,1)} %dynamic-slice_bitcast_fusion.3), channel_id=1, source_target_pairs={{0,8},{8,0},{16,24},{24,16},{1,9},{9,1},{17,25},{25,17},{2,10},{10... | collective-permute-start | bytes 1572872 | tf_op jit(solution)/shard_map/ppermute | solution.py:553
  678.4 13.0 %copy-start.5 = (bf16[2,2,2,128,512]{4,3,2,0,1:T(8,128)(2,1)S(1)}, bf16[2,2,2,128,512]{4,3,2,0,1:T(8,128)(2,1)}, u32[]{:S(2)}) copy-start(bf16[2,2,2,128,512]{4,3,2,0,1:T(8,128)(2,1)} %copy-done.4) | copy-start | bytes 3145732
  679.5 31.3 %collective-permute-start.10 = (bf16[2,2,2,80,512]{4,3,2,1,0:T(8,128)(2,1)}, bf16[2,2,2,80,512]{4,3,2,1,0:T(8,128)(2,1)S(1)}, u32[]{:S(2)}, u32[]{:S(2)}) collective-permute-start(bf16[2,2,2,80,512]{4,3,2,1,0:T(8,128)(2,1)} %dynamic-slice_bitcast_fusion.2), channel_id=1, source_target_pairs={{0,8},{8,0},{16,24},{24,16},{1,9},{9,1},{17,25},{25,17},{2,10},{10... | collective-permute-start | bytes 1966088 | tf_op jit(solution)/shard_map/ppermute | solution.py:553
  692.6 18.5 %collective-permute-start.16 = (bf16[2,128,512]{2,1,0:T(8,128)(2,1)S(1)}, bf16[2,128,512]{2,1,0:T(8,128)(2,1)S(1)}, u32[]{:S(2)}, u32[]{:S(2)}) collective-permute-start(bf16[2,128,512]{2,1,0:T(8,128)(2,1)S(1)} %dynamic-slice_bitcast_fusion.5), channel_id=1, source_target_pairs={{0,16},{16,0},{8,24},{24,8},{1,17},{17,1},{9,25},{25,9},{2,18},{18... | collective-permute-start | bytes 786440 | tf_op jit(solution)/shard_map/ppermute | solution.py:553
  694.4 53.1 %copy-start.6 = (f32[64,2560]{1,0:T(8,128)S(1)}, f32[64,2560]{1,0:T(8,128)}, u32[]{:S(2)}) copy-start(f32[64,2560]{1,0:T(8,128)} %bitcast_convert_fusion) | copy-start | bytes 1966084
  694.4 56.9 %copy-start.3 = (bf16[2048,1024]{1,0:T(8,128)(2,1)S(1)}, bf16[2048,1024]{1,0:T(8,128)(2,1)}, u32[]{:S(2)}) copy-start(bf16[2048,1024]{1,0:T(8,128)(2,1)} %get-tuple-element.85) | copy-start | bytes 12582916
  694.4 56.9 %collective-permute-start.8 = (bf16[2,512,1024]{2,1,0:T(8,128)(2,1)S(1)}, bf16[2,512,1024]{2,1,0:T(8,128)(2,1)S(1)}, u32[]{:S(2)}, u32[]{:S(2)}) collective-permute-start(bf16[2,512,1024]{2,1,0:T(8,128)(2,1)S(1)} %dynamic-slice_bitcast_fusion), channel_id=1, source_target_pairs={{0,1},{1,0},{2,3},{3,2},{4,5},{5,4},{6,7},{7,6},{8,9},{9,8},{10,11... | collective-permute-start | bytes 6291464 | tf_op jit(solution)/shard_map/ppermute | solution.py:616
  711.0 16.6 %collective-permute-start.11 = (bf16[2,2,80,512]{3,2,1,0:T(8,128)(2,1)S(1)}, bf16[2,2,80,512]{3,2,1,0:T(8,128)(2,1)S(1)}, u32[]{:S(2)}, u32[]{:S(2)}) collective-permute-start(bf16[2,2,80,512]{3,2,1,0:T(8,128)(2,1)S(1)} %dynamic-slice_bitcast_fusion.4), channel_id=1, source_target_pairs={{0,16},{16,0},{8,24},{24,8},{1,17},{17,1},{9,25},{25,9},{2,18},{18... | collective-permute-start | bytes 983048 | tf_op jit(solution)/shard_map/ppermute | solution.py:553
  711.1 33.7 %collective-permute-start.17 = (bf16[128,512]{1,0:T(8,128)(2,1)S(1)}, bf16[128,512]{1,0:T(8,128)(2,1)S(1)}, u32[]{:S(2)}, u32[]{:S(2)}) collective-permute-start(bf16[128,512]{1,0:T(8,128)(2,1)S(1)} %dynamic-slice_bitcast_fusion.7), channel_id=1, source_target_pairs={{0,1},{1,0},{2,3},{3,2},{4,5},{5,4},{6,7},{7,6},{8,9},{9,8},{10,11... | collective-permute-start | bytes 393224 | tf_op jit(solution)/shard_map/ppermute | solution.py:553
  727.7 17.2 %collective-permute-start.12 = (bf16[2,80,512]{2,1,0:T(8,128)(2,1)S(1)}, bf16[2,80,512]{2,1,0:T(8,128)(2,1)S(1)}, u32[]{:S(2)}, u32[]{:S(2)}) collective-permute-start(bf16[2,80,512]{2,1,0:T(8,128)(2,1)S(1)} %dynamic-slice_bitcast_fusion.6), channel_id=1, source_target_pairs={{0,4},{4,0},{1,5},{5,1},{2,6},{6,2},{3,7},{7,3},{8,12},{12,8},{9,1... | collective-permute-start | bytes 491528 | tf_op jit(solution)/shard_map/ppermute | solution.py:553
  745.0 4.5 collective-permute-start.13
  751.6 2.4 copy-start.1
Sparse Core Ops, SparseCore 0:
  17.6 88.8 all-gather.6
  109.6 81.6 all-gather.8
  194.4 76.8 all-gather.10
  345.4 96.0 reduce-scatter.2
  475.1 158.3 reduce-scatter.4

commit v2 on v1

--- a/solution.py
+++ b/solution.py
@@ -1,4 +1,5 @@
 import functools
+import itertools
 import math
 
 import jax
@@ -20,6 +21,7 @@
 BF = jnp.bfloat16
 F32 = jnp.float32
 VMEM_LIMIT = 60 * 2**20
+COST_PARTS = 1
 
 NN = (((1,), (0,)), ((), ()))
 NT = (((1,), (1,)), ((), ()))
@@ -35,7 +37,8 @@
 
 
 def cost(flops, nbytes, trans=0):
-    return pl.CostEstimate(flops=int(flops), bytes_accessed=int(nbytes), transcendentals=int(trans))
+    part = lambda n: int(n) // COST_PARTS
+    return pl.CostEstimate(flops=part(flops), bytes_accessed=part(nbytes), transcendentals=part(trans))
 
 
 def shape(dims, dtype):
@@ -70,14 +73,11 @@
     return jnp.sum(values.reshape(rows // 8, 8, columns), axis=0)
 
 
-def accumulate(ref, values):
+def clear_at_start(*refs):
     @pl.when(pl.program_id(0) == 0)
     def _():
-        ref[...] = values
-
-    @pl.when(pl.program_id(0) > 0)
-    def _():
-        ref[...] += values
+        for ref in refs:
+            ref[...] = jnp.zeros_like(ref)
 
 
 GAIN_ONE, SHIFT_ONE, QUERY_BIAS, VALUE_BIAS, OUTPUT_BIAS, GAIN_TWO, SHIFT_TWO, DOWN_BIAS = range(8)
@@ -90,6 +90,25 @@
 def weight_columns(ref, j, rows=slice(None)):
     block = ref[:, j, rows, :]
     return block.reshape(block.shape[0] * block.shape[1], block.shape[2])
+
+
+def pack_body(*refs):
+    out = refs[-1]
+    out[...] = jnp.zeros_like(out)
+    at = 0
+    for ref in refs[:-1]:
+        out[at : at + ref.shape[0], : ref.shape[1]] = ref[...]
+        at += ref.shape[0]
+
+
+def pack(matrices, vectors, extra):
+    rows = sum(m.shape[0] for m in matrices) + extra
+    return pl.pallas_call(
+        pack_body,
+        out_shape=shape((rows, matrices[0].shape[1]), BF),
+        compiler_params=params(),
+        name="pack",
+    )(*matrices, *[v.reshape(1, -1) for v in vectors])
 
 
 def project_body(x_ref, vec_ref, w_ref, x1_ref, q_ref, k_ref, v_ref):
@@ -129,26 +148,30 @@
     return jnp.where(in_first, first + (PIECE - 1), jnp.where(in_second, second + (PIECE - 1), places))
 
 
-def query_blocks(starts_ref, offset_ref, queries, keys, fixed_offset, run):
+def query_groups(starts_ref, offset_ref, queries, keys, fixed_offset, per, run):
     b = pl.program_id(0)
     first, second = starts_ref[b, 0], starts_ref[b, 1]
     offset = offset_ref[0]
     block = min(256, queries)
-    for n in range(queries // block):
-        begin = offset + n * block
-        last = reach_of(begin + (block - 1), first, second)
-        places = begin + lax.broadcasted_iota(jnp.int32, (1, block), 1)
-        reach = reach_of(places, first, second)
-        if fixed_offset:
-            options = range(n + 1, min(n + 2, keys // 256) + 1)
-        else:
-            options = range(1, keys // 256 + 1)
-        for tiles in options:
-            clear = n if fixed_offset else 0
-
-            @pl.when((last >= (tiles - 1) * 256) & (last < tiles * 256))
-            def _(n=n, tiles=tiles, clear=clear, reach=reach):
-                run(slice(n * block, (n + 1) * block), clear * 256, tiles * 256, reach)
+    count = queries // block
+
+    def options(n):
+        return range(n + 1, min(n + 2, keys // 256) + 1) if fixed_offset else range(1, keys // 256 + 1)
+
+    def item(n, tiles):
+        places = offset + n * block + lax.broadcasted_iota(jnp.int32, (1, block), 1)
+        clear = n * 256 if fixed_offset else 0
+        return slice(n * block, (n + 1) * block), clear, tiles * 256, reach_of(places, first, second)
+
+    last = [reach_of(offset + (n + 1) * block - 1, first, second) for n in range(count)]
+    for begin in range(0, count, per):
+        group = range(begin, min(begin + per, count))
+        for tiles in itertools.product(*[options(n) for n in group]):
+            fits = [(last[n] >= (t - 1) * 256) & (last[n] < t * 256) for n, t in zip(group, tiles)]
+
+            @pl.when(functools.reduce(jnp.logical_and, fits))
+            def _(group=group, tiles=tiles):
+                run([item(n, t) for n, t in zip(group, tiles)])
 
 
 def hide(scores, clear, reach):
@@ -167,120 +190,168 @@
     return jnp.where(mask, values, jnp.zeros_like(values))
 
 
-def attend_body(fixed_offset, starts_ref, offset_ref, q_ref, k_ref, v_ref, out_ref, lse_ref):
+def staggered(count, ahead, start, finish):
+    for i in range(min(ahead, count)):
+        start(i)
+    for i in range(count):
+        if i + ahead < count:
+            start(i + ahead)
+        finish(i)
+
+
+POWER = SCALE * LOG2E
+SAFE = 2.0**100
+
+
+def attend_body(fixed_offset, starts_ref, offset_ref, q_ref, k_ref, v_ref, out_ref, lse_ref, vt_ref, worst_ref):
     masks = head_masks()
     queries, keys = q_ref.shape[1], k_ref.shape[1]
-
-    def run(at, clear, span, reach):
-        q = q_ref[0, at, :]
-        k = k_ref[0, :span, :]
-        v = v_ref[0, :span, :]
-        total = None
-        scales = []
-        for h in range(2):
-            s = hide(dot(k, pick(masks[h], q), NT), clear, reach)
-            top = jnp.max(s, axis=0, keepdims=True)
-            p = jnp.exp2((s - top) * (SCALE * LOG2E))
-            size = jnp.sum(p, axis=0, keepdims=True)
-            lse_ref[0, 0, h : h + 1, at] = top * (SCALE * LOG2E) + jnp.log2(size)
-            scales.append(1.0 / size)
-            part = dot(pick(masks[h], v), p.astype(BF), TN)
-            total = part if total is None else total + part
-        half = HEAD_DIM
-        out_ref[:half, at] = (total[:half] * scales[0]).astype(BF)
-        out_ref[half:, at] = (total[half:] * scales[1]).astype(BF)
-
-    query_blocks(starts_ref, offset_ref, queries, keys, fixed_offset, run)
+    pairs = q_ref.shape[2] // 128
+    for p in range(pairs):
+        vt_ref[p * 128 : (p + 1) * 128, :] = v_ref[0, :, p * 128 : (p + 1) * 128].T
+    worst_ref[...] = jnp.zeros_like(worst_ref)
+
+    def run(exact, items):
+        units = [(it, p, h) for it in items for p in range(pairs) for h in range(2)]
+        held = [None] * len(units)
+
+        def start(i):
+            (at, clear, span, reach), p, h = units[i]
+            lanes = slice(p * 128, (p + 1) * 128)
+            held[i] = hide(dot(k_ref[0, :span, lanes], pick(masks[h], q_ref[0, at, lanes]), NT), clear, reach)
+
+        def finish(i):
+            (at, _, span, _), p, h = units[i]
+            s = held[i]
+            top = jnp.max(s, axis=0, keepdims=True) if exact else s[:1]
+            raised = jnp.exp2((s - top) * POWER)
+            size = jnp.sum(raised, axis=0, keepdims=True)
+            if not exact:
+                worst_ref[...] = jnp.maximum(worst_ref[...], size)
+            lse_ref[0, p, h : h + 1, at] = top * POWER + jnp.log2(size)
+            mine = slice(p * 128 + h * HEAD_DIM, p * 128 + (h + 1) * HEAD_DIM)
+            total = dot(vt_ref[mine, :span], raised.astype(BF), NN)
+            out_ref[mine, at] = (total * (1.0 / size)).astype(BF)
+
+        staggered(len(units), 2, start, finish)
+
+    args = (starts_ref, offset_ref, queries, keys, fixed_offset)
+    query_groups(*args, 2, functools.partial(run, False))
+
+    @pl.when(jnp.max(worst_ref[...]) >= SAFE)
+    def _():
+        query_groups(*args, 1, functools.partial(run, True))
 
 
 def attend(starts, offset, q, k, v, fixed_offset):
     count, queries, d = q.shape
     keys = k.shape[1]
-    pairs = d // 128
-    rows = lambda n: pl.BlockSpec((1, n, 128), lambda b, p, *_: (b, 0, p))
+    lanes = 256
+    rows = lambda n: pl.BlockSpec((1, n, lanes), lambda b, p, *_: (b, 0, p))
     return pl.pallas_call(
         functools.partial(attend_body, fixed_offset),
         grid_spec=pltpu.PrefetchScalarGridSpec(
             num_scalar_prefetch=2,
-            grid=(count, pairs),
+            grid=(count, d // lanes),
             in_specs=[rows(queries), rows(keys), rows(keys)],
             out_specs=[
-                pl.BlockSpec((128, queries), lambda b, p, *_: (p, b)),
-                pl.BlockSpec((1, 1, 2, queries), lambda b, p, *_: (b, p, 0, 0)),
+                pl.BlockSpec((lanes, queries), lambda b, p, *_: (p, b)),
+                pl.BlockSpec((1, lanes // 128, 2, queries), lambda b, p, *_: (b, p, 0, 0)),
             ],
+            scratch_shapes=[pltpu.VMEM((lanes, keys), BF), pltpu.VMEM((1, min(256, queries)), F32)],
         ),
-        out_shape=[shape((d, count * queries), BF), shape((count, pairs, 2, queries), F32)],
+        out_shape=[shape((d, count * queries), BF), shape((count, d // 128, 2, queries), F32)],
         compiler_params=params(),
-        cost_estimate=cost(12 * count * queries * keys * d, 8 * count * keys * d, count * pairs * 2 * queries * keys),
+        cost_estimate=cost(12 * count * queries * keys * d, 8 * count * keys * d, count * d // 64 * queries * keys),
         name="attend",
     )(starts, offset, q, k, v)
 
 
 def attend_back_body(
-    fixed_offset, starts_ref, offset_ref, q_ref, k_ref, v_ref, g_ref, lse_ref, dq_ref, dkv_ref, dk_acc, dv_acc
+    fixed_offset, starts_ref, offset_ref, q_ref, k_ref, v_ref, g_ref, att_ref, lse_ref,
+    dq_ref, dkv_ref, kt_ref, settled_ref, dk_acc, dv_acc,
 ):
     masks = head_masks()
     queries, keys = q_ref.shape[1], k_ref.shape[1]
+    pairs = q_ref.shape[2] // 128
     dk_acc[...] = jnp.zeros_like(dk_acc)
     dv_acc[...] = jnp.zeros_like(dv_acc)
-
-    def run(at, clear, span, reach):
-        q = q_ref[0, at, :]
-        g = g_ref[0, at, :]
-        k = k_ref[0, :span, :]
-        v = v_ref[0, :span, :]
-        dq = None
-        chances, slopes, qs, gs = [], [], [], []
+    for p in range(pairs):
+        lanes = slice(p * 128, (p + 1) * 128)
+        kt_ref[lanes, :] = k_ref[0, :, lanes].T
+        both = g_ref[0, :, lanes].T.astype(F32) * att_ref[lanes, :].astype(F32)
         for h in range(2):
-            qh, gh = pick(masks[h], q), pick(masks[h], g)
-            s = hide(dot(k, qh, NT), clear, reach)
-            p = jnp.exp2(s * (SCALE * LOG2E) - lse_ref[0, 0, h : h + 1, at])
-            dp = dot(v, gh, NT)
-            settled = jnp.sum(p * dp, axis=0, keepdims=True)
-            ds = (p * (dp - settled)).astype(BF)
-            part = dot(pick(masks[h], k), ds, TN)
-            dq = part if dq is None else dq + part
-            chances.append(p.astype(BF))
-            slopes.append(ds)
-            qs.append(qh)
-            gs.append(gh)
-        dv_acc[:span, :] += dot(jnp.concatenate(chances, axis=1), jnp.concatenate(gs, axis=0), NN)
-        dk_acc[:span, :] += dot(jnp.concatenate(slopes, axis=1), jnp.concatenate(qs, axis=0), NN)
-        dq_ref[0, at, :] = (dq.T * SCALE).astype(BF)
-
-    query_blocks(starts_ref, offset_ref, queries, keys, fixed_offset, run)
+            part = both[h * HEAD_DIM : (h + 1) * HEAD_DIM]
+            settled_ref[2 * p + h : 2 * p + h + 1, :] = jnp.sum(part, axis=0, keepdims=True)
+
+    def run(items):
+        units = [(it, p, h) for it in items for p in range(pairs) for h in range(2)]
+        held = [None] * len(units)
+        done = {}
+
+        def start(i):
+            (at, clear, span, reach), p, h = units[i]
+            lanes = slice(p * 128, (p + 1) * 128)
+            q, g = pick(masks[h], q_ref[0, at, lanes]), pick(masks[h], g_ref[0, at, lanes])
+            s = hide(dot(k_ref[0, :span, lanes], q, NT), clear, reach)
+            held[i] = (s, dot(v_ref[0, :span, lanes], g, NT), q, g)
+
+        def finish(i):
+            (at, _, span, _), p, h = units[i]
+            s, chance_grad, q, g = held[i]
+            n = 2 * p + h
+            chances = jnp.exp2(s * POWER - lse_ref[0, p, h : h + 1, at])
+            ds = (chances * (chance_grad - settled_ref[n : n + 1, at])).astype(BF)
+            dq = dot(kt_ref[n * HEAD_DIM : (n + 1) * HEAD_DIM, :span], ds, NN)
+            done[h] = (chances.astype(BF), ds, q, g, dq)
+            if h == 1:
+                lanes = slice(p * 128, (p + 1) * 128)
+                join = lambda m, axis: jnp.concatenate([done[0][m], done[1][m]], axis=axis)
+                dv_acc[:span, lanes] += dot(join(0, 1), join(3, 0), NN)
+                dk_acc[:span, lanes] += dot(join(1, 1), join(2, 0), NN)
+                dq_ref[0, at, lanes] = (join(4, 0).T * SCALE).astype(BF)
+
+        staggered(len(units), 2, start, finish)
+
+    query_groups(starts_ref, offset_ref, queries, keys, fixed_offset, 2, run)
     dkv_ref[0, 0] = (dk_acc[...] * SCALE).astype(BF)
     dkv_ref[1, 0] = dv_acc[...].astype(BF)
 
 
-def attend_back(starts, offset, q, k, v, g, lse, fixed_offset):
+def attend_back(starts, offset, q, k, v, g, att, lse, fixed_offset):
     count, queries, d = q.shape
     keys = k.shape[1]
-    pairs = d // 128
-    rows = lambda n: pl.BlockSpec((1, n, 128), lambda b, p, *_: (b, 0, p))
+    lanes = 256
+    rows = lambda n: pl.BlockSpec((1, n, lanes), lambda b, p, *_: (b, 0, p))
     return pl.pallas_call(
         functools.partial(attend_back_body, fixed_offset),
         grid_spec=pltpu.PrefetchScalarGridSpec(
             num_scalar_prefetch=2,
-            grid=(count, pairs),
+            grid=(count, d // lanes),
             in_specs=[
                 rows(queries),
                 rows(keys),
                 rows(keys),
                 rows(queries),
-                pl.BlockSpec((1, 1, 2, queries), lambda b, p, *_: (b, p, 0, 0)),
+                pl.BlockSpec((lanes, queries), lambda b, p, *_: (p, b)),
+                pl.BlockSpec((1, lanes // 128, 2, queries), lambda b, p, *_: (b, p, 0, 0)),
             ],
             out_specs=[
                 rows(queries),
-                pl.BlockSpec((2, 1, keys, 128), lambda b, p, *_: (0, b, 0, p)),
+                pl.BlockSpec((2, 1, keys, lanes), lambda b, p, *_: (0, b, 0, p)),
             ],
-            scratch_shapes=[pltpu.VMEM((keys, 128), F32)] * 2,
+            scratch_shapes=[
+                pltpu.VMEM((lanes, keys), BF),
+                pltpu.VMEM((lanes // HEAD_DIM, queries), F32),
+                pltpu.VMEM((keys, lanes), F32),
+                pltpu.VMEM((keys, lanes), F32),
+            ],
         ),
         out_shape=[shape((count, queries, d), BF), shape((2, count, keys, d), BF)],
         compiler_params=params(),
-        cost_estimate=cost(30 * count * queries * keys * d, 14 * count * keys * d, count * pairs * 2 * queries * keys),
+        cost_estimate=cost(30 * count * queries * keys * d, 14 * count * keys * d, count * d // 64 * queries * keys),
         name="attend_back",
-    )(starts, offset, q, k, v, g, lse)
+    )(starts, offset, q, k, v, g, att, lse)
 
 
 def hidden_chunk(up_ref):
@@ -342,9 +413,10 @@
 
 
 def fall_body(
-    mid_ref, act_ref, slope_ref, og_ref, vec_ref, wo_ref, up_ref, down_ref,
-    out_ref, bg_ref, mg_ref, br_ref, dat_ref, upb_ref, sums_ref,
+    begun, which_ref, mid_ref, act_ref, slope_ref, og_ref, vec_ref, wo_ref, up_ref, down_ref, *rest
 ):
+    out_ref, bg_ref, mg_ref, br_ref, dat_ref, upb_ref, sums_ref = rest[4:] if begun else rest
+    clear_at_start(upb_ref, sums_ref)
     og = og_ref[...]
     incoming = og.astype(F32)
     g, width = down_ref.shape[1], down_ref.shape[3]
@@ -365,7 +437,7 @@
             outs[j] = part if outs[j] is None else outs[j] + part
         bg = (slope_ref[:, at].astype(F32) * rise_grad).astype(BF)
         bg_ref[:, at] = bg
-        accumulate(upb_ref.at[:, at], fold(bg.astype(F32)))
+        upb_ref[:, at] += fold(bg.astype(F32))
         part = dot(bg, up_chunk(up_ref, n, size), NT)
         e = part if e is None else e + part
     middle = mid_ref[...]
@@ -380,42 +452,53 @@
         part = dot(branch[:, j * width : (j + 1) * width], weight_columns(wo_ref, j), NT)
         back = part if back is None else back + part
     dat_ref[...] = back.astype(BF)
-    accumulate(sums_ref.at[0], fold(e * hat))
-    accumulate(sums_ref.at[1], fold(e))
-    accumulate(sums_ref.at[2], fold(branch.astype(F32)))
-    accumulate(sums_ref.at[3], fold(incoming))
-
-
-def fall(middle, act, slope, og, vec, first, up, down, tile):
+    sums_ref[0] += fold(e * hat)
+    sums_ref[1] += fold(e)
+    sums_ref[2] += fold(branch.astype(F32))
+    sums_ref[3] += fold(incoming)
+
+
+def fall(middle, act, slope, og, vec, first, up, down, tile, which, sequences, halves, begun=()):
     tokens, d = og.shape
     dp, g, _, width = first.shape
     per = d // dp
     ff = act.shape[1]
-    tok = pl.BlockSpec((tile, d), lambda i: (i, 0))
-    wide = pl.BlockSpec((tile, ff), lambda i: (i, 0))
+    per_half = tokens // tile // sequences // halves
+    kept = tokens // halves
+
+    def block(i, w):
+        return (i // per_half) * (per_half * halves) + w[0] * per_half + i % per_half, 0
+
+    tok = pl.BlockSpec((tile, d), block)
+    wide = pl.BlockSpec((tile, ff), block)
+    fixed = lambda dims: once(dims, lambda i, w: (0,) * len(dims))
     return pl.pallas_call(
-        fall_body,
-        grid=(tokens // tile,),
-        in_specs=[
-            tok, wide, wide, tok,
-            once((8, d), lambda i: (0, 0)),
-            once((dp, g, per, width), lambda i: (0, 0, 3, 0)),
-            once(up.shape, lambda i: (0, 0, 0, 0)),
-            once(down.shape, lambda i: (0, 0, 0, 0)),
-        ],
-        out_specs=[
-            tok, wide, tok, tok, tok,
-            pl.BlockSpec((8, ff), lambda i: (0, 0)),
-            pl.BlockSpec((4, 8, d), lambda i: (0, 0, 0)),
-        ],
+        functools.partial(fall_body, bool(begun)),
+        grid_spec=pltpu.PrefetchScalarGridSpec(
+            num_scalar_prefetch=1,
+            grid=(kept // tile,),
+            in_specs=[
+                tok, wide, wide, tok,
+                fixed((8, d)),
+                once((dp, g, per, width), lambda i, w: (0, 0, 3, 0)),
+                fixed(up.shape),
+                fixed(down.shape),
+            ] + [pl.BlockSpec(memory_space=pl.ANY)] * len(begun),
+            out_specs=[
+                pl.BlockSpec((tile, d), lambda i, w: (i, 0)), wide, tok, tok, tok,
+                pl.BlockSpec((8, ff), lambda i, w: (0, 0)),
+                pl.BlockSpec((4, 8, d), lambda i, w: (0, 0, 0)),
+            ],
+        ),
         out_shape=[
-            shape((tokens, d), BF), shape((tokens, ff), BF), shape((tokens, d), F32), shape((tokens, d), BF),
+            shape((kept, d), BF), shape((tokens, ff), BF), shape((tokens, d), F32), shape((tokens, d), BF),
             shape((tokens, d), BF), shape((8, ff), F32), shape((4, 8, d), F32),
         ],
+        input_output_aliases={9 + n: 1 + n for n in range(len(begun))},
         compiler_params=params(),
-        cost_estimate=cost(2 * tokens * d * (d + 3 * ff), tokens * (16 * d + 6 * ff) + 2 * d * (d + 2 * ff)),
+        cost_estimate=cost(2 * kept * d * (d + 3 * ff), kept * (16 * d + 6 * ff) + 2 * d * (d + 2 * ff)),
         name="fall",
-    )(middle, act, slope, og, vec, first, up, down)
+    )(which, middle, act, slope, og, vec, first, up, down, *begun)
 
 
 def split_cores(core_ref, values, keep_ref, send_ref):
@@ -488,7 +571,8 @@
     )(core, x, dy)
 
 
-def input_body(x_ref, mg_ref, dq_ref, dkv_ref, vec_ref, w_ref, out_ref, sums_ref):
+def input_body(which_ref, x_ref, mg_ref, dq_ref, dkv_ref, vec_ref, w_ref, out_ref, sums_ref):
+    clear_at_start(sums_ref)
     groups, per, width = w_ref.shape[1], w_ref.shape[2] // 3, w_ref.shape[3]
     e = None
     grads = (dq_ref[...], dkv_ref[0], dkv_ref[1])
@@ -499,32 +583,44 @@
             e = part if e is None else e + part
     hat, inverse = norm_parts(x_ref[...].astype(F32))
     out_ref[...] = (mg_ref[...] + norm_back(e, hat, inverse, row(vec_ref, GAIN_ONE))).astype(BF)
-    accumulate(sums_ref.at[0], fold(e * hat))
-    accumulate(sums_ref.at[1], fold(e))
-    accumulate(sums_ref.at[2], fold(grads[0].astype(F32)))
-    accumulate(sums_ref.at[3], fold(grads[2].astype(F32)))
-
-
-def input_back(x, mg, dq, dkv, vec, first, tile):
+    sums_ref[0] += fold(e * hat)
+    sums_ref[1] += fold(e)
+    sums_ref[2] += fold(grads[0].astype(F32))
+    sums_ref[3] += fold(grads[2].astype(F32))
+
+
+def input_back(x, mg, dq, dkv, vec, first, tile, which, sequences, halves):
     tokens, d = x.shape
     dp, g, rows, width = first.shape
     per = d // dp
-    tok = pl.BlockSpec((tile, d), lambda i: (i, 0))
+    per_half = tokens // tile // sequences // halves
+
+    def block(i, which):
+        return (i // per_half) * (per_half * halves) + which[0] * per_half + i % per_half
+
+    tok = pl.BlockSpec((tile, d), lambda i, w: (block(i, w), 0))
+    kept = tokens // halves
     return pl.pallas_call(
         input_body,
-        grid=(tokens // tile,),
-        in_specs=[
-            tok, tok, tok,
-            pl.BlockSpec((2, tile, d), lambda i: (0, i, 0)),
-            once((8, d), lambda i: (0, 0)),
-            once((dp, g, 3 * per, width), lambda i: (0, 0, 0, 0)),
-        ],
-        out_specs=[tok, pl.BlockSpec((4, 8, d), lambda i: (0, 0, 0))],
-        out_shape=[shape((tokens, d), BF), shape((4, 8, d), F32)],
+        grid_spec=pltpu.PrefetchScalarGridSpec(
+            num_scalar_prefetch=1,
+            grid=(kept // tile,),
+            in_specs=[
+                tok, tok, tok,
+                pl.BlockSpec((2, tile, d), lambda i, w: (0, block(i, w), 0)),
+                once((8, d), lambda i, w: (0, 0)),
+                once((dp, g, 3 * per, width), lambda i, w: (0, 0, 0, 0)),
+            ],
+            out_specs=[
+                pl.BlockSpec((tile, d), lambda i, w: (i, 0)),
+                pl.BlockSpec((4, 8, d), lambda i, w: (0, 0, 0)),
+            ],
+        ),
+        out_shape=[shape((kept, d), BF), shape((4, 8, d), F32)],
         compiler_params=params(),
-        cost_estimate=cost(6 * tokens * d * d, 16 * tokens * d + 6 * d * d),
+        cost_estimate=cost(6 * kept * d * d, 16 * kept * d + 6 * d * d),
         name="input_back",
-    )(x, mg, dq, dkv, vec, first)
+    )(which, x, mg, dq, dkv, vec, first)
 
 
 def swap_cores(values):
@@ -547,22 +643,45 @@
 ALONG = ("seq", [(0, 1), (1, 0)])
 
 
+def cut(values, dim, own, route):
+    keep = lax.dynamic_index_in_dim(values, own, dim, keepdims=False)
+    return keep, lax.dynamic_index_in_dim(values, 1 - own, dim, keepdims=False), route
+
+
+def add_step(step, came):
+    return (step[0].astype(F32) + came.astype(F32)).astype(BF)
+
+
 def halve(values, dim, own, route):
-    keep = lax.dynamic_index_in_dim(values, own, dim, keepdims=False)
-    send = lax.dynamic_index_in_dim(values, 1 - own, dim, keepdims=False)
-    return (keep.astype(F32) + lax.ppermute(send, *route).astype(F32)).astype(BF)
-
-
-def add_chips_stepwise(mine, across_first):
-    z, x, y = (lax.axis_index(name) for name in ("z", "x", "seq"))
+    step = cut(values, dim, own, route)
+    return add_step(step, lax.ppermute(step[1], *route))
+
+
+def start_step(mine, across_first):
     values = mine.reshape((2, 2, 2) + mine.shape[1:])
     if across_first:
-        values = halve(values, 2, x, ACROSS)
-    values = halve(values, 1, z % 2, NEAR)
-    values = halve(values, 0, z // 2, FAR)
-    if not across_first:
-        values = halve(values, 0, x, ACROSS)
-    return halve(values, 0, y, ALONG).astype(F32)
+        return cut(values, 2, lax.axis_index("x"), ACROSS)
+    return cut(values, 1, lax.axis_index("z") % 2, NEAR)
+
+
+def next_step(values, across_first):
+    if across_first:
+        return cut(values, 1, lax.axis_index("z") % 2, NEAR)
+    return cut(values, 0, lax.axis_index("z") // 2, FAR)
+
+
+def last_steps(values, across_first):
+    if across_first:
+        values = halve(values, 0, lax.axis_index("z") // 2, FAR)
+    else:
+        values = halve(values, 0, lax.axis_index("x"), ACROSS)
+    return halve(values, 0, lax.axis_index("seq"), ALONG).astype(F32)
+
+
+def all_steps(mine):
+    step = start_step(mine, True)
+    step = next_step(add_step(step, lax.ppermute(step[1], *step[2])), True)
+    return last_steps(add_step(step, lax.ppermute(step[1], *step[2])), True)
 
 
 def body(
@@ -584,36 +703,27 @@
     core = lax.axis_index("core").astype(jnp.int32).reshape(1)
     paired = g == 2 and count % 2 == 0
 
-    vectors = jnp.concatenate(
-        [first_gain, first_shift, query_bias, value_bias, output_bias, second_gain, second_shift, down_bias, up_bias]
-    )
-    extra = -(-vectors.shape[0] // (16 * width)) * 16
-    vectors = jnp.pad(vectors, (0, extra * width - vectors.shape[0])).reshape(extra, width)
-    packed = jnp.concatenate([query_weight, key_weight, value_weight, output_weight, vectors], axis=0)
+    vectors = [first_gain, first_shift, query_bias, value_bias, output_bias, second_gain, second_shift, down_bias]
+    extra = 16
+    packed = pack([query_weight, key_weight, value_weight, output_weight], vectors + [up_bias], extra)
     first = lax.all_gather(packed, everyone, axis=0).reshape(dp, g, 4 * per + extra, width)
     up = lax.all_gather(up_weight, everyone, axis=0).reshape((dp, g) + up_weight.shape)
     down = lax.all_gather(down_weight, everyone, axis=0).reshape((dp, g) + down_weight.shape)
 
-    flat = first[:, :, 4 * per :, :].reshape(dp * g, extra * width)[:, : 8 * small + wide].astype(F32)
-    vec = flat[:, : 8 * small].reshape(dp * g, 8, small).transpose(1, 0, 2).reshape(8, d)
-    upb = flat[:, 8 * small :].reshape(1, ff)
-
     if paired:
         half = count // 2
 
-        def gather_rows(values):
+        def swap_rows(values, *earlier):
+            sent = lax.dynamic_slice_in_dim(values, (1 - place) * half, half, 0)
+            return lax.ppermute(after(sent, *earlier), "seq", [(0, 1), (1, 0)])
+
+        def gather_rows(values, came):
             kept = lax.dynamic_slice_in_dim(values, place * half, half, 0)
-            sent = lax.dynamic_slice_in_dim(values, (1 - place) * half, half, 0)
-            came = lax.ppermute(sent, "seq", [(0, 1), (1, 0)])
             low = jnp.where(place == 0, kept, came)
             high = jnp.where(place == 0, came, kept)
             return jnp.concatenate([low, high], axis=1).reshape(half * length, d)
 
-        def return_rows(values):
-            values = values.reshape(half, 2, local, d)
-            kept = lax.dynamic_index_in_dim(values, place, 1, keepdims=False)
-            sent = lax.dynamic_index_in_dim(values, 1 - place, 1, keepdims=False)
-            came = lax.ppermute(sent, "seq", [(0, 1), (1, 0)])
+        def join_rows(kept, came):
             low = jnp.where(place == 0, kept, came)
             high = jnp.where(place == 0, came, kept)
             return jnp.concatenate([low, high], axis=0)
@@ -622,42 +732,80 @@
         offset = jnp.zeros((1,), jnp.int32)
         sequences, queries = half, length
     else:
-        gather_rows = lambda values: values.reshape(count * local, d)
-        return_rows = lambda values: values.reshape(count, local, d)
+        swap_rows = lambda values, *earlier: values
+        gather_rows = lambda values, came: values.reshape(count * local, d)
         starts = piece_starts
         offset = (place * local).astype(jnp.int32).reshape(1)
         sequences, queries = count, local
 
     rows = sequences * queries
     tile = min(256, rows)
-    x = gather_rows(tokens)
-    og = gather_rows(after(out_grad, first))
+    x = gather_rows(tokens, swap_rows(tokens))
+    first = after(first, x)
+    vec = first[:, :, 4 * per : 4 * per + 8, :small].astype(F32).transpose(2, 0, 1, 3).reshape(8, d)
+    upb = first[:, :, 4 * per + 8, :wide].astype(F32).reshape(1, ff)
+    came = swap_rows(out_grad, first)
     x1, q, k, v = project(x, vec, first, tile)
     q, k, v = (t.reshape(sequences, queries, d) for t in (q, k, v))
     if not paired:
         k, v = (lax.all_gather(t, "seq", axis=1, tiled=True) for t in (k, v))
     att, lse = attend(starts, offset, q, k, v, paired)
+    og = gather_rows(out_grad, after(came, att))
     middle, x2, act, slope = rise(x, att, vec, upb, first, up, tile)
     down_mine = add_cores(*down_grad(core, act, og, dp, g))
     down_sum = add_chips(down_mine)
     act = after(act, down_mine)
-    out, bg, mg, branch, dat, upb_sums, sums_two = fall(middle, act, slope, og, vec, first, up, down, tile)
-    output = return_rows(out)
+    args = (middle, act, slope, og, vec, first, up, down, tile)
+    if paired:
+        turn = place.astype(jnp.int32).reshape(1)
+        out_sent, *begun, upb_sent, two_sent = fall(*args, 1 - turn, sequences, 2)
+        out, *begun, upb_sums, sums_two = fall(*args, turn, sequences, 2, tuple(begun))
+        bg, mg, branch, dat = begun
+        upb_sums, sums_two = upb_sums + upb_sent, sums_two + two_sent
+        came_out = lax.ppermute(out_sent.reshape(half, local, d), *ALONG)
+    else:
+        out, bg, mg, branch, dat, upb_sums, sums_two = fall(*args, jnp.zeros((1,), jnp.int32), sequences, 1)
+        output = out.reshape(count, local, d)
     up_parts = weight_grad(core, x2, bg[None], dp, g, TN, "up_grad")
     out_parts = weight_grad(core, att, branch[None], dp, g, NN, "out_grad")
+    if paired:
+        up_parts, out_parts, came_out = lax.optimization_barrier((up_parts, out_parts, came_out))
+        output = join_rows(out.reshape(half, local, d), came_out)
     up_mine = jnp.concatenate([add_cores(*up_parts), add_cores(*out_parts)], axis=-1)
     up_sum = add_chips(up_mine)
     dat = after(dat, up_mine, down_sum)
-    dq, dkv = attend_back(starts, offset, q, k, v, dat.reshape(sequences, queries, d), lse, paired)
-    dq = after(dq.reshape(rows, d), output)
+    dq, dkv = attend_back(starts, offset, q, k, v, dat.reshape(sequences, queries, d), att, lse, paired)
+    dq = dq.reshape(rows, d)
     if not paired:
         dkv = lax.psum_scatter(dkv, "seq", scatter_dimension=2, tiled=True)
     dkv = dkv.reshape(2, rows, d)
     query_parts = weight_grad(core, x1, dq[None], dp, g, TN, "query_grad")
     kv_parts = weight_grad(core, x1, dkv, dp, g, TN, "key_value_grad")
-    matrix_mine = jnp.concatenate([add_cores(*query_parts), add_cores(*kv_parts)], axis=2)
-    in_grad, sums_one = input_back(x, mg, dq, after(dkv, matrix_mine, up_sum), vec, first, tile)
-    input_grad = return_rows(in_grad)
+    query_mine, kv_mine = add_cores(*query_parts), add_cores(*kv_parts)
+    first_parts = jnp.concatenate([query_mine, kv_mine[:, :, :per]], axis=2)
+    second_parts = kv_mine[:, :, per:]
+    stepwise = (lax.axis_size("z"), lax.axis_size("x"), g) == (4, 2, 2)
+    dkv = after(dkv, first_parts, second_parts, up_sum)
+    args = (x, mg, dq, dkv, vec, first, tile)
+    if paired:
+        sent, sums_sent = input_back(*args, 1 - turn, sequences, 2)
+        came_in = lax.ppermute(sent.reshape(half, local, d), *ALONG)
+        if stepwise:
+            steps = [start_step(first_parts, True), start_step(second_parts, False)]
+            arrived = [after(lax.ppermute(move, *route), sent) for _, move, route in steps]
+            steps = [next_step(add_step(step, move), n == 0) for n, (step, move) in enumerate(zip(steps, arrived))]
+            arrived = [lax.ppermute(move, *route) for _, move, route in steps]
+            args = args[:3] + (after(dkv, steps[0][1], steps[1][1]),) + args[4:]
+        in_grad, sums_one = input_back(*args, turn, sequences, 2)
+        if stepwise:
+            arrived[0], arrived[1], came_in, sums_one = lax.optimization_barrier((*arrived, came_in, sums_one))
+            summed = [add_step(step, move) for step, move in zip(steps, arrived)]
+        sums_one = sums_one + sums_sent
+        came_in = lax.ppermute(sent.reshape(half, local, d), "seq", [(0, 1), (1, 0)])
+        input_grad = join_rows(in_grad.reshape(half, local, d), came_in)
+    else:
+        in_grad, sums_one = input_back(*args, jnp.zeros((1,), jnp.int32), sequences, 1)
+        input_grad = in_grad.reshape(count, local, d)
 
     one, two = jnp.sum(sums_one, axis=1), jnp.sum(sums_two, axis=1)
     eight = jnp.stack([one[0], one[1], one[2], one[3], two[2], two[0], two[1], two[3]])
@@ -671,12 +819,11 @@
         lax.dynamic_index_in_dim(lines, own, 0, keepdims=False),
         lax.dynamic_index_in_dim(lines, 1 - own, 0, keepdims=False),
     )
-    if (lax.axis_size("z"), lax.axis_size("x"), g) == (4, 2, 2):
-        tail = jnp.concatenate([matrix_mine[:, :, 2 * per :], line_mine], axis=2)
-        last = [add_chips_stepwise(matrix_mine[:, :, : 2 * per], True), add_chips_stepwise(tail, False)]
+    if stepwise:
+        last = [last_steps(summed[0], True), last_steps(summed[1], False), all_steps(line_mine)]
         last = jnp.concatenate(last, axis=0)
     else:
-        last = add_chips(jnp.concatenate([matrix_mine, line_mine], axis=2))
+        last = add_chips(jnp.concatenate([first_parts, second_parts, line_mine], axis=2))
     dw = [last[m * per : (m + 1) * per] for m in range(3)] + [up_sum[:, -width:]]
     up_sum = up_sum[:, :-width]
     line = last[3 * per :].reshape(extra * width)

time: 768 us -> 647 us (0.84)
  Pallas kernels: 433 us -> 367 us
  waiting for transfers between devices: 213 us -> 178 us
  local copies, waits for them, and re-layouts: 34.9 us -> 15.4 us
    all_gather x1, waiting for transfers between devices: 81.4 us -> 24.5 us  [body(): lax.all_gather(packed, everyone, axis=0)]
    pallas_call x1, Pallas kernels: 111 us -> 71.9 us  [attend_back(): pl.pallas_call(functools.partial(attend_back_body, fixed_offset), grid_sp...]
    pallas_call x1, Pallas kernels: 64.9 us -> 33.6 us  [attend(): pl.pallas_call(functools.partial(attend_body, fixed_offset), grid_spec=pl...]
    all_gather x1, waiting for transfers between devices: 0.01 us -> 24.9 us  [body(): lax.all_gather(up_weight, everyone, axis=0)]
    ppermute x12 -> x16, waiting for transfers between devices: 117 us -> 103 us  [the longest x2 50.2 us: swap_rows(): return lax.ppermute(after(sent, *earlier), 'seq', [(0, 1), (1, 0)])]
    pallas_call x2 -> x5, Pallas kernels: 109 us -> 113 us  [the longest x2 84 us: fall(): pl.pallas_call(functools.partial(fall_body, bool(begun)), grid_spec=pltpu...]
    ppermute x12 -> x16, starting transfers between devices: 20.6 us -> 21.3 us  [the longest x6 6.61 us: halve(): return add_step(step, lax.ppermute(step[1], *route))]
  transfers between devices with their start and end apart: 23 -> 27, of which waited for: 11 -> 17; matrix products, arithmetic and copies ran while one was open for 8% -> 9% of each run, Pallas kernels for 57% -> 57%
where the time goes in v2:
time: 647 us; the launch traced here: 643 us
  Pallas kernels  367 us (57%)
  waiting for transfers between devices  178 us (28%)
  other arithmetic  43.2 us (7%)
  starting transfers between devices  25.4 us (4%)
  local copies, waits for them, and re-layouts  15.4 us (2%)
  between operations  14.5 us (2%)
    pallas_call x2, Pallas kernels, fall(): pl.pallas_call(functools.partial(fall_body, bool(begun)), grid_spec=pltpu...  84 us
    pallas_call x1, Pallas kernels, attend_back(): pl.pallas_call(functools.partial(attend_back_body, fixed_offset), grid_sp...  71.9 us
    pallas_call x4, Pallas kernels, weight_grad(): pl.pallas_call(functools.partial(weight_grad_body, form), grid_spec=pltpu...  53.9 us
    pallas_call x1, Pallas kernels, rise(): pl.pallas_call(rise_body, grid=(tokens // tile,), in_specs=[tok, pl.Block...  50.3 us
    ppermute x2, waiting for transfers between devices, swap_rows(): return lax.ppermute(after(sent, *earlier), 'seq', [(0, 1), (1, 0)])  50.2 us
    pallas_call x1, Pallas kernels, attend(): pl.pallas_call(functools.partial(attend_body, fixed_offset), grid_spec=pl...  33.6 us
    pallas_call x2, Pallas kernels, input_back(): pl.pallas_call(input_body, grid_spec=pltpu.PrefetchScalarGridSpec(num_sca...  27.6 us
    all_gather x1, waiting for transfers between devices, body(): lax.all_gather(up_weight, everyone, axis=0)  24.9 us
  transfers between devices with their start and end apart: 27, of which 17 were waited for; matrix products, arithmetic and copies ran while one was open for 9% of the time, Pallas kernels for 57%

profile of v2, /device:TPU:0, one launch (start us, length us, event | category | flops | bytes accessed | tf_op | source)
XLA Modules:
  0.0 642.6 jit_solution(13628701545591499768)
XLA Ops:
  7.3 1.8 pack.1
  10.6 3.1 constant_dynamic-slice_fusion.6
  13.7 3.0 collective-permute-start
  17.3 3.2 constant_dynamic-slice_fusion.4
  20.5 50.2 %collective-permute-done = bf16[2,512,1024]{2,1,0:T(8,128)(2,1)S(1)} collective-permute-done((bf16[2,512,1024]{2,1,0:T(8,128)(2,1)}, bf16[2,512,1024]{2,1,0:T(8,128)(2,1)S(1)}, u32[]{:S(2)}, u32[]{:S(2)}) %collective-permute-start) | collective-permute-done | bytes 2097184 | tf_op jit(solution)/shard_map/ppermute | solution.py:718
  71.0 2.5 pad_maximum_fusion.1
  73.5 24.5 %all-gather.7.cloned.1.call-done = bf16[8704,512]{1,0:T(8,128)(2,1)} async-done(((bf16[272,512]{1,0:T(8,128)(2,1)}), bf16[8704,512]{1,0:T(8,128)(2,1)}) %all-gather.7.cloned.1.call-update) | async-done | bytes 8912912 | tf_op jit(solution)/shard_map/all_gather | solution.py:709
  98.0 0.8 convert_bitcast_fusion
  99.7 1.5 collective-permute-start.1
  101.3 20.5 %project.1 = (bf16[2048,1024]{1,0:T(8,128)(2,1)}, bf16[2048,1024]{1,0:T(8,128)(2,1)}, bf16[2048,1024]{1,0:T(8,128)(2,1)}, bf16[2048,1024]{1,0:T(8,128)(2,1)}) custom-call(bf16[2048,1024]{1,0:T(8,128)(2,1)} %bitcast.138, f32[8,1024]{1,0:T(8,128)} %reshape.235.vec_ref, bf16[16,2,272,512]{3,2,1,0:T(8,128)(2,1)} %bitcast.131), custom_call_target="tpu_custom_call" | custom-call | flops 12884901888 | bytes 27262976 | tf_op jit(solution)/shard_map/project/pallas_call | solution.py:133
  121.8 33.6 %attend.1 = (bf16[1024,2048]{1,0:T(8,128)(2,1)}, f32[2,8,2,1024]{3,2,1,0:T(2,128)}) custom-call(s32[2,2]{1,0:T(2,128)} %copy.65.starts_ref, s32[1]{0:T(128)} %constant.135.clone.1.offset_ref, bf16[2,1024,1024]{2,1,0:T(8,128)(2,1)} %bitcast.187, bf16[2,1024,1024]{2,1,0:T(8,128)(2,1)} %bitcast.189, bf16[2,1024,1024]{2,1,0:T(8,128)(2,1)} %bitcast.191), custom_call_target="tpu_custom_call" | custom-call | flops 25769803776 | bytes 16777216 | tf_op jit(solution)/shard_map/attend/pallas_call | solution.py:251
  155.4 0.9 slice.71
  156.8 24.9 %all-gather.9.cloned.1.call-done = bf16[2048,2048]{1,0:T(8,128)(2,1)} async-done(((bf16[64,2048]{1,0:T(8,128)(2,1)}), bf16[2048,2048]{1,0:T(8,128)(2,1)}) %all-gather.9.cloned.1.call-update) | async-done | bytes 8388624 | tf_op jit(solution)/shard_map/all_gather | solution.py:710
  181.7 50.3 %rise.1 = (f32[2048,1024]{1,0:T(8,128)}, bf16[2048,1024]{1,0:T(8,128)(2,1)}, bf16[2048,4096]{1,0:T(8,128)(2,1)}, bf16[2048,4096]{1,0:T(8,128)(2,1)}) custom-call(bf16[2048,1024]{1,0:T(8,128)(2,1)} %bitcast.139, bf16[1024,2048]{1,0:T(8,128)(2,1)} %get-tuple-element.78.att_ref.x_ref, f32[8,1024]{1,0:T(8,128)} %reshape.235.vec_ref, f32[1,4096]{1,0:T(1,128)} %convert.45.upb_ref, ...), custom_call_target="tpu_custom_call" | custom-call | flops 21474836480 | bytes 65011712 | tf_op jit(solution)/shard_map/rise/pallas_call | solution.py:396
  232.0 2.4 broadcast_select_fusion.5
  234.4 2.4 pad_maximum_fusion.2
  236.8 22.9 %down_grad.1 = (bf16[8,2,256,512]{3,2,1,0:T(8,128)(2,1)}, bf16[8,2,256,512]{3,2,1,0:T(8,128)(2,1)}) custom-call(s32[1]{0:T(128)} %bitcast.18.core_ref, bf16[2048,4096]{1,0:T(8,128)(2,1)} %get-tuple-element.85.act_ref, bf16[2048,1024]{1,0:T(8,128)(2,1)} %bitcast.147), custom_call_target="tpu_custom_call" | custom-call | flops 17179869184 | bytes 29360128 | tf_op jit(solution)/shard_map/down_grad/pallas_call | solution.py:526
  260.0 7.3 %collective-permute-done.2 = bf16[8,2,256,512]{3,2,1,0:T(8,128)(2,1)S(1)} collective-permute-done((bf16[8,2,256,512]{3,2,1,0:T(8,128)(2,1)}, bf16[8,2,256,512]{3,2,1,0:T(8,128)(2,1)S(1)}, u32[]{:S(2)}, u32[]{:S(2)}) %collective-permute-start.2) | collective-permute-done | bytes 4194336 | tf_op jit(solution)/shard_map/ppermute | solution.py:627
  267.3 5.2 add_convert_fusion.1
  272.7 42.0 %fall.2 = (bf16[1024,1024]{1,0:T(8,128)(2,1)}, bf16[2048,4096]{1,0:T(8,128)(2,1)}, f32[2048,1024]{1,0:T(8,128)}, bf16[2048,1024]{1,0:T(8,128)(2,1)}, bf16[2048,1...) custom-call(s32[1]{0:T(128)S(6)} %sub.36.which_ref, f32[2048,1024]{1,0:T(8,128)} %get-tuple-element.79.mid_ref, ...), custom_call_target="tpu_custom_call" | custom-call | flops 27917287424 | bytes 60817408 | tf_op jit(solution)/shard_map/fall/pallas_call | solution.py:475
  314.6 1.6 collective-permute-start.3
  316.2 42.0 %fall.3 = (bf16[1024,1024]{1,0:T(8,128)(2,1)}, bf16[2048,4096]{1,0:T(8,128)(2,1)}, f32[2048,1024]{1,0:T(8,128)}, bf16[2048,1024]{1,0:T(8,128)(2,1)}, bf16[2048,1...) custom-call(s32[1]{0:T(128)} %bitcast.which_ref, ...), custom_call_target="tpu_custom_call", output_to_operand_aliasing={{1}: (9, {}), {2}: (10, {}), {3}: (11, {}), {4}: (12, {})} | custom-call | flops 27917287424 | bytes 60817408 | tf_op jit(solution)/shard_map/fall/pallas_call | solution.py:475
  358.3 8.6 %out_grad.1 = (bf16[8,2,64,512]{3,2,1,0:T(8,128)(2,1)}, bf16[8,2,64,512]{3,2,1,0:T(8,128)(2,1)}) custom-call(s32[1]{0:T(128)} %bitcast.18.core_ref, bf16[1024,2048]{1,0:T(8,128)(2,1)} %get-tuple-element.78.att_ref.x_ref, bf16[1,2048,1024]{2,1,0:T(8,128)(2,1)} %bitcast.160), custom_call_target="tpu_custom_call" | custom-call | flops 4294967296 | bytes 10485760 | tf_op jit(solution)/shard_map/out_grad/pallas_call | solution.py:556
  366.8 23.3 %up_grad.1 = (bf16[8,2,64,2048]{3,2,1,0:T(8,128)(2,1)}, bf16[8,2,64,2048]{3,2,1,0:T(8,128)(2,1)}) custom-call(s32[1]{0:T(128)} %bitcast.18.core_ref, bf16[2048,1024]{1,0:T(8,128)(2,1)} %get-tuple-element.92.x_ref, bf16[1,2048,4096]{2,1,0:T(8,128)(2,1)} %bitcast.150), custom_call_target="tpu_custom_call" | custom-call | flops 17179869184 | bytes 29360128 | tf_op jit(solution)/shard_map/up_grad/pallas_call | solution.py:556
  390.1 20.5 %collective-permute-done.3 = bf16[2,512,1024]{2,1,0:T(8,128)(2,1)S(1)} collective-permute-done((bf16[2,512,1024]{2,1,0:T(8,128)(2,1)}, bf16[2,512,1024]{2,1,0:T(8,128)(2,1)S(1)}, u32[]{:S(2)}, u32[]{:S(2)}) %collective-permute-start.3) | collective-permute-done | bytes 2097184 | tf_op jit(solution)/shard_map/ppermute | solution.py:765
  411.1 8.4 %collective-permute-done.5 = bf16[8,2,64,512]{3,2,1,0:T(8,128)(2,1)S(1)} collective-permute-done((bf16[8,2,64,512]{3,2,1,0:T(8,128)(2,1)}, bf16[8,2,64,512]{3,2,1,0:T(8,128)(2,1)S(1)}, u32[]{:S(2)}, u32[]{:S(2)}) %collective-permute-start.5) | collective-permute-done | bytes 1048608 | tf_op jit(solution)/shard_map/ppermute | solution.py:627
  419.8 3.5 add_convert_fusion
  423.3 2.8 pad_maximum_fusion
  426.2 1.8 bitcast_convert_fusion.1
  428.0 71.9 %attend_back.1 = (bf16[2,1024,1024]{2,1,0:T(8,128)(2,1)}, bf16[2,2,1024,1024]{3,2,1,0:T(8,128)(2,1)}) custom-call(s32[2,2]{1,0:T(2,128)} %copy.65.starts_ref, s32[1]{0:T(128)} %constant.135.clone.1.offset_ref, bf16[2,1024,1024]{2,1,0:T(8,128)(2,1)} %bitcast.188, bf16[2,1024,1024]{2,1,0:T(8,128)(2,1)} %bitcast.190, bf16[2,1024,1024]{2,1,0:T(8,128)(2,1)} %bitcast.192, ...), custom_call_target="tpu_custom_call" | custom-call | flops 64424509440 | bytes 29360128 | tf_op jit(solution)/shard_map/attend_back/pallas_call | solution.py:326
  500.0 13.5 %key_value_grad.1 = (bf16[8,2,128,512]{3,2,1,0:T(8,128)(2,1)}, bf16[8,2,128,512]{3,2,1,0:T(8,128)(2,1)}) custom-call(s32[1]{0:T(128)} %bitcast.18.core_ref, bf16[2048,1024]{1,0:T(8,128)(2,1)} %get-tuple-element.111.x_ref, bf16[2,2048,1024]{2,1,0:T(8,128)(2,1)} %bitcast.142), custom_call_target="tpu_custom_call" | custom-call | flops 8589934592 | bytes 16777216 | tf_op jit(solution)/shard_map/key_value_grad/pallas_call | solution.py:556
  513.5 3.0 collective-permute-start.7
  516.5 8.6 %query_grad.1 = (bf16[8,2,64,512]{3,2,1,0:T(8,128)(2,1)}, bf16[8,2,64,512]{3,2,1,0:T(8,128)(2,1)}) custom-call(s32[1]{0:T(128)} %bitcast.18.core_ref, bf16[2048,1024]{1,0:T(8,128)(2,1)} %get-tuple-element.111.x_ref, bf16[1,2048,1024]{2,1,0:T(8,128)(2,1)} %bitcast.151), custom_call_target="tpu_custom_call" | custom-call | flops 4294967296 | bytes 10485760 | tf_op jit(solution)/shard_map/query_grad/pallas_call | solution.py:556
  525.2 1.1 add_reduce_fusion
  528.0 1.6 add_convert_fusion.3
  529.6 2.3 add_convert_fusion.2
  532.4 1.1 copy.79
  533.6 7.6 %reduce-scatter.5.cloned.1.call-done = bf16[1,64,2560]{2,1,0:T(8,128)(2,1)} async-done(((bf16[16,64,2560]{2,1,0:T(8,128)(2,1)}), bf16[1,64,2560]{2,1,0:T(8,128)(2,1)}) %reduce-scatter.5.cloned.1.call-update) | async-done | bytes 327696 | tf_op jit(solution)/shard_map/reduce_scatter | solution.py:637
  541.1 1.0 bitcast_convert_fusion
  542.2 13.8 %input_back.2 = (bf16[1024,1024]{1,0:T(8,128)(2,1)}, f32[4,8,1024]{2,1,0:T(8,128)}) custom-call(s32[1]{0:T(128)S(6)} %sub.36.which_ref, bf16[2048,1024]{1,0:T(8,128)(2,1)} %bitcast.140, f32[2048,1024]{1,0:T(8,128)} %get-tuple-element.101.mg_ref, bf16[2048,1024]{1,0:T(8,128)(2,1)} %bitcast.152, bf16[2,2048,1024]{2,1,0:T(8,128)(2,1)} %bitcast.143, ...), custom_call_target="tpu_custom_call" | custom-call | flops 6442450944 | bytes 23068672 | tf_op jit(solution)/shard_map/input_back/pallas_call | solution.py:603
  556.3 1.7 collective-permute-start.9
  557.9 2.5 broadcast_select_fusion.3
  560.4 2.4 pad_maximum_fusion.3
  562.8 6.8 %collective-permute-done.9 = bf16[2,2,2,64,512]{4,3,2,1,0:T(8,128)(2,1)S(1)} collective-permute-done((bf16[2,2,2,64,512]{4,3,2,1,0:T(8,128)(2,1)S(1)}, bf16[2,2,2,64,512]{4,3,2,1,0:T(8,128)(2,1)S(1)}, u32[]{:S(2)}, u32[]{:S(2)}) %collective-permute-start.9) | collective-permute-done | bytes 524320 | tf_op jit(solution)/shard_map/ppermute | solution.py:795
  569.8 2.7 collective-permute-start.12
  572.5 1.6 fusion
  574.1 1.6 collective-permute-start.11
  575.7 13.9 %input_back.3 = (bf16[1024,1024]{1,0:T(8,128)(2,1)}, f32[4,8,1024]{2,1,0:T(8,128)}) custom-call(s32[1]{0:T(128)} %bitcast.which_ref, bf16[2048,1024]{1,0:T(8,128)(2,1)} %bitcast.141, f32[2048,1024]{1,0:T(8,128)} %get-tuple-element.101.mg_ref, bf16[2048,1024]{1,0:T(8,128)(2,1)} %bitcast.153, bf16[2,2048,1024]{2,1,0:T(8,128)(2,1)} %bitcast.144, ...), custom_call_target="tpu_custom_call" | custom-call | flops 6442450944 | bytes 23068672 | tf_op jit(solution)/shard_map/input_back/pallas_call | solution.py:603
  591.1 11.7 %collective-permute-done.10 = bf16[2,512,1024]{2,1,0:T(8,128)(2,1)} collective-permute-done((bf16[2,512,1024]{2,1,0:T(8,128)(2,1)}, bf16[2,512,1024]{2,1,0:T(8,128)(2,1)}, u32[]{:S(2)}, u32[]{:S(2)}) %collective-permute-start.10) | collective-permute-done | bytes 2097184 | tf_op jit(solution)/shard_map/ppermute | solution.py:804
  602.9 1.2 add_reduce_fusion.2
  604.4 1.0 fusion.6
  605.5 0.9 collective-permute-start.20
  606.4 2.5 collective-permute-start.18
  609.1 1.9 broadcast_select_fusion.1
  611.6 2.4 pad_maximum_fusion.4
  614.0 1.6 collective-permute-done.21
  617.2 2.9 collective-permute-done.18
  620.2 1.4 collective-permute-done.14
  621.6 1.6 collective-permute-start.15
  624.0 2.0 collective-permute-done.15
  626.0 1.1 collective-permute-start.16
  627.2 1.1 collective-permute-done.19
  628.3 2.6 collective-permute-done.16
  632.5 2.3 collective-permute-done.17
  (108 shorter events, 16.1 us)
Async XLA Ops:
  7.2 9.4 %copy-start = (s32[4,2]{0,1:T(2,128)S(1)}, s32[4,2]{0,1:T(2,128)}, u32[]{:S(2)}) copy-start(s32[4,2]{0,1:T(2,128)} %param.34) | copy-start | bytes 100
  7.2 90.8 %all-gather.7.cloned.1.call-start = ((), (), s32[]{:S(2)}) async-start(), calls=%async_computation.4 | async-start | bytes 9191424 | tf_op jit(solution)/shard_map/all_gather | solution.py:709
  9.0 172.7 %all-gather.9.cloned.1.call-start = ((), (), s32[]{:S(2)}) async-start(), calls=%async_computation.5 | async-start | bytes 8650752 | tf_op jit(solution)/shard_map/all_gather | solution.py:710
  9.8 262.9 %all-gather.11.cloned.1.call-start = ((), (), s32[]{:S(2)}) async-start(), calls=%async_computation.6 | async-start | bytes 8650752 | tf_op jit(solution)/shard_map/all_gather | solution.py:711
  10.5 415.7 %reduce-scatter.3.cloned.1.call-start = ((), (), s32[]{:S(2)}) async-start(), calls=%async_computation.2 | async-start | bytes 4456448 | tf_op jit(solution)/shard_map/reduce_scatter | solution.py:637
  13.7 57.1 %collective-permute-start = (bf16[2,512,1024]{2,1,0:T(8,128)(2,1)}, bf16[2,512,1024]{2,1,0:T(8,128)(2,1)S(1)}, u32[]{:S(2)}, u32[]{:S(2)}) collective-permute-start(bf16[2,512,1024]{2,1,0:T(8,128)(2,1)} %constant_dynamic-slice_fusion.6), channel_id=1, source_target_pairs={{0,1},{1,0},{2,3},{3,2},{4,5},{5,4},{6,7},{7,6},{8,9},{9,8},{10,11... | collective-permute-start | bytes 6291464 | tf_op jit(solution)/shard_map/ppermute | solution.py:718
  17.3 53.5 %copy-start.2 = (bf16[4,512,1024]{2,1,0:T(8,128)(2,1)S(1)}, bf16[4,512,1024]{2,1,0:T(8,128)(2,1)}, u32[]{:S(2)}) copy-start(bf16[4,512,1024]{2,1,0:T(8,128)(2,1)} %param.18) | copy-start | bytes 12582916
  99.7 132.3 %collective-permute-start.1 = (bf16[2,512,1024]{2,1,0:T(8,128)(2,1)}, bf16[2,512,1024]{2,1,0:T(8,128)(2,1)S(1)}, u32[]{:S(2)}, u32[]{:S(2)}) collective-permute-start(bf16[2,512,1024]{2,1,0:T(8,128)(2,1)} %constant_dynamic-slice_fusion.4), channel_id=1, source_target_pairs={{0,1},{1,0},{2,3},{3,2},{4,5},{5,4},{6,7},{7,6},{8,9},{9,8},{10,11... | collective-permute-start | bytes 6291464 | tf_op jit(solution)/shard_map/ppermute | solution.py:718
  259.7 7.6 %collective-permute-start.2 = (bf16[8,2,256,512]{3,2,1,0:T(8,128)(2,1)}, bf16[8,2,256,512]{3,2,1,0:T(8,128)(2,1)S(1)}, u32[]{:S(2)}, u32[]{:S(2)}) collective-permute-start(bf16[8,2,256,512]{3,2,1,0:T(8,128)(2,1)} %get-tuple-element.84), channel_id=1, source_target_pairs={{0,2},{2,0},{1,3},{3,1},{4,6},{6,4},{5,7},{7,5},{8,10},{10,8},{9,1... | collective-permute-start | bytes 12582920 | tf_op jit(solution)/shard_map/ppermute | solution.py:627
  272.6 268.6 %reduce-scatter.5.cloned.1.call-start = ((), (), s32[]{:S(2)}) async-start(), calls=%async_computation.3 | async-start | bytes 5570560 | tf_op jit(solution)/shard_map/reduce_scatter | solution.py:637
  314.6 95.9 %collective-permute-start.3 = (bf16[2,512,1024]{2,1,0:T(8,128)(2,1)}, bf16[2,512,1024]{2,1,0:T(8,128)(2,1)S(1)}, u32[]{:S(2)}, u32[]{:S(2)}) collective-permute-start(bf16[2,512,1024]{2,1,0:T(8,128)(2,1)} %bitcast.186), channel_id=1, source_target_pairs={{0,1},{1,0},{2,3},{3,2},{4,5},{5,4},{6,7},{7,6},{8,9},{9,8},{10,11... | collective-permute-start | bytes 6291464 | tf_op jit(solution)/shard_map/ppermute | solution.py:765
  366.8 52.6 %copy-start.6 = (bf16[8,2,64,512]{3,2,1,0:T(8,128)(2,1)S(1)}, bf16[8,2,64,512]{3,2,1,0:T(8,128)(2,1)}, u32[]{:S(2)}) copy-start(bf16[8,2,64,512]{3,2,1,0:T(8,128)(2,1)} %get-tuple-element.105) | copy-start | bytes 3145732
  410.6 12.7 %copy-start.4 = (bf16[2,512,1024]{2,1,0:T(8,128)(2,1)}, bf16[2,512,1024]{2,1,0:T(8,128)(2,1)S(1)}, u32[]{:S(2)}) copy-start(bf16[2,512,1024]{2,1,0:T(8,128)(2,1)S(1)} %collective-permute-done.3) | copy-start | bytes 6291460
  410.6 9.2 %collective-permute-start.4 = (bf16[8,2,64,2048]{3,2,1,0:T(8,128)(2,1)}, bf16[8,2,64,2048]{3,2,1,0:T(8,128)(2,1)S(1)}, u32[]{:S(2)}, u32[]{:S(2)}) collective-permute-start(bf16[8,2,64,2048]{3,2,1,0:T(8,128)(2,1)} %get-tuple-element.104), channel_id=1, source_target_pairs={{0,2},{2,0},{1,3},{3,1},{4,6},{6,4},{5,7},{7,5},{8,10},{10,8},{9,1... | collective-permute-start | bytes 12582920 | tf_op jit(solution)/shard_map/ppermute | solution.py:627
  410.6 8.8 %collective-permute-start.5 = (bf16[8,2,64,512]{3,2,1,0:T(8,128)(2,1)}, bf16[8,2,64,512]{3,2,1,0:T(8,128)(2,1)S(1)}, u32[]{:S(2)}, u32[]{:S(2)}) collective-permute-start(bf16[8,2,64,512]{3,2,1,0:T(8,128)(2,1)} %get-tuple-element.106), channel_id=1, source_target_pairs={{0,2},{2,0},{1,3},{3,1},{4,6},{6,4},{5,7},{7,5},{8,10},{10,8},{9,1... | collective-permute-start | bytes 3145736 | tf_op jit(solution)/shard_map/ppermute | solution.py:627
  513.5 16.1 %collective-permute-start.7 = (bf16[8,2,128,512]{3,2,1,0:T(8,128)(2,1)}, bf16[8,2,128,512]{3,2,1,0:T(8,128)(2,1)}, u32[]{:S(2)}, u32[]{:S(2)}) collective-permute-start(bf16[8,2,128,512]{3,2,1,0:T(8,128)(2,1)} %get-tuple-element.115), channel_id=1, source_target_pairs={{0,2},{2,0},{1,3},{3,1},{4,6},{6,4},{5,7},{7,5},{8,10},{10,8},{9,1... | collective-permute-start | bytes 6291464 | tf_op jit(solution)/shard_map/ppermute | solution.py:627
  516.4 8.7 %copy-start.8 = (f32[8,4096]{1,0:T(8,128)S(1)}, f32[8,4096]{1,0:T(8,128)}, u32[]{:S(2)}) copy-start(f32[8,4096]{1,0:T(8,128)} %get-tuple-element.128) | copy-start | bytes 393220
  516.4 10.4 %copy-start.7 = (f32[4,8,1024]{2,1,0:T(8,128)S(1)}, f32[4,8,1024]{2,1,0:T(8,128)}, u32[]{:S(2)}) copy-start(f32[4,8,1024]{2,1,0:T(8,128)} %get-tuple-element.126) | copy-start | bytes 393220
  516.4 10.4 %copy-start.9 = (f32[4,8,1024]{2,1,0:T(8,128)S(1)}, f32[4,8,1024]{2,1,0:T(8,128)}, u32[]{:S(2)}) copy-start(f32[4,8,1024]{2,1,0:T(8,128)} %get-tuple-element.125) | copy-start | bytes 393220
  525.1 4.5 copy-start.3
  525.1 2.9 collective-permute-start.6
  526.9 5.0 copy-start.10
  533.6 36.0 %collective-permute-start.8 = (bf16[2,2,2,128,512]{4,3,2,0,1:T(8,128)(2,1)}, bf16[2,2,2,128,512]{4,3,2,0,1:T(8,128)(2,1)}, u32[]{:S(2)}, u32[]{:S(2)}) collective-permute-start(bf16[2,2,2,128,512]{4,3,2,0,1:T(8,128)(2,1)} %bitcast.127), channel_id=1, source_target_pairs={{0,4},{4,0},{1,5},{5,1},{2,6},{6,2},{3,7},{7,3},{8,12},{12,8},{9,1... | collective-permute-start | bytes 3145736 | tf_op jit(solution)/shard_map/ppermute | solution.py:795
  555.9 46.8 %collective-permute-start.10 = (bf16[2,512,1024]{2,1,0:T(8,128)(2,1)}, bf16[2,512,1024]{2,1,0:T(8,128)(2,1)}, u32[]{:S(2)}, u32[]{:S(2)}) collective-permute-start(bf16[2,512,1024]{2,1,0:T(8,128)(2,1)} %bitcast.185), channel_id=1, source_target_pairs={{0,1},{1,0},{2,3},{3,2},{4,5},{5,4},{6,7},{7,6},{8,9},{9,8},{10,11... | collective-permute-start | bytes 6291464 | tf_op jit(solution)/shard_map/ppermute | solution.py:804
  556.3 13.3 %collective-permute-start.9 = (bf16[2,2,2,64,512]{4,3,2,1,0:T(8,128)(2,1)S(1)}, bf16[2,2,2,64,512]{4,3,2,1,0:T(8,128)(2,1)S(1)}, u32[]{:S(2)}, u32[]{:S(2)}) collective-permute-start(bf16[2,2,2,64,512]{4,3,2,1,0:T(8,128)(2,1)S(1)} %dynamic-slice_bitcast_fusion), channel_id=1, source_target_pairs={{0,8},{8,0},{16,24},{24,16},{1,9},{9,1},{17,25},{25,17},{2,10},{10... | collective-permute-start | bytes 1572872 | tf_op jit(solution)/shard_map/ppermute | solution.py:795
  569.8 21.3 %collective-permute-start.12 = (bf16[2,2,64,512]{3,2,1,0:T(8,128)(2,1)S(1)}, bf16[2,2,64,512]{3,2,1,0:T(8,128)(2,1)}, u32[]{:S(2)}, u32[]{:S(2)}) collective-permute-start(bf16[2,2,64,512]{3,2,1,0:T(8,128)(2,1)S(1)} %dynamic-slice_bitcast_fusion.3), channel_id=1, source_target_pairs={{0,16},{16,0},{8,24},{24,8},{1,17},{17,1},{9,25},{25,9},{2,18},{18... | collective-permute-start | bytes 786440 | tf_op jit(solution)/shard_map/ppermute | solution.py:797
  574.1 30.0 %slice-start = ((bf16[4,1024]{1,0:T(4,128)(2,1)}), bf16[2,1024]{1,0:T(2,128)(2,1)S(1)}, s32[]{:S(2)}) async-start(bf16[4,1024]{1,0:T(4,128)(2,1)} %copy-done.10), calls=%async_computation.7 | async-start | bytes 8192 | tf_op jit(solution)/shard_map/slice | solution.py:811
  574.1 30.0 %copy-start.12 = (bf16[1,1024]{1,0:T(2,128)(2,1)S(1)}, bf16[1,1024]{1,0:T(2,128)(2,1)}, u32[]{:S(2)}) copy-start(bf16[1,1024]{1,0:T(2,128)(2,1)} %get-tuple-element.156) | copy-start | bytes 6148
  574.1 16.9 %collective-permute-start.11 = (bf16[2,2,128,512]{3,2,1,0:T(8,128)(2,1)S(1)}, bf16[2,2,128,512]{3,2,1,0:T(8,128)(2,1)S(1)}, u32[]{:S(2)}, u32[]{:S(2)}) collective-permute-start(bf16[2,2,128,512]{3,2,1,0:T(8,128)(2,1)S(1)} %dynamic-slice_bitcast_fusion.1), channel_id=1, source_target_pairs={{0,8},{8,0},{16,24},{24,16},{1,9},{9,1},{17,25},{25,17},{2,10},{10... | collective-permute-start | bytes 1572872 | tf_op jit(solution)/shard_map/ppermute | solution.py:797
  589.6 19.2 %copy-start.11 = (bf16[8,2,2,128]{3,0,2,1:T(8,128)(2,1)S(1)}, bf16[8,2,2,128]{3,0,2,1:T(8,128)(2,1)}, u32[]{:S(2)}) copy-start(bf16[8,2,2,128]{3,0,2,1:T(8,128)(2,1)} %copy.81) | copy-start | bytes 24580
  602.9 6.2 copy-start.5
  605.5 5.5 collective-permute-start.20
  606.4 13.8 %collective-permute-start.18 = (bf16[2,128,512]{2,1,0:T(8,128)(2,1)S(1)}, bf16[2,128,512]{2,1,0:T(8,128)(2,1)S(1)}, u32[]{:S(2)}, u32[]{:S(2)}) collective-permute-start(bf16[2,128,512]{2,1,0:T(8,128)(2,1)S(1)} %dynamic-slice_bitcast_fusion.2), channel_id=1, source_target_pairs={{0,16},{16,0},{8,24},{24,8},{1,17},{17,1},{9,25},{25,9},{2,18},{18... | collective-permute-start | bytes 786440 | tf_op jit(solution)/shard_map/ppermute | solution.py:657
  609.0 7.3 %collective-permute-start.13 = (bf16[8,2,16,512]{3,2,1,0:T(8,128)(2,1)S(1)}, bf16[8,2,16,512]{3,2,1,0:T(8,128)(2,1)S(1)}, u32[]{:S(2)}, u32[]{:S(2)}) collective-permute-start(bf16[8,2,16,512]{3,2,1,0:T(8,128)(2,1)S(1)} %bitcast.170), channel_id=1, source_target_pairs={{0,2},{2,0},{1,3},{3,1},{4,6},{6,4},{5,7},{7,5},{8,10},{10,8},{9,1... | collective-permute-start | bytes 786440 | tf_op jit(solution)/shard_map/ppermute | solution.py:627
  611.1 4.5 collective-permute-start.21
  611.6 24.3 %copy-start.1 = (s32[4,2]{0,1:T(2,128)S(1)}, s32[4,2]{0,1:T(2,128)}, u32[]{:S(2)}) copy-start(s32[4,2]{0,1:T(2,128)} %param.34) | copy-start | bytes 100
  616.4 5.2 collective-permute-start.14
  621.6 4.3 collective-permute-start.15
  623.2 5.0 collective-permute-start.19
  626.0 4.9 collective-permute-start.16
  630.9 3.8 collective-permute-start.17
Sparse Core Ops, SparseCore 0:
  11.5 86.4 all-gather.6
  101.1 80.5 all-gather.8
  184.8 76.9 all-gather.10
  272.7 118.1 reduce-scatter.2
  426.3 114.8 reduce-scatter.4

commit v3 on v2

--- a/solution.py
+++ b/solution.py
@@ -364,52 +364,69 @@
     return block.reshape(block.shape[0] * block.shape[1], size)
 
 
-def rise_body(x_ref, att_ref, vec_ref, upb_ref, wo_ref, up_ref, mid_ref, x2_ref, act_ref, slope_ref):
+def settle_body(x_ref, att_ref, vec_ref, wo_ref, mid_ref, x2_ref):
     att = att_ref[...]
-    width = wo_ref.shape[3]
     parts = [dot(att, weight_columns(wo_ref, j), TN) for j in range(wo_ref.shape[1])]
     branch = jnp.concatenate(parts, axis=1)
     middle = x_ref[...].astype(F32) + (branch + row(vec_ref, OUTPUT_BIAS))
     mid_ref[...] = middle
     hat, _ = norm_parts(middle)
-    x2 = (hat * row(vec_ref, GAIN_TWO) + row(vec_ref, SHIFT_TWO)).astype(BF)
-    x2_ref[...] = x2
+    x2_ref[...] = (hat * row(vec_ref, GAIN_TWO) + row(vec_ref, SHIFT_TWO)).astype(BF)
+
+
+def settle(x, att, vec, first, tile):
+    tokens, d = x.shape
+    dp, g, _, width = first.shape
+    per = d // dp
+    tok = pl.BlockSpec((tile, d), lambda i: (i, 0))
+    return pl.pallas_call(
+        settle_body,
+        grid=(tokens // tile,),
+        in_specs=[
+            tok,
+            pl.BlockSpec((d, tile), lambda i: (0, i)),
+            once((8, d), lambda i: (0, 0)),
+            once((dp, g, per, width), lambda i: (0, 0, 3, 0)),
+        ],
+        out_specs=[tok, tok],
+        out_shape=[shape((tokens, d), F32), shape((tokens, d), BF)],
+        compiler_params=params(),
+        cost_estimate=cost(2 * tokens * d * d, 10 * tokens * d + 2 * d * d),
+        name="settle",
+    )(x, att, vec, first)
+
+
+def rise_body(x2_ref, upb_ref, up_ref, act_ref, slope_ref):
+    x2 = x2_ref[...]
     size = hidden_chunk(up_ref)
     for n in range(up_ref.shape[1] * up_ref.shape[3] // size):
         at = slice(n * size, (n + 1) * size)
         x = dot(x2, up_chunk(up_ref, n, size), NN) + upb_ref[:, at]
         square = x * x
-        t = jnp.tanh(x * (BENDING + (BENDING * CUBIC_TERM) * square))
-        half = 0.5 * (1.0 + t)
+        half = 0.5 + 0.5 * jnp.tanh(x * (BENDING + (BENDING * CUBIC_TERM) * square))
         act_ref[:, at] = (x * half).astype(BF)
-        bend = (0.5 * BENDING) * x * (1.0 + (3.0 * CUBIC_TERM) * square)
-        slope_ref[:, at] = (half + bend * (1.0 - t * t)).astype(BF)
-
-
-def rise(x, att, vec, upb, first, up, tile):
-    tokens, d = x.shape
-    dp, g, _, width = first.shape
-    per = d // dp
+        bend = x * (2.0 * BENDING + (6.0 * BENDING * CUBIC_TERM) * square)
+        slope_ref[:, at] = (half + half * (1.0 - half) * bend).astype(BF)
+
+
+def rise(x2, upb, up, tile):
+    tokens, d = x2.shape
     ff = upb.shape[1]
-    tok = pl.BlockSpec((tile, d), lambda i: (i, 0))
     wide = pl.BlockSpec((tile, ff), lambda i: (i, 0))
     return pl.pallas_call(
         rise_body,
         grid=(tokens // tile,),
         in_specs=[
-            tok,
-            pl.BlockSpec((d, tile), lambda i: (0, i)),
-            once((8, d), lambda i: (0, 0)),
+            pl.BlockSpec((tile, d), lambda i: (i, 0)),
             once((1, ff), lambda i: (0, 0)),
-            once((dp, g, per, width), lambda i: (0, 0, 3, 0)),
             once(up.shape, lambda i: (0, 0, 0, 0)),
         ],
-        out_specs=[tok, tok, wide, wide],
-        out_shape=[shape((tokens, d), F32), shape((tokens, d), BF), shape((tokens, ff), BF), shape((tokens, ff), BF)],
-        compiler_params=params(),
-        cost_estimate=cost(2 * tokens * d * (d + ff), tokens * (10 * d + 4 * ff) + 2 * d * (d + ff), tokens * ff),
+        out_specs=[wide, wide],
+        out_shape=[shape((tokens, ff), BF), shape((tokens, ff), BF)],
+        compiler_params=params(),
+        cost_estimate=cost(2 * tokens * d * ff, tokens * (2 * d + 4 * ff) + 2 * d * ff, tokens * ff),
         name="rise",
-    )(x, att, vec, upb, first, up)
+    )(x2, upb, up)
 
 
 def fall_body(
@@ -751,7 +768,8 @@
         k, v = (lax.all_gather(t, "seq", axis=1, tiled=True) for t in (k, v))
     att, lse = attend(starts, offset, q, k, v, paired)
     og = gather_rows(out_grad, after(came, att))
-    middle, x2, act, slope = rise(x, att, vec, upb, first, up, tile)
+    middle, x2 = settle(x, att, vec, first, tile)
+    act, slope = rise(after(x2, og), upb, up, min(512, rows))
     down_mine = add_cores(*down_grad(core, act, og, dp, g))
     down_sum = add_chips(down_mine)
     act = after(act, down_mine)

time: 647 us -> 639 us (0.988)
  waiting for transfers between devices: 178 us -> 155 us
  Pallas kernels: 367 us -> 385 us
    all_gather x1, waiting for transfers between devices: 24.9 us -> 0.01 us  [body(): lax.all_gather(up_weight, everyone, axis=0)]
    pallas_call x1, Pallas kernels: 33.6 us -> 46.4 us  [attend(): pl.pallas_call(functools.partial(attend_body, fixed_offset), grid_spec=pl...]
    pallas_call x1 -> x2, Pallas kernels: 50.3 us -> 53 us  [the longest x1 40.1 us: rise(): pl.pallas_call(rise_body, grid=(tokens // tile,), in_specs=[pl.BlockSpec(...]
  transfers between devices with their start and end apart: 27 -> 27, of which waited for: 17 -> 16; matrix products, arithmetic and copies ran while one was open for 9% -> 9% of each run, Pallas kernels for 57% -> 60%
where the time goes in v3:
time: 639 us; the launch traced here: 635 us
  Pallas kernels  385 us (60%)
  waiting for transfers between devices  155 us (24%)
  other arithmetic  42.7 us (7%)
  starting transfers between devices  22.7 us (4%)
  local copies, waits for them, and re-layouts  15.4 us (2%)
  between operations  14.7 us (2%)
    pallas_call x2, Pallas kernels, fall(): pl.pallas_call(functools.partial(fall_body, bool(begun)), grid_spec=pltpu...  84.2 us
    pallas_call x1, Pallas kernels, attend_back(): pl.pallas_call(functools.partial(attend_back_body, fixed_offset), grid_sp...  74.5 us
    pallas_call x4, Pallas kernels, weight_grad(): pl.pallas_call(functools.partial(weight_grad_body, form), grid_spec=pltpu...  53.9 us
    ppermute x2, waiting for transfers between devices, swap_rows(): return lax.ppermute(after(sent, *earlier), 'seq', [(0, 1), (1, 0)])  50.2 us
    pallas_call x1, Pallas kernels, attend(): pl.pallas_call(functools.partial(attend_body, fixed_offset), grid_spec=pl...  46.4 us
    pallas_call x1, Pallas kernels, rise(): pl.pallas_call(rise_body, grid=(tokens // tile,), in_specs=[pl.BlockSpec(...  40.1 us
    pallas_call x2, Pallas kernels, input_back(): pl.pallas_call(input_body, grid_spec=pltpu.PrefetchScalarGridSpec(num_sca...  27.7 us
    all_gather x1, waiting for transfers between devices, body(): lax.all_gather(packed, everyone, axis=0)  24.5 us
  transfers between devices with their start and end apart: 27, of which 16 were waited for; matrix products, arithmetic and copies ran while one was open for 9% of the time, Pallas kernels for 60%

profile of v3, /device:TPU:0, one launch (start us, length us, event | category | flops | bytes accessed | tf_op | source)
XLA Modules:
  0.0 635.3 jit_solution(6035950426619226400)
XLA Ops:
  7.3 1.8 pack.1
  10.6 3.1 constant_dynamic-slice_fusion.6
  13.7 3.0 collective-permute-start
  17.4 3.2 constant_dynamic-slice_fusion.4
  20.6 50.2 %collective-permute-done = bf16[2,512,1024]{2,1,0:T(8,128)(2,1)S(1)} collective-permute-done((bf16[2,512,1024]{2,1,0:T(8,128)(2,1)}, bf16[2,512,1024]{2,1,0:T(8,128)(2,1)S(1)}, u32[]{:S(2)}, u32[]{:S(2)}) %collective-permute-start) | collective-permute-done | bytes 2097184 | tf_op jit(solution)/shard_map/ppermute | solution.py:735
  71.0 2.5 pad_maximum_fusion.1
  73.5 24.5 %all-gather.7.cloned.1.call-done = bf16[8704,512]{1,0:T(8,128)(2,1)} async-done(((bf16[272,512]{1,0:T(8,128)(2,1)}), bf16[8704,512]{1,0:T(8,128)(2,1)}) %all-gather.7.cloned.1.call-update) | async-done | bytes 8912912 | tf_op jit(solution)/shard_map/all_gather | solution.py:726
  98.0 0.8 slice.71
  99.5 0.8 convert_bitcast_fusion
  100.4 0.8 reshape.235.vec_ref
  101.2 1.5 collective-permute-start.1
  102.7 20.5 %project.1 = (bf16[2048,1024]{1,0:T(8,128)(2,1)}, bf16[2048,1024]{1,0:T(8,128)(2,1)}, bf16[2048,1024]{1,0:T(8,128)(2,1)}, bf16[2048,1024]{1,0:T(8,128)(2,1)}) custom-call(bf16[2048,1024]{1,0:T(8,128)(2,1)} %bitcast.138, f32[8,1024]{1,0:T(8,128)} %reshape.235.vec_ref, bf16[16,2,272,512]{3,2,1,0:T(8,128)(2,1)} %bitcast.132), custom_call_target="tpu_custom_call" | custom-call | flops 12884901888 | bytes 27262976 | tf_op jit(solution)/shard_map/project/pallas_call | solution.py:133
  123.2 46.4 %attend.1 = (bf16[1024,2048]{1,0:T(8,128)(2,1)}, f32[2,8,2,1024]{3,2,1,0:T(2,128)}) custom-call(s32[2,2]{1,0:T(2,128)} %copy.65.starts_ref, s32[1]{0:T(128)} %constant.135.clone.1.offset_ref, bf16[2,1024,1024]{2,1,0:T(8,128)(2,1)} %bitcast.187, bf16[2,1024,1024]{2,1,0:T(8,128)(2,1)} %bitcast.189, bf16[2,1024,1024]{2,1,0:T(8,128)(2,1)} %bitcast.191), custom_call_target="tpu_custom_call" | custom-call | flops 25769803776 | bytes 16777216 | tf_op jit(solution)/shard_map/attend/pallas_call | solution.py:251
  169.7 12.9 %settle.1 = (f32[2048,1024]{1,0:T(8,128)}, bf16[2048,1024]{1,0:T(8,128)(2,1)}) custom-call(bf16[2048,1024]{1,0:T(8,128)(2,1)} %bitcast.139, bf16[1024,2048]{1,0:T(8,128)(2,1)} %get-tuple-element.79.att_ref.x_ref, f32[8,1024]{1,0:T(8,128)} %reshape.235.vec_ref, bf16[16,2,272,512]{3,2,1,0:T(8,128)(2,1)} %bitcast.133), custom_call_target="tpu_custom_call" | custom-call | flops 4294967296 | bytes 23068672 | tf_op jit(solution)/shard_map/settle/pallas_call | solution.py:382
  182.5 1.9 broadcast_select_fusion.5
  184.4 2.4 pad_maximum_fusion.2
  186.8 40.1 %rise.1 = (bf16[2048,4096]{1,0:T(8,128)(2,1)}, bf16[2048,4096]{1,0:T(8,128)(2,1)}) custom-call(bf16[2048,1024]{1,0:T(8,128)(2,1)} %get-tuple-element.84.x2_ref.x_ref, f32[1,4096]{1,0:T(1,128)} %convert.45.upb_ref, bf16[16,2,64,2048]{3,2,1,0:T(8,128)(2,1)} %bitcast.155), custom_call_target="tpu_custom_call" | custom-call | flops 17179869184 | bytes 46137344 | tf_op jit(solution)/shard_map/rise/pallas_call | solution.py:416
  227.0 23.0 %down_grad.1 = (bf16[8,2,256,512]{3,2,1,0:T(8,128)(2,1)}, bf16[8,2,256,512]{3,2,1,0:T(8,128)(2,1)}) custom-call(s32[1]{0:T(128)} %bitcast.19.core_ref, bf16[2048,4096]{1,0:T(8,128)(2,1)} %get-tuple-element.88.act_ref, bf16[2048,1024]{1,0:T(8,128)(2,1)} %bitcast.147), custom_call_target="tpu_custom_call" | custom-call | flops 17179869184 | bytes 29360128 | tf_op jit(solution)/shard_map/down_grad/pallas_call | solution.py:543
  250.3 7.5 %collective-permute-done.2 = bf16[8,2,256,512]{3,2,1,0:T(8,128)(2,1)S(1)} collective-permute-done((bf16[8,2,256,512]{3,2,1,0:T(8,128)(2,1)}, bf16[8,2,256,512]{3,2,1,0:T(8,128)(2,1)S(1)}, u32[]{:S(2)}, u32[]{:S(2)}) %collective-permute-start.2) | collective-permute-done | bytes 4194336 | tf_op jit(solution)/shard_map/ppermute | solution.py:644
  257.8 5.3 add_convert_fusion.1
  263.2 42.0 %fall.2 = (bf16[1024,1024]{1,0:T(8,128)(2,1)}, bf16[2048,4096]{1,0:T(8,128)(2,1)}, f32[2048,1024]{1,0:T(8,128)}, bf16[2048,1024]{1,0:T(8,128)(2,1)}, bf16[2048,1...) custom-call(s32[1]{0:T(128)S(6)} %sub.36.which_ref, f32[2048,1024]{1,0:T(8,128)} %get-tuple-element.80.mid_ref, ...), custom_call_target="tpu_custom_call" | custom-call | flops 27917287424 | bytes 60817408 | tf_op jit(solution)/shard_map/fall/pallas_call | solution.py:492
  305.1 1.3 collective-permute-start.3
  306.4 42.3 %fall.3 = (bf16[1024,1024]{1,0:T(8,128)(2,1)}, bf16[2048,4096]{1,0:T(8,128)(2,1)}, f32[2048,1024]{1,0:T(8,128)}, bf16[2048,1024]{1,0:T(8,128)(2,1)}, bf16[2048,1...) custom-call(s32[1]{0:T(128)} %bitcast.which_ref, ...), custom_call_target="tpu_custom_call", output_to_operand_aliasing={{1}: (9, {}), {2}: (10, {}), {3}: (11, {}), {4}: (12, {})} | custom-call | flops 27917287424 | bytes 60817408 | tf_op jit(solution)/shard_map/fall/pallas_call | solution.py:492
  348.7 8.5 %out_grad.1 = (bf16[8,2,64,512]{3,2,1,0:T(8,128)(2,1)}, bf16[8,2,64,512]{3,2,1,0:T(8,128)(2,1)}) custom-call(s32[1]{0:T(128)} %bitcast.19.core_ref, bf16[1024,2048]{1,0:T(8,128)(2,1)} %get-tuple-element.79.att_ref.x_ref, bf16[1,2048,1024]{2,1,0:T(8,128)(2,1)} %bitcast.160), custom_call_target="tpu_custom_call" | custom-call | flops 4294967296 | bytes 10485760 | tf_op jit(solution)/shard_map/out_grad/pallas_call | solution.py:573
  357.2 23.3 %up_grad.1 = (bf16[8,2,64,2048]{3,2,1,0:T(8,128)(2,1)}, bf16[8,2,64,2048]{3,2,1,0:T(8,128)(2,1)}) custom-call(s32[1]{0:T(128)} %bitcast.19.core_ref, bf16[2048,1024]{1,0:T(8,128)(2,1)} %get-tuple-element.84.x2_ref.x_ref, bf16[1,2048,4096]{2,1,0:T(8,128)(2,1)} %bitcast.150), custom_call_target="tpu_custom_call" | custom-call | flops 17179869184 | bytes 29360128 | tf_op jit(solution)/shard_map/up_grad/pallas_call | solution.py:573
  380.5 22.5 %collective-permute-done.3 = bf16[2,512,1024]{2,1,0:T(8,128)(2,1)S(1)} collective-permute-done((bf16[2,512,1024]{2,1,0:T(8,128)(2,1)}, bf16[2,512,1024]{2,1,0:T(8,128)(2,1)S(1)}, u32[]{:S(2)}, u32[]{:S(2)}) %collective-permute-start.3) | collective-permute-done | bytes 2097184 | tf_op jit(solution)/shard_map/ppermute | solution.py:783
  403.5 8.4 %collective-permute-done.5 = bf16[8,2,64,512]{3,2,1,0:T(8,128)(2,1)S(1)} collective-permute-done((bf16[8,2,64,512]{3,2,1,0:T(8,128)(2,1)}, bf16[8,2,64,512]{3,2,1,0:T(8,128)(2,1)S(1)}, u32[]{:S(2)}, u32[]{:S(2)}) %collective-permute-start.5) | collective-permute-done | bytes 1048608 | tf_op jit(solution)/shard_map/ppermute | solution.py:644
  412.2 3.5 add_convert_fusion
  415.7 2.8 pad_maximum_fusion
  418.6 1.8 bitcast_convert_fusion.1
  420.4 74.5 %attend_back.1 = (bf16[2,1024,1024]{2,1,0:T(8,128)(2,1)}, bf16[2,2,1024,1024]{3,2,1,0:T(8,128)(2,1)}) custom-call(s32[2,2]{1,0:T(2,128)} %copy.65.starts_ref, s32[1]{0:T(128)} %constant.135.clone.1.offset_ref, bf16[2,1024,1024]{2,1,0:T(8,128)(2,1)} %bitcast.188, bf16[2,1024,1024]{2,1,0:T(8,128)(2,1)} %bitcast.190, bf16[2,1024,1024]{2,1,0:T(8,128)(2,1)} %bitcast.192, ...), custom_call_target="tpu_custom_call" | custom-call | flops 64424509440 | bytes 29360128 | tf_op jit(solution)/shard_map/attend_back/pallas_call | solution.py:326
  494.9 13.4 %key_value_grad.1 = (bf16[8,2,128,512]{3,2,1,0:T(8,128)(2,1)}, bf16[8,2,128,512]{3,2,1,0:T(8,128)(2,1)}) custom-call(s32[1]{0:T(128)} %bitcast.19.core_ref, bf16[2048,1024]{1,0:T(8,128)(2,1)} %get-tuple-element.113.x_ref, bf16[2,2048,1024]{2,1,0:T(8,128)(2,1)} %bitcast.142), custom_call_target="tpu_custom_call" | custom-call | flops 8589934592 | bytes 16777216 | tf_op jit(solution)/shard_map/key_value_grad/pallas_call | solution.py:573
  508.4 8.7 %query_grad.1 = (bf16[8,2,64,512]{3,2,1,0:T(8,128)(2,1)}, bf16[8,2,64,512]{3,2,1,0:T(8,128)(2,1)}) custom-call(s32[1]{0:T(128)} %bitcast.19.core_ref, bf16[2048,1024]{1,0:T(8,128)(2,1)} %get-tuple-element.113.x_ref, bf16[1,2048,1024]{2,1,0:T(8,128)(2,1)} %bitcast.151), custom_call_target="tpu_custom_call" | custom-call | flops 4294967296 | bytes 10485760 | tf_op jit(solution)/shard_map/query_grad/pallas_call | solution.py:573
  517.5 1.1 add_reduce_fusion
  520.0 1.6 add_convert_fusion.3
  521.7 2.3 add_convert_fusion.2
  524.5 1.1 copy.79
  525.6 7.7 %reduce-scatter.5.cloned.1.call-done = bf16[1,64,2560]{2,1,0:T(8,128)(2,1)} async-done(((bf16[16,64,2560]{2,1,0:T(8,128)(2,1)}), bf16[1,64,2560]{2,1,0:T(8,128)(2,1)}) %reduce-scatter.5.cloned.1.call-update) | async-done | bytes 327696 | tf_op jit(solution)/shard_map/reduce_scatter | solution.py:654
  533.3 1.0 bitcast_convert_fusion
  534.4 13.8 %input_back.2 = (bf16[1024,1024]{1,0:T(8,128)(2,1)}, f32[4,8,1024]{2,1,0:T(8,128)}) custom-call(s32[1]{0:T(128)S(6)} %sub.36.which_ref, bf16[2048,1024]{1,0:T(8,128)(2,1)} %bitcast.140, f32[2048,1024]{1,0:T(8,128)} %get-tuple-element.103.mg_ref, bf16[2048,1024]{1,0:T(8,128)(2,1)} %bitcast.152, bf16[2,2048,1024]{2,1,0:T(8,128)(2,1)} %bitcast.143, ...), custom_call_target="tpu_custom_call" | custom-call | flops 6442450944 | bytes 23068672 | tf_op jit(solution)/shard_map/input_back/pallas_call | solution.py:620
  548.7 1.6 collective-permute-start.9
  550.3 2.5 broadcast_select_fusion.3
  552.8 2.4 pad_maximum_fusion.3
  555.2 6.8 %collective-permute-done.9 = bf16[2,2,2,64,512]{4,3,2,1,0:T(8,128)(2,1)S(1)} collective-permute-done((bf16[2,2,2,64,512]{4,3,2,1,0:T(8,128)(2,1)S(1)}, bf16[2,2,2,64,512]{4,3,2,1,0:T(8,128)(2,1)S(1)}, u32[]{:S(2)}, u32[]{:S(2)}) %collective-permute-start.9) | collective-permute-done | bytes 524320 | tf_op jit(solution)/shard_map/ppermute | solution.py:813
  562.2 2.7 collective-permute-start.12
  564.9 1.6 fusion
  566.5 1.6 collective-permute-start.11
  568.1 13.9 %input_back.3 = (bf16[1024,1024]{1,0:T(8,128)(2,1)}, f32[4,8,1024]{2,1,0:T(8,128)}) custom-call(s32[1]{0:T(128)} %bitcast.which_ref, bf16[2048,1024]{1,0:T(8,128)(2,1)} %bitcast.141, f32[2048,1024]{1,0:T(8,128)} %get-tuple-element.103.mg_ref, bf16[2048,1024]{1,0:T(8,128)(2,1)} %bitcast.153, bf16[2,2048,1024]{2,1,0:T(8,128)(2,1)} %bitcast.144, ...), custom_call_target="tpu_custom_call" | custom-call | flops 6442450944 | bytes 23068672 | tf_op jit(solution)/shard_map/input_back/pallas_call | solution.py:620
  582.7 0.8 slice.105
  583.5 11.6 %collective-permute-done.10 = bf16[2,512,1024]{2,1,0:T(8,128)(2,1)} collective-permute-done((bf16[2,512,1024]{2,1,0:T(8,128)(2,1)}, bf16[2,512,1024]{2,1,0:T(8,128)(2,1)}, u32[]{:S(2)}, u32[]{:S(2)}) %collective-permute-start.10) | collective-permute-done | bytes 2097184 | tf_op jit(solution)/shard_map/ppermute | solution.py:822
  595.2 1.2 add_reduce_fusion.2
  596.7 1.0 fusion.6
  598.6 2.6 collective-permute-start.18
  601.5 1.9 broadcast_select_fusion.1
  604.0 2.4 pad_maximum_fusion.4
  606.4 1.6 collective-permute-done.21
  609.6 2.7 collective-permute-done.18
  612.4 1.6 collective-permute-done.14
  614.1 1.6 collective-permute-start.15
  616.4 2.0 collective-permute-done.15
  618.4 1.1 collective-permute-start.16
  619.5 1.1 collective-permute-done.19
  620.7 2.6 collective-permute-done.16
  624.8 2.3 collective-permute-done.17
  (109 shorter events, 15.6 us)
Async XLA Ops:
  7.2 9.4 %copy-start = (s32[4,2]{0,1:T(2,128)S(1)}, s32[4,2]{0,1:T(2,128)}, u32[]{:S(2)}) copy-start(s32[4,2]{0,1:T(2,128)} %param.34) | copy-start | bytes 100
  7.2 90.8 %all-gather.7.cloned.1.call-start = ((), (), s32[]{:S(2)}) async-start(), calls=%async_computation.4 | async-start | bytes 9191424 | tf_op jit(solution)/shard_map/all_gather | solution.py:726
  9.0 177.8 %all-gather.9.cloned.1.call-start = ((), (), s32[]{:S(2)}) async-start(), calls=%async_computation.5 | async-start | bytes 8650752 | tf_op jit(solution)/shard_map/all_gather | solution.py:727
  9.8 253.4 %all-gather.11.cloned.1.call-start = ((), (), s32[]{:S(2)}) async-start(), calls=%async_computation.6 | async-start | bytes 8650752 | tf_op jit(solution)/shard_map/all_gather | solution.py:728
  10.5 408.1 %reduce-scatter.3.cloned.1.call-start = ((), (), s32[]{:S(2)}) async-start(), calls=%async_computation.2 | async-start | bytes 4456448 | tf_op jit(solution)/shard_map/reduce_scatter | solution.py:654
  13.7 57.1 %collective-permute-start = (bf16[2,512,1024]{2,1,0:T(8,128)(2,1)}, bf16[2,512,1024]{2,1,0:T(8,128)(2,1)S(1)}, u32[]{:S(2)}, u32[]{:S(2)}) collective-permute-start(bf16[2,512,1024]{2,1,0:T(8,128)(2,1)} %constant_dynamic-slice_fusion.6), channel_id=1, source_target_pairs={{0,1},{1,0},{2,3},{3,2},{4,5},{5,4},{6,7},{7,6},{8,9},{9,8},{10,11... | collective-permute-start | bytes 6291464 | tf_op jit(solution)/shard_map/ppermute | solution.py:735
  17.4 53.4 %copy-start.2 = (bf16[4,512,1024]{2,1,0:T(8,128)(2,1)S(1)}, bf16[4,512,1024]{2,1,0:T(8,128)(2,1)}, u32[]{:S(2)}) copy-start(bf16[4,512,1024]{2,1,0:T(8,128)(2,1)} %param.18) | copy-start | bytes 12582916
  101.2 81.3 %collective-permute-start.1 = (bf16[2,512,1024]{2,1,0:T(8,128)(2,1)}, bf16[2,512,1024]{2,1,0:T(8,128)(2,1)S(1)}, u32[]{:S(2)}, u32[]{:S(2)}) collective-permute-start(bf16[2,512,1024]{2,1,0:T(8,128)(2,1)} %constant_dynamic-slice_fusion.4), channel_id=1, source_target_pairs={{0,1},{1,0},{2,3},{3,2},{4,5},{5,4},{6,7},{7,6},{8,9},{9,8},{10,11... | collective-permute-start | bytes 6291464 | tf_op jit(solution)/shard_map/ppermute | solution.py:735
  249.9 7.9 %collective-permute-start.2 = (bf16[8,2,256,512]{3,2,1,0:T(8,128)(2,1)}, bf16[8,2,256,512]{3,2,1,0:T(8,128)(2,1)S(1)}, u32[]{:S(2)}, u32[]{:S(2)}) collective-permute-start(bf16[8,2,256,512]{3,2,1,0:T(8,128)(2,1)} %get-tuple-element.87), channel_id=1, source_target_pairs={{0,2},{2,0},{1,3},{3,1},{4,6},{6,4},{5,7},{7,5},{8,10},{10,8},{9,1... | collective-permute-start | bytes 12582920 | tf_op jit(solution)/shard_map/ppermute | solution.py:644
  263.1 270.3 %reduce-scatter.5.cloned.1.call-start = ((), (), s32[]{:S(2)}) async-start(), calls=%async_computation.3 | async-start | bytes 5570560 | tf_op jit(solution)/shard_map/reduce_scatter | solution.py:654
  305.1 97.8 %collective-permute-start.3 = (bf16[2,512,1024]{2,1,0:T(8,128)(2,1)}, bf16[2,512,1024]{2,1,0:T(8,128)(2,1)S(1)}, u32[]{:S(2)}, u32[]{:S(2)}) collective-permute-start(bf16[2,512,1024]{2,1,0:T(8,128)(2,1)} %bitcast.186), channel_id=1, source_target_pairs={{0,1},{1,0},{2,3},{3,2},{4,5},{5,4},{6,7},{7,6},{8,9},{9,8},{10,11... | collective-permute-start | bytes 6291464 | tf_op jit(solution)/shard_map/ppermute | solution.py:783
  357.2 54.6 %copy-start.6 = (bf16[8,2,64,512]{3,2,1,0:T(8,128)(2,1)S(1)}, bf16[8,2,64,512]{3,2,1,0:T(8,128)(2,1)}, u32[]{:S(2)}) copy-start(bf16[8,2,64,512]{3,2,1,0:T(8,128)(2,1)} %get-tuple-element.107) | copy-start | bytes 3145732
  403.0 12.7 %copy-start.4 = (bf16[2,512,1024]{2,1,0:T(8,128)(2,1)}, bf16[2,512,1024]{2,1,0:T(8,128)(2,1)S(1)}, u32[]{:S(2)}) copy-start(bf16[2,512,1024]{2,1,0:T(8,128)(2,1)S(1)} %collective-permute-done.3) | copy-start | bytes 6291460
  403.0 9.2 %collective-permute-start.4 = (bf16[8,2,64,2048]{3,2,1,0:T(8,128)(2,1)}, bf16[8,2,64,2048]{3,2,1,0:T(8,128)(2,1)S(1)}, u32[]{:S(2)}, u32[]{:S(2)}) collective-permute-start(bf16[8,2,64,2048]{3,2,1,0:T(8,128)(2,1)} %get-tuple-element.106), channel_id=1, source_target_pairs={{0,2},{2,0},{1,3},{3,1},{4,6},{6,4},{5,7},{7,5},{8,10},{10,8},{9,1... | collective-permute-start | bytes 12582920 | tf_op jit(solution)/shard_map/ppermute | solution.py:644
  403.0 8.9 %collective-permute-start.5 = (bf16[8,2,64,512]{3,2,1,0:T(8,128)(2,1)}, bf16[8,2,64,512]{3,2,1,0:T(8,128)(2,1)S(1)}, u32[]{:S(2)}, u32[]{:S(2)}) collective-permute-start(bf16[8,2,64,512]{3,2,1,0:T(8,128)(2,1)} %get-tuple-element.108), channel_id=1, source_target_pairs={{0,2},{2,0},{1,3},{3,1},{4,6},{6,4},{5,7},{7,5},{8,10},{10,8},{9,1... | collective-permute-start | bytes 3145736 | tf_op jit(solution)/shard_map/ppermute | solution.py:644
  508.4 13.3 %collective-permute-start.7 = (bf16[8,2,128,512]{3,2,1,0:T(8,128)(2,1)}, bf16[8,2,128,512]{3,2,1,0:T(8,128)(2,1)}, u32[]{:S(2)}, u32[]{:S(2)}) collective-permute-start(bf16[8,2,128,512]{3,2,1,0:T(8,128)(2,1)} %get-tuple-element.117), channel_id=1, source_target_pairs={{0,2},{2,0},{1,3},{3,1},{4,6},{6,4},{5,7},{7,5},{8,10},{10,8},{9,1... | collective-permute-start | bytes 6291464 | tf_op jit(solution)/shard_map/ppermute | solution.py:644
  508.4 9.2 %copy-start.8 = (f32[8,4096]{1,0:T(8,128)S(1)}, f32[8,4096]{1,0:T(8,128)}, u32[]{:S(2)}) copy-start(f32[8,4096]{1,0:T(8,128)} %get-tuple-element.130) | copy-start | bytes 393220
  508.4 10.9 %copy-start.7 = (f32[4,8,1024]{2,1,0:T(8,128)S(1)}, f32[4,8,1024]{2,1,0:T(8,128)}, u32[]{:S(2)}) copy-start(f32[4,8,1024]{2,1,0:T(8,128)} %get-tuple-element.128) | copy-start | bytes 393220
  508.4 10.9 %copy-start.9 = (f32[4,8,1024]{2,1,0:T(8,128)S(1)}, f32[4,8,1024]{2,1,0:T(8,128)}, u32[]{:S(2)}) copy-start(f32[4,8,1024]{2,1,0:T(8,128)} %get-tuple-element.127) | copy-start | bytes 393220
  517.1 4.6 copy-start.3
  517.1 2.9 collective-permute-start.6
  519.3 4.6 copy-start.10
  525.6 36.4 %collective-permute-start.8 = (bf16[2,2,2,128,512]{4,3,2,0,1:T(8,128)(2,1)}, bf16[2,2,2,128,512]{4,3,2,0,1:T(8,128)(2,1)}, u32[]{:S(2)}, u32[]{:S(2)}) collective-permute-start(bf16[2,2,2,128,512]{4,3,2,0,1:T(8,128)(2,1)} %bitcast.127), channel_id=1, source_target_pairs={{0,4},{4,0},{1,5},{5,1},{2,6},{6,2},{3,7},{7,3},{8,12},{12,8},{9,1... | collective-permute-start | bytes 3145736 | tf_op jit(solution)/shard_map/ppermute | solution.py:813
  548.2 46.9 %collective-permute-start.10 = (bf16[2,512,1024]{2,1,0:T(8,128)(2,1)}, bf16[2,512,1024]{2,1,0:T(8,128)(2,1)}, u32[]{:S(2)}, u32[]{:S(2)}) collective-permute-start(bf16[2,512,1024]{2,1,0:T(8,128)(2,1)} %bitcast.185), channel_id=1, source_target_pairs={{0,1},{1,0},{2,3},{3,2},{4,5},{5,4},{6,7},{7,6},{8,9},{9,8},{10,11... | collective-permute-start | bytes 6291464 | tf_op jit(solution)/shard_map/ppermute | solution.py:822
  548.7 13.3 %collective-permute-start.9 = (bf16[2,2,2,64,512]{4,3,2,1,0:T(8,128)(2,1)S(1)}, bf16[2,2,2,64,512]{4,3,2,1,0:T(8,128)(2,1)S(1)}, u32[]{:S(2)}, u32[]{:S(2)}) collective-permute-start(bf16[2,2,2,64,512]{4,3,2,1,0:T(8,128)(2,1)S(1)} %dynamic-slice_bitcast_fusion), channel_id=1, source_target_pairs={{0,8},{8,0},{16,24},{24,16},{1,9},{9,1},{17,25},{25,17},{2,10},{10... | collective-permute-start | bytes 1572872 | tf_op jit(solution)/shard_map/ppermute | solution.py:813
  562.2 21.3 %collective-permute-start.12 = (bf16[2,2,64,512]{3,2,1,0:T(8,128)(2,1)S(1)}, bf16[2,2,64,512]{3,2,1,0:T(8,128)(2,1)}, u32[]{:S(2)}, u32[]{:S(2)}) collective-permute-start(bf16[2,2,64,512]{3,2,1,0:T(8,128)(2,1)S(1)} %dynamic-slice_bitcast_fusion.3), channel_id=1, source_target_pairs={{0,16},{16,0},{8,24},{24,8},{1,17},{17,1},{9,25},{25,9},{2,18},{18... | collective-permute-start | bytes 786440 | tf_op jit(solution)/shard_map/ppermute | solution.py:815
  566.5 29.9 %slice-start = ((bf16[4,1024]{1,0:T(4,128)(2,1)}), bf16[2,1024]{1,0:T(2,128)(2,1)S(1)}, s32[]{:S(2)}) async-start(bf16[4,1024]{1,0:T(4,128)(2,1)} %copy-done.10), calls=%async_computation.7 | async-start | bytes 8192 | tf_op jit(solution)/shard_map/slice | solution.py:829
  566.5 29.9 %copy-start.12 = (bf16[1,1024]{1,0:T(2,128)(2,1)S(1)}, bf16[1,1024]{1,0:T(2,128)(2,1)}, u32[]{:S(2)}) copy-start(bf16[1,1024]{1,0:T(2,128)(2,1)} %get-tuple-element.158) | copy-start | bytes 6148
  566.5 17.0 %collective-permute-start.11 = (bf16[2,2,128,512]{3,2,1,0:T(8,128)(2,1)S(1)}, bf16[2,2,128,512]{3,2,1,0:T(8,128)(2,1)S(1)}, u32[]{:S(2)}, u32[]{:S(2)}) collective-permute-start(bf16[2,2,128,512]{3,2,1,0:T(8,128)(2,1)S(1)} %dynamic-slice_bitcast_fusion.1), channel_id=1, source_target_pairs={{0,8},{8,0},{16,24},{24,16},{1,9},{9,1},{17,25},{25,17},{2,10},{10... | collective-permute-start | bytes 1572872 | tf_op jit(solution)/shard_map/ppermute | solution.py:815
  582.0 19.2 %copy-start.11 = (bf16[8,2,2,128]{3,0,2,1:T(8,128)(2,1)S(1)}, bf16[8,2,2,128]{3,0,2,1:T(8,128)(2,1)}, u32[]{:S(2)}) copy-start(bf16[8,2,2,128]{3,0,2,1:T(8,128)(2,1)} %copy.81) | copy-start | bytes 24580
  595.2 6.3 copy-start.5
  597.8 5.6 collective-permute-start.20
  598.6 13.7 %collective-permute-start.18 = (bf16[2,128,512]{2,1,0:T(8,128)(2,1)S(1)}, bf16[2,128,512]{2,1,0:T(8,128)(2,1)S(1)}, u32[]{:S(2)}, u32[]{:S(2)}) collective-permute-start(bf16[2,128,512]{2,1,0:T(8,128)(2,1)S(1)} %dynamic-slice_bitcast_fusion.2), channel_id=1, source_target_pairs={{0,16},{16,0},{8,24},{24,8},{1,17},{17,1},{9,25},{25,9},{2,18},{18... | collective-permute-start | bytes 786440 | tf_op jit(solution)/shard_map/ppermute | solution.py:674
  601.4 7.3 %collective-permute-start.13 = (bf16[8,2,16,512]{3,2,1,0:T(8,128)(2,1)S(1)}, bf16[8,2,16,512]{3,2,1,0:T(8,128)(2,1)S(1)}, u32[]{:S(2)}, u32[]{:S(2)}) collective-permute-start(bf16[8,2,16,512]{3,2,1,0:T(8,128)(2,1)S(1)} %bitcast.170), channel_id=1, source_target_pairs={{0,2},{2,0},{1,3},{3,1},{4,6},{6,4},{5,7},{7,5},{8,10},{10,8},{9,1... | collective-permute-start | bytes 786440 | tf_op jit(solution)/shard_map/ppermute | solution.py:644
  603.5 4.5 collective-permute-start.21
  604.0 24.3 %copy-start.1 = (s32[4,2]{0,1:T(2,128)S(1)}, s32[4,2]{0,1:T(2,128)}, u32[]{:S(2)}) copy-start(s32[4,2]{0,1:T(2,128)} %param.34) | copy-start | bytes 100
  608.8 5.2 collective-permute-start.14
  614.1 4.3 collective-permute-start.15
  615.7 5.0 collective-permute-start.19
  618.4 4.9 collective-permute-start.16
  623.3 3.8 collective-permute-start.17
Sparse Core Ops, SparseCore 0:
  11.5 86.4 all-gather.6
  101.1 81.8 all-gather.8
  186.1 76.7 all-gather.10
  265.1 118.8 reduce-scatter.2
  418.7 114.6 reduce-scatter.4

commit v4 on v3

--- a/solution.py
+++ b/solution.py
@@ -246,7 +246,7 @@
 def attend(starts, offset, q, k, v, fixed_offset):
     count, queries, d = q.shape
     keys = k.shape[1]
-    lanes = 256
+    lanes = min(512, d)
     rows = lambda n: pl.BlockSpec((1, n, lanes), lambda b, p, *_: (b, 0, p))
     return pl.pallas_call(
         functools.partial(attend_body, fixed_offset),
@@ -762,13 +762,13 @@
     vec = first[:, :, 4 * per : 4 * per + 8, :small].astype(F32).transpose(2, 0, 1, 3).reshape(8, d)
     upb = first[:, :, 4 * per + 8, :wide].astype(F32).reshape(1, ff)
     came = swap_rows(out_grad, first)
-    x1, q, k, v = project(x, vec, first, tile)
+    x1, q, k, v = project(x, vec, first, min(512, rows))
     q, k, v = (t.reshape(sequences, queries, d) for t in (q, k, v))
     if not paired:
         k, v = (lax.all_gather(t, "seq", axis=1, tiled=True) for t in (k, v))
     att, lse = attend(starts, offset, q, k, v, paired)
     og = gather_rows(out_grad, after(came, att))
-    middle, x2 = settle(x, att, vec, first, tile)
+    middle, x2 = settle(x, att, vec, first, min(512, rows))
     act, slope = rise(after(x2, og), upb, up, min(512, rows))
     down_mine = add_cores(*down_grad(core, act, og, dp, g))
     down_sum = add_chips(down_mine)

time: 639 us -> 640 us (level)
  Pallas kernels: 385 us -> 376 us
  waiting for transfers between devices: 155 us -> 164 us
    pallas_call x1, Pallas kernels: 46.4 us -> 39.6 us  [attend(): pl.pallas_call(functools.partial(attend_body, fixed_offset), grid_spec=pl...]
  transfers between devices with their start and end apart: 27 -> 27, of which waited for: 16 -> 19; matrix products, arithmetic and copies ran while one was open for 9% -> 9% of each run, Pallas kernels for 60% -> 59%
where the time goes in v4:
time: 640 us; the launch traced here: 635 us
  Pallas kernels  376 us (59%)
  waiting for transfers between devices  164 us (26%)
  other arithmetic  42.7 us (7%)
  starting transfers between devices  22.2 us (3%)
  local copies, waits for them, and re-layouts  15.5 us (2%)
  between operations  14.7 us (2%)
    pallas_call x2, Pallas kernels, fall(): pl.pallas_call(functools.partial(fall_body, bool(begun)), grid_spec=pltpu...  84.2 us
    pallas_call x1, Pallas kernels, attend_back(): pl.pallas_call(functools.partial(attend_back_body, fixed_offset), grid_sp...  74.6 us
    pallas_call x4, Pallas kernels, weight_grad(): pl.pallas_call(functools.partial(weight_grad_body, form), grid_spec=pltpu...  53.9 us
    ppermute x2, waiting for transfers between devices, swap_rows(): return lax.ppermute(after(sent, *earlier), 'seq', [(0, 1), (1, 0)])  50.2 us
    pallas_call x1, Pallas kernels, rise(): pl.pallas_call(rise_body, grid=(tokens // tile,), in_specs=[pl.BlockSpec(...  40.2 us
    pallas_call x1, Pallas kernels, attend(): pl.pallas_call(functools.partial(attend_body, fixed_offset), grid_spec=pl...  39.6 us
    pallas_call x2, Pallas kernels, input_back(): pl.pallas_call(input_body, grid_spec=pltpu.PrefetchScalarGridSpec(num_sca...  27.7 us
    all_gather x1, waiting for transfers between devices, body(): lax.all_gather(packed, everyone, axis=0)  24.5 us
  transfers between devices with their start and end apart: 27, of which 19 were waited for; matrix products, arithmetic and copies ran while one was open for 9% of the time, Pallas kernels for 59%

profile of v4, /device:TPU:0, one launch (start us, length us, event | category | flops | bytes accessed | tf_op | source)
XLA Modules:
  0.0 635.0 jit_solution(13207700996433803201)
XLA Ops:
  7.3 1.8 pack.1
  10.6 3.1 constant_dynamic-slice_fusion.6
  13.7 3.0 collective-permute-start
  17.4 3.2 constant_dynamic-slice_fusion.4
  20.6 50.2 %collective-permute-done = bf16[2,512,1024]{2,1,0:T(8,128)(2,1)S(1)} collective-permute-done((bf16[2,512,1024]{2,1,0:T(8,128)(2,1)}, bf16[2,512,1024]{2,1,0:T(8,128)(2,1)S(1)}, u32[]{:S(2)}, u32[]{:S(2)}) %collective-permute-start) | collective-permute-done | bytes 2097184 | tf_op jit(solution)/shard_map/ppermute | solution.py:735
  71.0 2.5 pad_maximum_fusion.1
  73.5 24.5 %all-gather.7.cloned.1.call-done = bf16[8704,512]{1,0:T(8,128)(2,1)} async-done(((bf16[272,512]{1,0:T(8,128)(2,1)}), bf16[8704,512]{1,0:T(8,128)(2,1)}) %all-gather.7.cloned.1.call-update) | async-done | bytes 8912912 | tf_op jit(solution)/shard_map/all_gather | solution.py:726
  98.0 0.8 slice.71
  101.2 1.5 collective-permute-start.1
  102.7 19.8 %project.1 = (bf16[2048,1024]{1,0:T(8,128)(2,1)}, bf16[2048,1024]{1,0:T(8,128)(2,1)}, bf16[2048,1024]{1,0:T(8,128)(2,1)}, bf16[2048,1024]{1,0:T(8,128)(2,1)}) custom-call(bf16[2048,1024]{1,0:T(8,128)(2,1)} %bitcast.138, f32[8,1024]{1,0:T(8,128)} %reshape.235.vec_ref, bf16[16,2,272,512]{3,2,1,0:T(8,128)(2,1)} %bitcast.132), custom_call_target="tpu_custom_call" | custom-call | flops 12884901888 | bytes 27262976 | tf_op jit(solution)/shard_map/project/pallas_call | solution.py:133
  122.5 39.6 %attend.1 = (bf16[1024,2048]{1,0:T(8,128)(2,1)}, f32[2,8,2,1024]{3,2,1,0:T(2,128)}) custom-call(s32[2,2]{1,0:T(2,128)} %copy.65.starts_ref, s32[1]{0:T(128)} %constant.135.clone.1.offset_ref, bf16[2,1024,1024]{2,1,0:T(8,128)(2,1)} %bitcast.187, bf16[2,1024,1024]{2,1,0:T(8,128)(2,1)} %bitcast.189, bf16[2,1024,1024]{2,1,0:T(8,128)(2,1)} %bitcast.191), custom_call_target="tpu_custom_call" | custom-call | flops 25769803776 | bytes 16777216 | tf_op jit(solution)/shard_map/attend/pallas_call | solution.py:251
  162.1 11.4 %settle.1 = (f32[2048,1024]{1,0:T(8,128)}, bf16[2048,1024]{1,0:T(8,128)(2,1)}) custom-call(bf16[2048,1024]{1,0:T(8,128)(2,1)} %bitcast.139, bf16[1024,2048]{1,0:T(8,128)(2,1)} %get-tuple-element.79.att_ref.x_ref, f32[8,1024]{1,0:T(8,128)} %reshape.235.vec_ref, bf16[16,2,272,512]{3,2,1,0:T(8,128)(2,1)} %bitcast.133), custom_call_target="tpu_custom_call" | custom-call | flops 4294967296 | bytes 23068672 | tf_op jit(solution)/shard_map/settle/pallas_call | solution.py:382
  173.5 1.9 broadcast_select_fusion.5
  175.4 2.4 pad_maximum_fusion.2
  177.8 5.2 all-gather.9.cloned.1.call-done
  183.0 40.2 %rise.1 = (bf16[2048,4096]{1,0:T(8,128)(2,1)}, bf16[2048,4096]{1,0:T(8,128)(2,1)}) custom-call(bf16[2048,1024]{1,0:T(8,128)(2,1)} %get-tuple-element.84.x2_ref.x_ref, f32[1,4096]{1,0:T(1,128)} %convert.45.upb_ref, bf16[16,2,64,2048]{3,2,1,0:T(8,128)(2,1)} %bitcast.155), custom_call_target="tpu_custom_call" | custom-call | flops 17179869184 | bytes 46137344 | tf_op jit(solution)/shard_map/rise/pallas_call | solution.py:416
  223.2 23.1 %down_grad.1 = (bf16[8,2,256,512]{3,2,1,0:T(8,128)(2,1)}, bf16[8,2,256,512]{3,2,1,0:T(8,128)(2,1)}) custom-call(s32[1]{0:T(128)} %bitcast.19.core_ref, bf16[2048,4096]{1,0:T(8,128)(2,1)} %get-tuple-element.88.act_ref, bf16[2048,1024]{1,0:T(8,128)(2,1)} %bitcast.147), custom_call_target="tpu_custom_call" | custom-call | flops 17179869184 | bytes 29360128 | tf_op jit(solution)/shard_map/down_grad/pallas_call | solution.py:543
  246.5 7.2 %collective-permute-done.2 = bf16[8,2,256,512]{3,2,1,0:T(8,128)(2,1)S(1)} collective-permute-done((bf16[8,2,256,512]{3,2,1,0:T(8,128)(2,1)}, bf16[8,2,256,512]{3,2,1,0:T(8,128)(2,1)S(1)}, u32[]{:S(2)}, u32[]{:S(2)}) %collective-permute-start.2) | collective-permute-done | bytes 4194336 | tf_op jit(solution)/shard_map/ppermute | solution.py:644
  253.7 5.2 add_convert_fusion.1
  259.0 3.8 all-gather.11.cloned.1.call-done
  262.9 41.9 %fall.2 = (bf16[1024,1024]{1,0:T(8,128)(2,1)}, bf16[2048,4096]{1,0:T(8,128)(2,1)}, f32[2048,1024]{1,0:T(8,128)}, bf16[2048,1024]{1,0:T(8,128)(2,1)}, bf16[2048,1...) custom-call(s32[1]{0:T(128)S(6)} %sub.36.which_ref, f32[2048,1024]{1,0:T(8,128)} %get-tuple-element.80.mid_ref, ...), custom_call_target="tpu_custom_call" | custom-call | flops 27917287424 | bytes 60817408 | tf_op jit(solution)/shard_map/fall/pallas_call | solution.py:492
  304.8 1.6 collective-permute-start.3
  306.4 42.3 %fall.3 = (bf16[1024,1024]{1,0:T(8,128)(2,1)}, bf16[2048,4096]{1,0:T(8,128)(2,1)}, f32[2048,1024]{1,0:T(8,128)}, bf16[2048,1024]{1,0:T(8,128)(2,1)}, bf16[2048,1...) custom-call(s32[1]{0:T(128)} %bitcast.which_ref, ...), custom_call_target="tpu_custom_call", output_to_operand_aliasing={{1}: (9, {}), {2}: (10, {}), {3}: (11, {}), {4}: (12, {})} | custom-call | flops 27917287424 | bytes 60817408 | tf_op jit(solution)/shard_map/fall/pallas_call | solution.py:492
  348.7 8.5 %out_grad.1 = (bf16[8,2,64,512]{3,2,1,0:T(8,128)(2,1)}, bf16[8,2,64,512]{3,2,1,0:T(8,128)(2,1)}) custom-call(s32[1]{0:T(128)} %bitcast.19.core_ref, bf16[1024,2048]{1,0:T(8,128)(2,1)} %get-tuple-element.79.att_ref.x_ref, bf16[1,2048,1024]{2,1,0:T(8,128)(2,1)} %bitcast.160), custom_call_target="tpu_custom_call" | custom-call | flops 4294967296 | bytes 10485760 | tf_op jit(solution)/shard_map/out_grad/pallas_call | solution.py:573
  357.2 23.3 %up_grad.1 = (bf16[8,2,64,2048]{3,2,1,0:T(8,128)(2,1)}, bf16[8,2,64,2048]{3,2,1,0:T(8,128)(2,1)}) custom-call(s32[1]{0:T(128)} %bitcast.19.core_ref, bf16[2048,1024]{1,0:T(8,128)(2,1)} %get-tuple-element.84.x2_ref.x_ref, bf16[1,2048,4096]{2,1,0:T(8,128)(2,1)} %bitcast.150), custom_call_target="tpu_custom_call" | custom-call | flops 17179869184 | bytes 29360128 | tf_op jit(solution)/shard_map/up_grad/pallas_call | solution.py:573
  380.5 22.3 %collective-permute-done.3 = bf16[2,512,1024]{2,1,0:T(8,128)(2,1)S(1)} collective-permute-done((bf16[2,512,1024]{2,1,0:T(8,128)(2,1)}, bf16[2,512,1024]{2,1,0:T(8,128)(2,1)S(1)}, u32[]{:S(2)}, u32[]{:S(2)}) %collective-permute-start.3) | collective-permute-done | bytes 2097184 | tf_op jit(solution)/shard_map/ppermute | solution.py:783
  403.3 8.4 %collective-permute-done.5 = bf16[8,2,64,512]{3,2,1,0:T(8,128)(2,1)S(1)} collective-permute-done((bf16[8,2,64,512]{3,2,1,0:T(8,128)(2,1)}, bf16[8,2,64,512]{3,2,1,0:T(8,128)(2,1)S(1)}, u32[]{:S(2)}, u32[]{:S(2)}) %collective-permute-start.5) | collective-permute-done | bytes 1048608 | tf_op jit(solution)/shard_map/ppermute | solution.py:644
  412.1 3.5 add_convert_fusion
  415.6 2.8 pad_maximum_fusion
  418.5 1.8 bitcast_convert_fusion.1
  420.3 74.6 %attend_back.1 = (bf16[2,1024,1024]{2,1,0:T(8,128)(2,1)}, bf16[2,2,1024,1024]{3,2,1,0:T(8,128)(2,1)}) custom-call(s32[2,2]{1,0:T(2,128)} %copy.65.starts_ref, s32[1]{0:T(128)} %constant.135.clone.1.offset_ref, bf16[2,1024,1024]{2,1,0:T(8,128)(2,1)} %bitcast.188, bf16[2,1024,1024]{2,1,0:T(8,128)(2,1)} %bitcast.190, bf16[2,1024,1024]{2,1,0:T(8,128)(2,1)} %bitcast.192, ...), custom_call_target="tpu_custom_call" | custom-call | flops 64424509440 | bytes 29360128 | tf_op jit(solution)/shard_map/attend_back/pallas_call | solution.py:326
  494.8 13.4 %key_value_grad.1 = (bf16[8,2,128,512]{3,2,1,0:T(8,128)(2,1)}, bf16[8,2,128,512]{3,2,1,0:T(8,128)(2,1)}) custom-call(s32[1]{0:T(128)} %bitcast.19.core_ref, bf16[2048,1024]{1,0:T(8,128)(2,1)} %get-tuple-element.113.x_ref, bf16[2,2048,1024]{2,1,0:T(8,128)(2,1)} %bitcast.142), custom_call_target="tpu_custom_call" | custom-call | flops 8589934592 | bytes 16777216 | tf_op jit(solution)/shard_map/key_value_grad/pallas_call | solution.py:573
  508.5 8.6 %query_grad.1 = (bf16[8,2,64,512]{3,2,1,0:T(8,128)(2,1)}, bf16[8,2,64,512]{3,2,1,0:T(8,128)(2,1)}) custom-call(s32[1]{0:T(128)} %bitcast.19.core_ref, bf16[2048,1024]{1,0:T(8,128)(2,1)} %get-tuple-element.113.x_ref, bf16[1,2048,1024]{2,1,0:T(8,128)(2,1)} %bitcast.151), custom_call_target="tpu_custom_call" | custom-call | flops 4294967296 | bytes 10485760 | tf_op jit(solution)/shard_map/query_grad/pallas_call | solution.py:573
  517.4 1.2 add_reduce_fusion
  520.0 1.6 add_convert_fusion.3
  521.6 2.3 add_convert_fusion.2
  524.5 1.1 copy.79
  525.6 7.9 %reduce-scatter.5.cloned.1.call-done = bf16[1,64,2560]{2,1,0:T(8,128)(2,1)} async-done(((bf16[16,64,2560]{2,1,0:T(8,128)(2,1)}), bf16[1,64,2560]{2,1,0:T(8,128)(2,1)}) %reduce-scatter.5.cloned.1.call-update) | async-done | bytes 327696 | tf_op jit(solution)/shard_map/reduce_scatter | solution.py:654
  533.5 1.0 bitcast_convert_fusion
  534.5 13.8 %input_back.2 = (bf16[1024,1024]{1,0:T(8,128)(2,1)}, f32[4,8,1024]{2,1,0:T(8,128)}) custom-call(s32[1]{0:T(128)S(6)} %sub.36.which_ref, bf16[2048,1024]{1,0:T(8,128)(2,1)} %bitcast.140, f32[2048,1024]{1,0:T(8,128)} %get-tuple-element.103.mg_ref, bf16[2048,1024]{1,0:T(8,128)(2,1)} %bitcast.152, bf16[2,2048,1024]{2,1,0:T(8,128)(2,1)} %bitcast.143, ...), custom_call_target="tpu_custom_call" | custom-call | flops 6442450944 | bytes 23068672 | tf_op jit(solution)/shard_map/input_back/pallas_call | solution.py:620
  548.6 1.6 collective-permute-start.9
  550.2 2.5 broadcast_select_fusion.3
  552.7 2.4 pad_maximum_fusion.3
  555.0 6.8 %collective-permute-done.9 = bf16[2,2,2,64,512]{4,3,2,1,0:T(8,128)(2,1)S(1)} collective-permute-done((bf16[2,2,2,64,512]{4,3,2,1,0:T(8,128)(2,1)S(1)}, bf16[2,2,2,64,512]{4,3,2,1,0:T(8,128)(2,1)S(1)}, u32[]{:S(2)}, u32[]{:S(2)}) %collective-permute-start.9) | collective-permute-done | bytes 524320 | tf_op jit(solution)/shard_map/ppermute | solution.py:813
  562.0 2.7 collective-permute-start.12
  564.7 1.6 fusion
  566.4 1.6 collective-permute-start.11
  568.0 13.9 %input_back.3 = (bf16[1024,1024]{1,0:T(8,128)(2,1)}, f32[4,8,1024]{2,1,0:T(8,128)}) custom-call(s32[1]{0:T(128)} %bitcast.which_ref, bf16[2048,1024]{1,0:T(8,128)(2,1)} %bitcast.141, f32[2048,1024]{1,0:T(8,128)} %get-tuple-element.103.mg_ref, bf16[2048,1024]{1,0:T(8,128)(2,1)} %bitcast.153, bf16[2,2048,1024]{2,1,0:T(8,128)(2,1)} %bitcast.144, ...), custom_call_target="tpu_custom_call" | custom-call | flops 6442450944 | bytes 23068672 | tf_op jit(solution)/shard_map/input_back/pallas_call | solution.py:620
  583.4 12.3 %collective-permute-done.10 = bf16[2,512,1024]{2,1,0:T(8,128)(2,1)} collective-permute-done((bf16[2,512,1024]{2,1,0:T(8,128)(2,1)}, bf16[2,512,1024]{2,1,0:T(8,128)(2,1)}, u32[]{:S(2)}, u32[]{:S(2)}) %collective-permute-start.10) | collective-permute-done | bytes 2097184 | tf_op jit(solution)/shard_map/ppermute | solution.py:822
  595.9 1.2 add_reduce_fusion.2
  597.3 1.0 fusion.6
  598.5 2.6 collective-permute-start.18
  601.4 1.9 broadcast_select_fusion.1
  603.9 2.4 pad_maximum_fusion.4
  606.3 1.6 collective-permute-done.21
  609.5 2.8 collective-permute-done.18
  612.3 1.4 collective-permute-done.14
  613.8 1.7 collective-permute-start.15
  616.3 1.8 collective-permute-done.15
  618.2 1.2 collective-permute-start.16
  619.4 1.1 collective-permute-done.19
  620.6 2.5 collective-permute-done.16
  623.1 0.9 collective-permute-start.17
  624.7 2.2 collective-permute-done.17
  (109 shorter events, 16.4 us)
Async XLA Ops:
  7.2 9.4 %copy-start = (s32[4,2]{0,1:T(2,128)S(1)}, s32[4,2]{0,1:T(2,128)}, u32[]{:S(2)}) copy-start(s32[4,2]{0,1:T(2,128)} %param.34) | copy-start | bytes 100
  7.2 90.8 %all-gather.7.cloned.1.call-start = ((), (), s32[]{:S(2)}) async-start(), calls=%async_computation.4 | async-start | bytes 9191424 | tf_op jit(solution)/shard_map/all_gather | solution.py:726
  9.0 173.9 %all-gather.9.cloned.1.call-start = ((), (), s32[]{:S(2)}) async-start(), calls=%async_computation.5 | async-start | bytes 8650752 | tf_op jit(solution)/shard_map/all_gather | solution.py:727
  9.8 253.1 %all-gather.11.cloned.1.call-start = ((), (), s32[]{:S(2)}) async-start(), calls=%async_computation.6 | async-start | bytes 8650752 | tf_op jit(solution)/shard_map/all_gather | solution.py:728
  10.5 407.9 %reduce-scatter.3.cloned.1.call-start = ((), (), s32[]{:S(2)}) async-start(), calls=%async_computation.2 | async-start | bytes 4456448 | tf_op jit(solution)/shard_map/reduce_scatter | solution.py:654
  13.7 57.1 %collective-permute-start = (bf16[2,512,1024]{2,1,0:T(8,128)(2,1)}, bf16[2,512,1024]{2,1,0:T(8,128)(2,1)S(1)}, u32[]{:S(2)}, u32[]{:S(2)}) collective-permute-start(bf16[2,512,1024]{2,1,0:T(8,128)(2,1)} %constant_dynamic-slice_fusion.6), channel_id=1, source_target_pairs={{0,1},{1,0},{2,3},{3,2},{4,5},{5,4},{6,7},{7,6},{8,9},{9,8},{10,11... | collective-permute-start | bytes 6291464 | tf_op jit(solution)/shard_map/ppermute | solution.py:735
  17.4 53.4 %copy-start.2 = (bf16[4,512,1024]{2,1,0:T(8,128)(2,1)S(1)}, bf16[4,512,1024]{2,1,0:T(8,128)(2,1)}, u32[]{:S(2)}) copy-start(bf16[4,512,1024]{2,1,0:T(8,128)(2,1)} %param.18) | copy-start | bytes 12582916
  101.2 72.3 %collective-permute-start.1 = (bf16[2,512,1024]{2,1,0:T(8,128)(2,1)}, bf16[2,512,1024]{2,1,0:T(8,128)(2,1)S(1)}, u32[]{:S(2)}, u32[]{:S(2)}) collective-permute-start(bf16[2,512,1024]{2,1,0:T(8,128)(2,1)} %constant_dynamic-slice_fusion.4), channel_id=1, source_target_pairs={{0,1},{1,0},{2,3},{3,2},{4,5},{5,4},{6,7},{7,6},{8,9},{9,8},{10,11... | collective-permute-start | bytes 6291464 | tf_op jit(solution)/shard_map/ppermute | solution.py:735
  246.2 7.5 %collective-permute-start.2 = (bf16[8,2,256,512]{3,2,1,0:T(8,128)(2,1)}, bf16[8,2,256,512]{3,2,1,0:T(8,128)(2,1)S(1)}, u32[]{:S(2)}, u32[]{:S(2)}) collective-permute-start(bf16[8,2,256,512]{3,2,1,0:T(8,128)(2,1)} %get-tuple-element.87), channel_id=1, source_target_pairs={{0,2},{2,0},{1,3},{3,1},{4,6},{6,4},{5,7},{7,5},{8,10},{10,8},{9,1... | collective-permute-start | bytes 12582920 | tf_op jit(solution)/shard_map/ppermute | solution.py:644
  259.0 274.5 %reduce-scatter.5.cloned.1.call-start = ((), (), s32[]{:S(2)}) async-start(), calls=%async_computation.3 | async-start | bytes 5570560 | tf_op jit(solution)/shard_map/reduce_scatter | solution.py:654
  304.8 98.0 %collective-permute-start.3 = (bf16[2,512,1024]{2,1,0:T(8,128)(2,1)}, bf16[2,512,1024]{2,1,0:T(8,128)(2,1)S(1)}, u32[]{:S(2)}, u32[]{:S(2)}) collective-permute-start(bf16[2,512,1024]{2,1,0:T(8,128)(2,1)} %bitcast.186), channel_id=1, source_target_pairs={{0,1},{1,0},{2,3},{3,2},{4,5},{5,4},{6,7},{7,6},{8,9},{9,8},{10,11... | collective-permute-start | bytes 6291464 | tf_op jit(solution)/shard_map/ppermute | solution.py:783
  357.2 54.5 %copy-start.6 = (bf16[8,2,64,512]{3,2,1,0:T(8,128)(2,1)S(1)}, bf16[8,2,64,512]{3,2,1,0:T(8,128)(2,1)}, u32[]{:S(2)}) copy-start(bf16[8,2,64,512]{3,2,1,0:T(8,128)(2,1)} %get-tuple-element.107) | copy-start | bytes 3145732
  402.8 12.7 %copy-start.4 = (bf16[2,512,1024]{2,1,0:T(8,128)(2,1)}, bf16[2,512,1024]{2,1,0:T(8,128)(2,1)S(1)}, u32[]{:S(2)}) copy-start(bf16[2,512,1024]{2,1,0:T(8,128)(2,1)S(1)} %collective-permute-done.3) | copy-start | bytes 6291460
  402.8 9.2 %collective-permute-start.4 = (bf16[8,2,64,2048]{3,2,1,0:T(8,128)(2,1)}, bf16[8,2,64,2048]{3,2,1,0:T(8,128)(2,1)S(1)}, u32[]{:S(2)}, u32[]{:S(2)}) collective-permute-start(bf16[8,2,64,2048]{3,2,1,0:T(8,128)(2,1)} %get-tuple-element.106), channel_id=1, source_target_pairs={{0,2},{2,0},{1,3},{3,1},{4,6},{6,4},{5,7},{7,5},{8,10},{10,8},{9,1... | collective-permute-start | bytes 12582920 | tf_op jit(solution)/shard_map/ppermute | solution.py:644
  402.8 8.9 %collective-permute-start.5 = (bf16[8,2,64,512]{3,2,1,0:T(8,128)(2,1)}, bf16[8,2,64,512]{3,2,1,0:T(8,128)(2,1)S(1)}, u32[]{:S(2)}, u32[]{:S(2)}) collective-permute-start(bf16[8,2,64,512]{3,2,1,0:T(8,128)(2,1)} %get-tuple-element.108), channel_id=1, source_target_pairs={{0,2},{2,0},{1,3},{3,1},{4,6},{6,4},{5,7},{7,5},{8,10},{10,8},{9,1... | collective-permute-start | bytes 3145736 | tf_op jit(solution)/shard_map/ppermute | solution.py:644
  508.3 13.3 %collective-permute-start.7 = (bf16[8,2,128,512]{3,2,1,0:T(8,128)(2,1)}, bf16[8,2,128,512]{3,2,1,0:T(8,128)(2,1)}, u32[]{:S(2)}, u32[]{:S(2)}) collective-permute-start(bf16[8,2,128,512]{3,2,1,0:T(8,128)(2,1)} %get-tuple-element.117), channel_id=1, source_target_pairs={{0,2},{2,0},{1,3},{3,1},{4,6},{6,4},{5,7},{7,5},{8,10},{10,8},{9,1... | collective-permute-start | bytes 6291464 | tf_op jit(solution)/shard_map/ppermute | solution.py:644
  508.4 9.0 %copy-start.8 = (f32[8,4096]{1,0:T(8,128)S(1)}, f32[8,4096]{1,0:T(8,128)}, u32[]{:S(2)}) copy-start(f32[8,4096]{1,0:T(8,128)} %get-tuple-element.130) | copy-start | bytes 393220
  508.5 10.8 %copy-start.7 = (f32[4,8,1024]{2,1,0:T(8,128)S(1)}, f32[4,8,1024]{2,1,0:T(8,128)}, u32[]{:S(2)}) copy-start(f32[4,8,1024]{2,1,0:T(8,128)} %get-tuple-element.128) | copy-start | bytes 393220
  508.5 10.8 %copy-start.9 = (f32[4,8,1024]{2,1,0:T(8,128)S(1)}, f32[4,8,1024]{2,1,0:T(8,128)}, u32[]{:S(2)}) copy-start(f32[4,8,1024]{2,1,0:T(8,128)} %get-tuple-element.127) | copy-start | bytes 393220
  517.1 4.5 copy-start.3
  517.1 2.9 collective-permute-start.6
  519.3 4.7 copy-start.10
  525.6 36.3 %collective-permute-start.8 = (bf16[2,2,2,128,512]{4,3,2,0,1:T(8,128)(2,1)}, bf16[2,2,2,128,512]{4,3,2,0,1:T(8,128)(2,1)}, u32[]{:S(2)}, u32[]{:S(2)}) collective-permute-start(bf16[2,2,2,128,512]{4,3,2,0,1:T(8,128)(2,1)} %bitcast.127), channel_id=1, source_target_pairs={{0,4},{4,0},{1,5},{5,1},{2,6},{6,2},{3,7},{7,3},{8,12},{12,8},{9,1... | collective-permute-start | bytes 3145736 | tf_op jit(solution)/shard_map/ppermute | solution.py:813
  548.3 47.4 %collective-permute-start.10 = (bf16[2,512,1024]{2,1,0:T(8,128)(2,1)}, bf16[2,512,1024]{2,1,0:T(8,128)(2,1)}, u32[]{:S(2)}, u32[]{:S(2)}) collective-permute-start(bf16[2,512,1024]{2,1,0:T(8,128)(2,1)} %bitcast.185), channel_id=1, source_target_pairs={{0,1},{1,0},{2,3},{3,2},{4,5},{5,4},{6,7},{7,6},{8,9},{9,8},{10,11... | collective-permute-start | bytes 6291464 | tf_op jit(solution)/shard_map/ppermute | solution.py:822
  548.6 13.3 %collective-permute-start.9 = (bf16[2,2,2,64,512]{4,3,2,1,0:T(8,128)(2,1)S(1)}, bf16[2,2,2,64,512]{4,3,2,1,0:T(8,128)(2,1)S(1)}, u32[]{:S(2)}, u32[]{:S(2)}) collective-permute-start(bf16[2,2,2,64,512]{4,3,2,1,0:T(8,128)(2,1)S(1)} %dynamic-slice_bitcast_fusion), channel_id=1, source_target_pairs={{0,8},{8,0},{16,24},{24,16},{1,9},{9,1},{17,25},{25,17},{2,10},{10... | collective-permute-start | bytes 1572872 | tf_op jit(solution)/shard_map/ppermute | solution.py:813
  562.0 21.4 %collective-permute-start.12 = (bf16[2,2,64,512]{3,2,1,0:T(8,128)(2,1)S(1)}, bf16[2,2,64,512]{3,2,1,0:T(8,128)(2,1)}, u32[]{:S(2)}, u32[]{:S(2)}) collective-permute-start(bf16[2,2,64,512]{3,2,1,0:T(8,128)(2,1)S(1)} %dynamic-slice_bitcast_fusion.3), channel_id=1, source_target_pairs={{0,16},{16,0},{8,24},{24,8},{1,17},{17,1},{9,25},{25,9},{2,18},{18... | collective-permute-start | bytes 786440 | tf_op jit(solution)/shard_map/ppermute | solution.py:815
  566.4 30.7 %slice-start = ((bf16[4,1024]{1,0:T(4,128)(2,1)}), bf16[2,1024]{1,0:T(2,128)(2,1)S(1)}, s32[]{:S(2)}) async-start(bf16[4,1024]{1,0:T(4,128)(2,1)} %copy-done.10), calls=%async_computation.7 | async-start | bytes 8192 | tf_op jit(solution)/shard_map/slice | solution.py:829
  566.4 30.7 %copy-start.12 = (bf16[1,1024]{1,0:T(2,128)(2,1)S(1)}, bf16[1,1024]{1,0:T(2,128)(2,1)}, u32[]{:S(2)}) copy-start(bf16[1,1024]{1,0:T(2,128)(2,1)} %get-tuple-element.158) | copy-start | bytes 6148
  566.4 17.0 %collective-permute-start.11 = (bf16[2,2,128,512]{3,2,1,0:T(8,128)(2,1)S(1)}, bf16[2,2,128,512]{3,2,1,0:T(8,128)(2,1)S(1)}, u32[]{:S(2)}, u32[]{:S(2)}) collective-permute-start(bf16[2,2,128,512]{3,2,1,0:T(8,128)(2,1)S(1)} %dynamic-slice_bitcast_fusion.1), channel_id=1, source_target_pairs={{0,8},{8,0},{16,24},{24,16},{1,9},{9,1},{17,25},{25,17},{2,10},{10... | collective-permute-start | bytes 1572872 | tf_op jit(solution)/shard_map/ppermute | solution.py:815
  581.9 19.2 %copy-start.11 = (bf16[8,2,2,128]{3,0,2,1:T(8,128)(2,1)S(1)}, bf16[8,2,2,128]{3,0,2,1:T(8,128)(2,1)}, u32[]{:S(2)}) copy-start(bf16[8,2,2,128]{3,0,2,1:T(8,128)(2,1)} %copy.81) | copy-start | bytes 24580
  595.8 5.5 copy-start.5
  598.4 5.0 collective-permute-start.20
  598.5 13.7 %collective-permute-start.18 = (bf16[2,128,512]{2,1,0:T(8,128)(2,1)S(1)}, bf16[2,128,512]{2,1,0:T(8,128)(2,1)S(1)}, u32[]{:S(2)}, u32[]{:S(2)}) collective-permute-start(bf16[2,128,512]{2,1,0:T(8,128)(2,1)S(1)} %dynamic-slice_bitcast_fusion.2), channel_id=1, source_target_pairs={{0,16},{16,0},{8,24},{24,8},{1,17},{17,1},{9,25},{25,9},{2,18},{18... | collective-permute-start | bytes 786440 | tf_op jit(solution)/shard_map/ppermute | solution.py:674
  601.3 7.3 %collective-permute-start.13 = (bf16[8,2,16,512]{3,2,1,0:T(8,128)(2,1)S(1)}, bf16[8,2,16,512]{3,2,1,0:T(8,128)(2,1)S(1)}, u32[]{:S(2)}, u32[]{:S(2)}) collective-permute-start(bf16[8,2,16,512]{3,2,1,0:T(8,128)(2,1)S(1)} %bitcast.170), channel_id=1, source_target_pairs={{0,2},{2,0},{1,3},{3,1},{4,6},{6,4},{5,7},{7,5},{8,10},{10,8},{9,1... | collective-permute-start | bytes 786440 | tf_op jit(solution)/shard_map/ppermute | solution.py:644
  603.5 4.4 collective-permute-start.21
  603.9 24.1 %copy-start.1 = (s32[4,2]{0,1:T(2,128)S(1)}, s32[4,2]{0,1:T(2,128)}, u32[]{:S(2)}) copy-start(s32[4,2]{0,1:T(2,128)} %param.34) | copy-start | bytes 100
  608.7 5.0 collective-permute-start.14
  613.8 4.3 collective-permute-start.15
  615.5 5.0 collective-permute-start.19
  618.2 4.9 collective-permute-start.16
  623.1 3.8 collective-permute-start.17
Sparse Core Ops, SparseCore 0:
  11.5 86.4 all-gather.6
  101.1 81.8 all-gather.8
  186.1 76.7 all-gather.10
  265.0 119.1 reduce-scatter.2
  418.6 114.8 reduce-scatter.4
